TPU v7x, 32 devices: a whole 2x2x4 slice. The times are simulated.
32 devices in a mesh: groups: 2 (over y), dev: 2 (over core), side: 8 (over z, x).
Axes of the slice: x: 2, y: 2, z: 4, core: 2. Of those that a mesh axis runs over, the one named last changes fastest.
Arguments:
- queries: bfloat16 [4, 4, 8, 24, 128], P('groups', 'dev', 'side'), parts along dimension 0, may hold values from -2.5 to 2.5
- cache_keys: bfloat16 [4, 4, 8, 128, 4, 128], P('groups', 'dev', 'side'), parts along dimension 0, may hold values from -2.5 to 2.5
- cache_values: bfloat16 [4, 4, 8, 128, 4, 128], P('groups', 'dev', 'side'), parts along dimension 0, may hold values from -6 to 6
- new_keys: bfloat16 [4, 4, 8, 4, 128], P('groups', 'dev', 'side'), parts along dimension 0, may hold values from -2.5 to 2.5
- new_values: bfloat16 [4, 4, 8, 4, 128], P('groups', 'dev', 'side'), parts along dimension 0, may hold values from -6 to 6
- lengths: int32 [4, 4, 8], P('groups', 'dev', 'side'), parts along dimension 0, may hold values from 1 to 128, as said below
- out_weight: bfloat16 [3072, 3072], P(None, 'dev'), may hold values from -0.109375 to 0.109375
- residual: bfloat16 [4, 4, 8, 3072], P('groups', None, 'side', 'dev'), parts along dimension 0
- norm_gain: float32 [3072], replicated, may hold values from 0.1 to 1.9
- routes: int32 [4, 4, 8, 4], P('groups'), parts along dimension 0, may hold values from 0 to 7, all different within a row; in each aligned block of 16 rows (0 to 15, 16 to 31, ..., all dimensions but the last counted through in order) at most 9 rows name the same one
- route_probs: float32 [4, 4, 8, 4], P('groups', None, 'side'), parts along dimension 0, may hold values from 0.05 to 1
- w_gate: bfloat16 [8, 5376, 3072], P('side', 'dev'), may hold values from -0.109375 to 0.109375
- w_up: bfloat16 [8, 5376, 3072], P('side', 'dev'), may hold values from -0.109375 to 0.109375
- w_down: bfloat16 [8, 5376, 3072], P('side', 'dev'), may hold values from -0.078125 to 0.078125
Outputs:
- layer_out: bfloat16 [4, 4, 8, 3072], P('groups', None, 'side', 'dev'), parts along dimension 0
There are 2 independent parts, one for each index of `groups`. A program takes and returns all parts, laid end to end along the dimension named above; an argument that names none is the same for every part. Nothing has to cross between parts.
Inputs may be any that keep to these rules, and one draw needn't show every extreme that they name: `routes`: each row names 4 different experts and every expert is named by some row; within one micro-batch the 16 rows held by one index of dev (aligned blocks in the order of the first three dimensions) name any one expert at most 9 times, and some block reaches 9. `lengths`: some row has 128 valid positions and some row has 1.
All inputs are finite; a program needn't handle non-finite values.
Results may differ from a plain program's by a relative error of at most 0.006.
Values may be sent and summed in bfloat16 or wider, within the bound.
No kernel may reach another device: no remote copies, remote signals or barrier semaphores. Data moves between devices by JAX's collectives and lax.ppermute only.
A program may use at most 128 MiB of HBM per device.

v0:
```python
import math

import jax
import jax.numpy as jnp
from jax import lax
from jax.sharding import PartitionSpec as P

norm_epsilon = 1e-05


def attend(queries, cache_keys, cache_values, new_keys, new_values, lengths):
    leading = queries.shape[:-2]
    head_count = queries.shape[-2]
    head_width = queries.shape[-1]
    key_heads = cache_keys.shape[-2]
    cache_size = cache_keys.shape[-3]
    grouped = queries.reshape(leading + (key_heads, head_count // key_heads, head_width))
    factor = 1.0 / math.sqrt(head_width)
    scores = (
        jnp.einsum("...kgd,...ckd->...kgc", grouped, cache_keys, preferred_element_type=jnp.float32)
        * factor
    )
    fresh = (
        jnp.einsum("...kgd,...kd->...kg", grouped, new_keys, preferred_element_type=jnp.float32)
        * factor
    )
    visible = jnp.arange(cache_size, dtype=jnp.int32) < lengths[..., None, None, None]
    raised = jnp.where(visible, jnp.exp(scores), 0.0)
    raised_new = jnp.exp(fresh)
    denominator = jnp.sum(raised, axis=-1) + raised_new
    weights = (raised / denominator[..., None]).astype(jnp.bfloat16)
    weight_new = (raised_new / denominator).astype(jnp.bfloat16)
    mixed = jnp.einsum(
        "...kgc,...ckd->...kgd", weights, cache_values, preferred_element_type=jnp.float32
    )
    mixed = mixed + jnp.einsum(
        "...kg,...kd->...kgd", weight_new, new_values, preferred_element_type=jnp.float32
    )
    return mixed.astype(jnp.bfloat16).reshape(leading + (head_count * head_width,))


def normalize(values, scale_gain):
    widened = values.astype(jnp.float32)
    center = jnp.mean(widened, axis=-1, keepdims=True)
    spread = jnp.mean(jnp.square(widened - center), axis=-1, keepdims=True)
    return ((widened - center) * lax.rsqrt(spread + norm_epsilon) * scale_gain).astype(jnp.bfloat16)


def layer(
    queries,
    cache_keys,
    cache_values,
    new_keys,
    new_values,
    lengths,
    out_weight,
    residual,
    norm_gain,
    routes,
    route_probs,
    w_gate,
    w_up,
    w_down,
):
    batch_count = queries.shape[0]
    row_count = queries.shape[1]
    side_count = lax.axis_size("side")
    dev_count = lax.axis_size("dev")
    side_index = lax.axis_index("side")
    dev_index = lax.axis_index("dev")
    top_count = routes.shape[-1]
    column_width = residual.shape[-1]
    block_rows = row_count * side_count
    capacity = min(block_rows, block_rows * top_count // side_count + max(1, row_count // 2))
    attended = attend(queries, cache_keys, cache_values, new_keys, new_values, lengths)
    projected = jnp.einsum(
        "brsk,kc->brsc",
        lax.all_gather(attended, "dev", axis=1, tiled=True),
        out_weight,
        preferred_element_type=jnp.float32,
    ).astype(jnp.bfloat16)
    updated = (residual.astype(jnp.float32) + projected.astype(jnp.float32)).astype(jnp.bfloat16)
    expert_ids = jnp.arange(side_count, dtype=jnp.int32)
    slot_ids = jnp.arange(row_count, dtype=jnp.int32)
    column_routes = lax.dynamic_index_in_dim(routes, side_index, axis=2, keepdims=False)
    column_routes = column_routes.reshape(batch_count, dev_count, row_count, top_count)
    member = jnp.sum((column_routes[..., None] == expert_ids).astype(jnp.int32), axis=-2)
    earlier = jnp.cumsum(member, axis=2) - member
    placed = member[..., None] * (earlier[..., None] == slot_ids).astype(jnp.int32)
    updated_rows = updated.reshape(batch_count, dev_count, row_count, column_width)
    outgoing = jnp.einsum(
        "bdrej,bdrc->dejbc",
        placed.astype(jnp.bfloat16),
        updated_rows,
        preferred_element_type=jnp.float32,
    ).astype(jnp.bfloat16)
    arrived = lax.all_to_all(
        lax.all_to_all(outgoing, "dev", split_axis=0, concat_axis=4, tiled=True),
        "side",
        split_axis=1,
        concat_axis=1,
        tiled=True,
    )[0]
    block_routes = lax.dynamic_slice_in_dim(routes, dev_index * row_count, row_count, axis=1)
    chosen = jnp.sum((block_routes == side_index).astype(jnp.int32), axis=-1)
    counts = jnp.sum(chosen, axis=1)
    offsets = jnp.cumsum(counts, axis=1) - counts
    slot_place = offsets[:, :, None] + slot_ids
    filled = slot_ids < counts[:, :, None]
    capacity_ids = jnp.arange(capacity, dtype=jnp.int32)
    picker = ((slot_place[..., None] == capacity_ids) & filled[..., None]).astype(jnp.bfloat16)
    packed = jnp.einsum(
        "bsjp,sjbd->pbd", picker, arrived, preferred_element_type=jnp.float32
    ).astype(jnp.bfloat16)
    normed = normalize(packed, norm_gain)
    rows_piece = lax.all_gather(normed, "dev", axis=0, tiled=True)
    gate_part = jnp.einsum("nbd,fd->nbf", rows_piece, w_gate[0], preferred_element_type=jnp.float32)
    up_part = jnp.einsum("nbd,fd->nbf", rows_piece, w_up[0], preferred_element_type=jnp.float32)
    hidden = (jax.nn.silu(gate_part) * up_part).astype(jnp.bfloat16)
    summed = lax.psum_scatter(
        jnp.einsum("nbf,fd->nbd", hidden, w_down[0], preferred_element_type=jnp.float32).astype(
            jnp.bfloat16
        ),
        "dev",
        scatter_dimension=0,
        tiled=True,
    )
    unpacked = jnp.einsum(
        "bsjp,pbd->sjbd", picker, summed, preferred_element_type=jnp.float32
    ).astype(jnp.bfloat16)
    unpacked = unpacked.reshape(side_count, row_count, batch_count, dev_count, column_width)
    returned = lax.all_to_all(
        lax.all_to_all(unpacked, "dev", split_axis=3, concat_axis=1, tiled=True),
        "side",
        split_axis=0,
        concat_axis=0,
        tiled=True,
    )
    column_probs = route_probs[:, :, 0, :].reshape(batch_count, dev_count, row_count, top_count)
    gate_weights = column_probs / jnp.sum(column_probs, axis=-1, keepdims=True)
    gate_by_expert = jnp.sum(
        gate_weights[..., None] * (column_routes[..., None] == expert_ids), axis=-2
    )
    coefficient = placed.astype(jnp.float32) * gate_by_expert[..., None]
    values = (
        returned[:, :, :, 0, :]
        .reshape(side_count, dev_count, row_count, batch_count, column_width)
        .astype(jnp.float32)
    )
    mixture = jnp.einsum("bdrej,edjbc->bdrc", coefficient, values, precision=lax.Precision.HIGHEST)
    mixture = mixture.reshape(batch_count, dev_count * row_count, 1, column_width)
    return (updated.astype(jnp.float32) + mixture).astype(jnp.bfloat16)


def body(
    queries,
    cache_keys,
    cache_values,
    new_keys,
    new_values,
    lengths,
    out_weight,
    residual,
    norm_gain,
    routes,
    route_probs,
    w_gate,
    w_up,
    w_down,
):
    result = layer(
        queries,
        cache_keys,
        cache_values,
        new_keys,
        new_values,
        lengths,
        out_weight,
        residual,
        norm_gain,
        routes,
        route_probs,
        w_gate,
        w_up,
        w_down,
    )
    return result


def solution(mesh):
    placed = (
        P("groups", "dev", "side", None, None),
        P("groups", "dev", "side", None, None, None),
        P("groups", "dev", "side", None, None, None),
        P("groups", "dev", "side", None, None),
        P("groups", "dev", "side", None, None),
        P("groups", "dev", "side"),
        P(None, "dev"),
        P("groups", None, "side", "dev"),
        P(),
        P("groups", None, None, None),
        P("groups", None, "side", None),
        P("side", "dev", None),
        P("side", "dev", None),
        P("side", "dev", None),
    )
    return jax.shard_map(
        body,
        mesh=mesh,
        in_specs=placed,
        out_specs=P("groups", None, "side", "dev"),
        check_vma=False,
    )
```

profile of v0, /device:TPU:0, one launch (start us, length us, event | category | flops | bytes accessed | tf_op | source)
XLA Modules:
  0.0 114.3 jit_solution(13071021562852089729)
XLA Ops:
  6.5 1.1 dynamic-slice_reduce_fusion
  7.7 0.8 copy.76
  8.5 0.8 iota_compare_fusion.3
  9.3 0.7 bitcast_convert_fusion
  10.0 0.8 fusion.57
  11.3 1.4 %fusion.40 = bf16[2,2,4,6,128]{4,3,2,1,0:T(8,128)(2,1)S(1)} fusion(bf16[2,2,128,4,128]{4,3,2,1,0:T(4,128)(2,1)} %bitcast.119, f32[2,2,4,6,128]{4,3,2,1,0:T(8,128)S(1)} %get-tuple-element.8, f32[2,2,4,128]{3,2,1,0:T(4,128)S(1)} %bitcast_convert_fusion, f32[2,2,4,6]{3,2,1,0:T(4,128)S(1)} %get-tuple-element.6, f32[2,2,4,6]{3,2,1,0:T(4,128)S(1)} %get-tuple-element.5), kind=kOutput, calls=%fused_computation.28 | convolution fusion | flops 3207168 | bytes 606976 | tf_op jit(solution)/shard_map/...kgc,...ckd->...kgd/dot_general | solution.py:33
  12.7 1.9 %all_gather.6 = bf16[2,4,1,3072]{3,0,2,1:T(2,128)(2,1)S(1)} all-gather(bf16[2,2,1,3072]{3,0,2,1:T(2,128)(2,1)S(1)} %copy.80), channel_id=1, replica_groups=mesh['groups'=2,'dev'=2,'side'=8] {'dev'}, dimensions={1}, use_global_device_ids=true | all-gather | bytes 73728 | tf_op jit(solution)/shard_map/all_gather | solution.py:78
  14.6 5.1 %fusion.35 = bf16[2,4,1,1536]{3,1,0,2:T(4,128)(2,1)S(1)} fusion(bf16[3072,1536]{1,0:T(8,128)(2,1)} %param.20, bf16[2,4,1,3072]{3,0,2,1:T(2,128)(2,1)S(1)} %all_gather.6, bf16[2,4,1,1536]{3,1,2,0:T(4,128)(2,1)} %param.21), kind=kOutput, calls=%fused_computation.23 | convolution fusion | flops 75558912 | bytes 9535488 | tf_op jit(solution)/shard_map/brsk,kc->brsc/dot_general | solution.py:76
  20.0 3.9 %all_to_all.46 = bf16[2,8,2,2,1536]{4,1,2,3,0:T(8,128)(2,1)S(1)} all-to-all(bf16[2,8,2,2,1536]{4,1,2,3,0:T(8,128)(2,1)S(1)} %fusion.22), channel_id=1, replica_groups=mesh['groups'=2,'dev'=2,'side'=8] {'dev'}, dimensions={0} | all-to-all | bytes 393216 | tf_op jit(solution)/shard_map/all_to_all | solution.py:98
  24.1 0.8 reshape.150
  24.9 7.1 %all-to-all-start.1 = ((bf16[1,8,2,2,3072]{4,2,3,0,1:T(2,128)(2,1)}), bf16[1,8,2,2,3072]{4,2,3,0,1:T(2,128)(2,1)S(1)}, u32[]{:S(2)}, u32[]{:S(2)}) async-start(bf16[1,8,2,2,3072]{4,2,3,0,1:T(2,128)(2,1)} %reshape.150), calls=%async_computation.1 | async-start | bytes 393216 | tf_op jit(solution)/shard_map/all_to_all | solution.py:97
  32.1 0.7 convert_reduce_fusion.1
  33.0 7.3 %all-to-all-done.1 = bf16[1,8,2,2,3072]{4,2,3,0,1:T(2,128)(2,1)S(1)} async-done(((bf16[1,8,2,2,3072]{4,2,3,0,1:T(2,128)(2,1)}), bf16[1,8,2,2,3072]{4,2,3,0,1:T(2,128)(2,1)S(1)}, u32[]{:S(2)}, u32[]{:S(2)}) %all-to-all-start.1) | async-done | bytes 196640 | tf_op jit(solution)/shard_map/all_to_all | solution.py:97
  41.2 2.0 %all_gather.7 = bf16[18,2,3072]{2,1,0:T(2,128)(2,1)S(1)} all-gather(bf16[9,2,3072]{2,1,0:T(2,128)(2,1)S(1)} %copy.87), channel_id=1, replica_groups=mesh['groups'=2,'dev'=2,'side'=8] {'dev'}, dimensions={0}, use_global_device_ids=true | all-gather | bytes 331776 | tf_op jit(solution)/shard_map/all_gather | solution.py:116
  43.2 10.6 %fusion.4 = f32[18,2,2688]{2,0,1:T(8,128)S(1)} fusion(bf16[1,2688,3072]{2,1,0:T(8,128)(2,1)} %param.25, bf16[18,2,3072]{2,1,0:T(2,128)(2,1)S(1)} %all_gather.7), kind=kOutput, calls=%fused_computation.4 | convolution fusion | flops 594542592 | bytes 17123328 | tf_op jit(solution)/shard_map/nbd,fd->nbf/dot_general | solution.py:117
  53.8 14.7 %fusion.14 = bf16[18,2,3072]{2,0,1:T(8,128)(2,1)S(1)} fusion(bf16[1,2688,3072]{2,1,0:T(8,128)(2,1)} %param.27, bf16[1,2688,3072]{2,1,0:T(8,128)(2,1)} %param.26, f32[18,2,2688]{2,0,1:T(8,128)S(1)} %fusion.4, bf16[18,2,3072]{2,1,0:T(2,128)(2,1)S(1)} %all_gather.7), kind=kOutput, calls=%fused_computation.10 | convolution fusion | flops 1189776384 | bytes 33859584 | tf_op jit(solution)/shard_map/nbf,fd->nbd/dot_general | solution.py:121
  68.5 0.9 copy.90
  70.9 15.4 %all-reduce.3.cloned.1.call-done = bf16[18,2,3072]{2,1,0:T(2,128)(2,1)} async-done(((bf16[18,2,3072]{2,1,0:T(2,128)(2,1)}), bf16[18,2,3072]{2,1,0:T(2,128)(2,1)}) %all-reduce.3.cloned.1.call-update) | async-done | bytes 221200
  86.3 1.0 dynamic-slice_bitcast_fusion
  87.6 3.9 %all_to_all.47 = bf16[8,2,2,2,1536]{4,0,2,1,3:T(8,128)(2,1)S(1)} all-to-all(bf16[8,2,2,2,1536]{4,0,2,1,3:T(8,128)(2,1)S(1)} %copy.92), channel_id=1, replica_groups=mesh['groups'=2,'dev'=2,'side'=8] {'dev'}, dimensions={3} | all-to-all | bytes 393216 | tf_op jit(solution)/shard_map/all_to_all | solution.py:133
  91.5 0.8 copy.93
  92.3 5.8 %all-to-all-start.3 = ((bf16[8,4,2,1,1536]{4,1,3,2,0:T(4,128)(2,1)}), bf16[8,4,2,1,1536]{4,1,3,2,0:T(4,128)(2,1)S(1)}, u32[]{:S(2)}, u32[]{:S(2)}) async-start(bf16[8,4,2,1,1536]{4,1,3,2,0:T(4,128)(2,1)} %copy.93), calls=%async_computation.3 | async-start | bytes 393216 | tf_op jit(solution)/shard_map/all_to_all | solution.py:132
  98.3 8.1 %all-to-all-done.3 = bf16[8,4,2,1,1536]{4,1,3,2,0:T(4,128)(2,1)S(1)} async-done(((bf16[8,4,2,1,1536]{4,1,3,2,0:T(4,128)(2,1)}), bf16[8,4,2,1,1536]{4,1,3,2,0:T(4,128)(2,1)S(1)}, u32[]{:S(2)}, u32[]{:S(2)}) %all-to-all-start.3) | async-done | bytes 196640 | tf_op jit(solution)/shard_map/all_to_all | solution.py:132
  106.8 0.6 fusion.61
  (40 shorter events, 3.9 us)
Async XLA Ops:
  6.5 4.2 %copy-start = (bf16[2,2,1,128,4,128]{5,4,3,2,1,0:T(4,128)(2,1)S(1)}, bf16[2,2,1,128,4,128]{5,4,3,2,1,0:T(4,128)(2,1)}, u32[]{:S(2)}) copy-start(bf16[2,2,1,128,4,128]{5,4,3,2,1,0:T(4,128)(2,1)} %param.15) | copy-start | bytes 1572868
  6.5 34.4 %copy-start.2 = (f32[3072]{0:T(1024)S(1)}, f32[3072]{0:T(1024)}, u32[]{:S(2)}) copy-start(f32[3072]{0:T(1024)} %param.22) | copy-start | bytes 36868
  24.9 15.4 %all-to-all-start.1 = ((bf16[1,8,2,2,3072]{4,2,3,0,1:T(2,128)(2,1)}), bf16[1,8,2,2,3072]{4,2,3,0,1:T(2,128)(2,1)S(1)}, u32[]{:S(2)}, u32[]{:S(2)}) async-start(bf16[1,8,2,2,3072]{4,2,3,0,1:T(2,128)(2,1)} %reshape.150), calls=%async_computation.1 | async-start | bytes 393216 | tf_op jit(solution)/shard_map/all_to_all | solution.py:97
  32.0 54.3 %all-reduce.3.cloned.1.call-start = ((), (), s32[]{:S(2)}) async-start(), calls=%async_computation.4 | async-start | bytes 442368
  53.8 15.7 %copy-start.1 = (f32[2,4,1,4]{3,2,1,0:T(1,128)S(1)}, f32[2,4,1,4]{3,2,1,0:T(1,128)}, u32[]{:S(2)}) copy-start(f32[2,4,1,4]{3,2,1,0:T(1,128)} %param.24) | copy-start | bytes 388
  53.8 15.9 %copy-start.3 = (u32[32]{0:T(128)S(1)}, u32[32]{0:T(128)}, u32[]{:S(2)}) copy-start(u32[32]{0:T(128)} %constant.55) | copy-start | bytes 388
  92.3 14.1 %all-to-all-start.3 = ((bf16[8,4,2,1,1536]{4,1,3,2,0:T(4,128)(2,1)}), bf16[8,4,2,1,1536]{4,1,3,2,0:T(4,128)(2,1)S(1)}, u32[]{:S(2)}, u32[]{:S(2)}) async-start(bf16[8,4,2,1,1536]{4,1,3,2,0:T(4,128)(2,1)} %copy.93), calls=%async_computation.3 | async-start | bytes 393216 | tf_op jit(solution)/shard_map/all_to_all | solution.py:132
Sparse Core Ops, SparseCore 0:
  69.6 16.6 all-reduce.2
where the time goes:
time: 115 us; the launch traced here: 114 us
  matrix products  34.2 us (30%)
  waiting for transfers between devices  30.8 us (27%)
  between operations  14.2 us (12%)
  starting transfers between devices  13 us (11%)
  blocking collectives  11.7 us (10%)
  local copies, waits for them, and re-layouts  6.55 us (6%)
  other arithmetic  3.81 us (3%)
    unnamed x2, waiting for transfers between devices  15.4 us
    dot_general x1, matrix products, layer(): jnp.einsum('nbf,fd->nbd', hidden, w_down[0], preferred_element_type=jnp.f...  14.7 us
    dot_general x1, matrix products, layer(): jnp.einsum('nbd,fd->nbf', rows_piece, w_gate[0], preferred_element_type=j...  10.6 us
    all_to_all x1, waiting for transfers between devices, layer(): lax.all_to_all(lax.all_to_all(unpacked, 'dev', split_axis=3, concat_axis=...  8.09 us
    all_to_all x1, waiting for transfers between devices, layer(): lax.all_to_all(lax.all_to_all(outgoing, 'dev', split_axis=0, concat_axis=...  7.29 us
    all_to_all x1, starting transfers between devices, layer(): lax.all_to_all(lax.all_to_all(outgoing, 'dev', split_axis=0, concat_axis=...  7.14 us
    all_to_all x1, starting transfers between devices, layer(): lax.all_to_all(lax.all_to_all(unpacked, 'dev', split_axis=3, concat_axis=...  5.8 us
    dot_general x1, matrix products, layer(): jnp.einsum('brsk,kc->brsc', lax.all_gather(attended, 'dev', axis=1, tiled...  5.07 us
  transfers between devices with their start and end apart: 3, of which 3 were waited for; matrix products, arithmetic and copies ran while one was open for 2% of the time, Pallas kernels for 0%

commit v1 on v0

v1 whole, which is shorter than its diff:
```python
import functools
import math

import jax
import jax.numpy as jnp
from jax import lax
from jax.experimental import pallas as pl
from jax.experimental.pallas import tpu as pltpu
from jax.sharding import PartitionSpec as P

norm_epsilon = 1e-05
vmem_bytes = 60 * 1024 * 1024
last_last = (((1,), (1,)), ((), ()))

smem_spec = pl.BlockSpec(memory_space=pltpu.SMEM)
vmem_spec = pl.BlockSpec(memory_space=pltpu.VMEM)


def attend_kernel(lengths, queries, keys, values, new_keys, new_values, out, scratch):
    row_count, head_count, head_width = queries.shape
    pair_count = keys.shape[1]
    key_heads = new_keys.shape[1]
    width = head_count // key_heads
    local_rows = lengths.shape[2]
    factor = 1.0 / math.sqrt(head_width)
    pair = lax.broadcasted_iota(jnp.int32, (head_count, pair_count), 1)
    head = lax.broadcasted_iota(jnp.int32, (head_count, pair_count), 0)
    own_key = (pair % key_heads) == (head // width)
    position = jnp.where(own_key, pair // key_heads, pair_count)
    key_head = lax.broadcasted_iota(jnp.int32, (head_count, head_width), 0) // width

    def spread(block):
        wide = block.astype(jnp.float32)
        result = jnp.zeros((head_count, head_width), jnp.float32)
        for index in range(key_heads):
            result = jnp.where(key_head == index, wide[index : index + 1, :], result)
        return result

    for row in range(row_count):
        query = queries[row]
        scores = (
            lax.dot_general(query, keys[row], last_last, preferred_element_type=jnp.float32)
            * factor
        )
        length = lengths[row // local_rows, 0, row % local_rows]
        raised = jnp.where(position < length, jnp.exp(scores), 0.0)
        fresh = (
            jnp.sum(query.astype(jnp.float32) * spread(new_keys[row]), axis=-1, keepdims=True)
            * factor
        )
        raised_new = jnp.exp(fresh)
        denominator = jnp.sum(raised, axis=-1, keepdims=True) + raised_new
        weights = (raised / denominator).astype(jnp.bfloat16)
        weight_new = (raised_new / denominator).astype(jnp.bfloat16).astype(jnp.float32)
        mixed = jnp.dot(weights, values[row], preferred_element_type=jnp.float32)
        mixed = mixed + weight_new * spread(new_values[row])
        scratch[pl.ds(row * head_count, head_count), :] = mixed
    pieces = [
        scratch[pl.ds(index, row_count, stride=head_count), :] for index in range(head_count)
    ]
    out[...] = jnp.concatenate(pieces, axis=1).astype(jnp.bfloat16)


def attend(queries, cache_keys, cache_values, new_keys, new_values, lengths):
    batch_count, local_rows = queries.shape[:2]
    rows = batch_count * local_rows
    head_count, head_width = queries.shape[-2:]
    key_heads = cache_keys.shape[-2]
    pairs = cache_keys.shape[-3] * key_heads
    return pl.pallas_call(
        attend_kernel,
        out_shape=jax.ShapeDtypeStruct((rows, head_count * head_width), jnp.bfloat16),
        in_specs=[smem_spec] + [vmem_spec] * 5,
        out_specs=vmem_spec,
        scratch_shapes=[pltpu.VMEM((rows * head_count, head_width), jnp.float32)],
        compiler_params=pltpu.CompilerParams(vmem_limit_bytes=vmem_bytes),
        name="attend",
    )(
        jnp.swapaxes(lengths, 1, 2),
        queries.reshape(rows, head_count, head_width),
        cache_keys.reshape(rows, pairs, head_width),
        cache_values.reshape(rows, pairs, head_width),
        new_keys.reshape(rows, key_heads, head_width),
        new_values.reshape(rows, key_heads, head_width),
    )


def halves(dev_index, own, other):
    first = jnp.where(dev_index == 0, own, other)
    second = jnp.where(dev_index == 0, other, own)
    return first, second


def project_kernel(dev_count, *refs):
    attended, (out_weight, residual, updated, copies, total) = refs[:-5], refs[-5:]
    batch_count, row_count, _ = residual.shape
    local_rows = row_count // dev_count
    step = pl.program_id(0)
    depth = out_weight.shape[0]
    columns = pl.ds(pl.multiple_of(step * depth, depth), depth)
    dev_index = lax.axis_index("dev")

    @pl.when(step == 0)
    def _():
        total[...] = jnp.zeros_like(total)

    parts = [ref[:, columns] for ref in attended]
    if len(parts) == 2:
        parts = [p.astype(jnp.float32) for p in parts]
        rows = jnp.concatenate(halves(dev_index, *parts), axis=0).astype(jnp.bfloat16)
    else:
        rows = parts[0]
    total[...] += jnp.dot(rows, out_weight[...], preferred_element_type=jnp.float32)

    @pl.when(step == pl.num_programs(0) - 1)
    def _():
        result = total[...]
        for batch in range(batch_count):
            pieces = []
            for dev in range(dev_count):
                start = (dev * batch_count + batch) * local_rows
                pieces.append(result[start : start + local_rows, :])
            projected = jnp.concatenate(pieces, axis=0).astype(jnp.bfloat16)
            rows = (
                residual[batch].astype(jnp.float32) + projected.astype(jnp.float32)
            ).astype(jnp.bfloat16)
            updated[batch] = rows
            for side in range(copies.shape[0]):
                copies[side, batch] = rows


def project(attended, out_weight, residual, dev_count, side_count):
    batch_count, row_count, width = residual.shape
    inner = out_weight.shape[0]
    depth = 512
    rows = batch_count * row_count
    return pl.pallas_call(
        functools.partial(project_kernel, dev_count),
        grid=(inner // depth,),
        out_shape=(
            jax.ShapeDtypeStruct((batch_count, row_count, width), jnp.bfloat16),
            jax.ShapeDtypeStruct((side_count, batch_count, row_count, width), jnp.bfloat16),
        ),
        in_specs=[pl.BlockSpec(part.shape, lambda k: (0, 0)) for part in attended]
        + [
            pl.BlockSpec((depth, width), lambda k: (k, 0)),
            pl.BlockSpec((batch_count, row_count, width), lambda k: (0, 0, 0)),
        ],
        out_specs=(
            pl.BlockSpec((batch_count, row_count, width), lambda k: (0, 0, 0)),
            pl.BlockSpec((side_count, batch_count, row_count, width), lambda k: (0, 0, 0, 0)),
        ),
        scratch_shapes=[pltpu.VMEM((rows, width), jnp.float32)],
        compiler_params=pltpu.CompilerParams(vmem_limit_bytes=vmem_bytes),
        name="project",
    )(*attended, out_weight, residual)


def expert_kernel(dev_count, part_count, *refs):
    parts, refs = refs[:part_count], refs[part_count:]
    gain, w_gate, w_up, w_down = refs[:4]
    outs, (normed, total) = refs[4:-2], refs[-2:]
    step = pl.program_id(1)
    dev_index = lax.axis_index("dev")

    @pl.when(step == 0)
    def _():
        wide = [part[...].astype(jnp.float32) for part in parts]
        if part_count == 2:
            wide = halves(dev_index, *wide)
        values = jnp.concatenate(wide, axis=1) if part_count > 1 else wide[0]
        center = jnp.mean(values, axis=-1, keepdims=True)
        values = values - center
        spread = jnp.mean(jnp.square(values), axis=-1, keepdims=True)
        normed[...] = (values * lax.rsqrt(spread + norm_epsilon) * gain[...]).astype(jnp.bfloat16)
        total[...] = jnp.zeros_like(total)

    rows = normed[...]
    gate = lax.dot_general(rows, w_gate[...], last_last, preferred_element_type=jnp.float32)
    up = lax.dot_general(rows, w_up[...], last_last, preferred_element_type=jnp.float32)
    hidden = (gate / (1.0 + jnp.exp(-gate)) * up).astype(jnp.bfloat16)
    total[...] += jnp.dot(hidden, w_down[...], preferred_element_type=jnp.float32)

    @pl.when(step == pl.num_programs(1) - 1)
    def _():
        if len(outs) == 2:
            half = total.shape[1] // 2
            low, high = total[:, :half], total[:, half:]
            outs[0][...] = jnp.where(dev_index == 0, low, high).astype(jnp.bfloat16)
            outs[1][...] = jnp.where(dev_index == 0, high, low).astype(jnp.bfloat16)
        else:
            outs[0][...] = total[...].astype(jnp.bfloat16)


def experts(parts, gain, w_gate, w_up, w_down, dev_count):
    rows = parts[0].shape[0]
    units, width = w_gate.shape
    block = min(rows, 128)
    chunk = 384 if units % 384 == 0 else units
    out_width = width // 2 if dev_count == 2 else width
    out_count = 2 if dev_count == 2 else 1
    return pl.pallas_call(
        functools.partial(expert_kernel, dev_count, len(parts)),
        grid=(rows // block, units // chunk),
        out_shape=[jax.ShapeDtypeStruct((rows, out_width), jnp.bfloat16)] * out_count,
        in_specs=[pl.BlockSpec((block, part.shape[1]), lambda r, f: (r, 0)) for part in parts]
        + [pl.BlockSpec((1, width), lambda r, f: (0, 0))]
        + [pl.BlockSpec((chunk, width), lambda r, f: (f, 0))] * 3,
        out_specs=[pl.BlockSpec((block, out_width), lambda r, f: (r, 0))] * out_count,
        scratch_shapes=[
            pltpu.VMEM((block, width), jnp.bfloat16),
            pltpu.VMEM((block, width), jnp.float32),
        ],
        compiler_params=pltpu.CompilerParams(vmem_limit_bytes=vmem_bytes),
        name="experts",
    )(*parts, gain.reshape(1, width), w_gate, w_up, w_down)


def combine_kernel(routes, probs, updated, returned, out):
    side_count = returned.shape[0]
    batch_count, row_count, width = updated.shape
    top_count = routes.shape[2]
    side_index = lax.axis_index("side")
    row_ids = lax.broadcasted_iota(jnp.int32, (row_count, 128), 0)
    lane_ids = lax.broadcasted_iota(jnp.int32, (row_count, 128), 1)
    for batch in range(batch_count):

        def place(row, shares):
            for top in range(top_count):
                expert = routes[batch, row, top, side_index]
                shares = jnp.where(
                    (row_ids == row) & (lane_ids == expert), probs[batch, row, 0, top], shares
                )
            return shares

        shares = jnp.zeros((row_count, 128), jnp.float32)
        if row_count <= 8:
            for row in range(row_count):
                shares = place(row, shares)
        else:
            shares = lax.fori_loop(0, row_count, place, shares)
        shares = shares / jnp.sum(shares, axis=-1, keepdims=True)
        mixture = jnp.zeros((row_count, width), jnp.float32)
        for expert in range(side_count):
            mixture = mixture + shares[:, expert : expert + 1] * returned[
                expert, batch
            ].astype(jnp.float32)
        out[batch] = (updated[batch].astype(jnp.float32) + mixture).astype(jnp.bfloat16)


def combine(routes, probs, updated, returned):
    return pl.pallas_call(
        combine_kernel,
        out_shape=jax.ShapeDtypeStruct(updated.shape, jnp.bfloat16),
        in_specs=[smem_spec, smem_spec, vmem_spec, vmem_spec],
        out_specs=vmem_spec,
        compiler_params=pltpu.CompilerParams(vmem_limit_bytes=vmem_bytes),
        name="combine",
    )(jnp.swapaxes(routes, 2, 3), probs, updated, returned)


def body(
    queries,
    cache_keys,
    cache_values,
    new_keys,
    new_values,
    lengths,
    out_weight,
    residual,
    norm_gain,
    routes,
    route_probs,
    w_gate,
    w_up,
    w_down,
):
    side_count = lax.axis_size("side")
    dev_count = lax.axis_size("dev")
    batch_count, row_count, _, column_width = residual.shape
    rows = batch_count * row_count
    swap = [(0, 1), (1, 0)]

    attended = attend(queries, cache_keys, cache_values, new_keys, new_values, lengths)
    if dev_count == 2:
        attended = (attended, lax.ppermute(attended, "dev", swap))
    else:
        attended = (lax.all_gather(attended, "dev", axis=0, tiled=True),)
    updated, copies = project(
        attended,
        out_weight,
        residual.reshape(batch_count, row_count, column_width),
        dev_count,
        side_count,
    )
    arrived = lax.all_to_all(copies, "side", split_axis=0, concat_axis=0, tiled=True)
    arrived = arrived.reshape(side_count * rows, column_width)
    if dev_count == 2:
        parts = (arrived, lax.ppermute(arrived, "dev", swap))
    else:
        parts = (lax.all_gather(arrived, "dev", axis=1, tiled=True),)
    sums = experts(parts, norm_gain, w_gate[0], w_up[0], w_down[0], dev_count)
    if dev_count == 2:
        own, given = sums
        total = own.astype(jnp.float32) + lax.ppermute(given, "dev", swap).astype(jnp.float32)
    else:
        pieces = sums[0].reshape(side_count * rows, dev_count, column_width)
        pieces = lax.all_to_all(pieces, "dev", split_axis=1, concat_axis=1, tiled=True)
        total = jnp.sum(pieces.astype(jnp.float32), axis=1)
    total = total.astype(jnp.bfloat16).reshape(side_count, batch_count, row_count, column_width)
    returned = lax.all_to_all(total, "side", split_axis=0, concat_axis=0, tiled=True)
    result = combine(routes, route_probs, updated, returned)
    return result.reshape(residual.shape)


def solution(mesh):
    placed = (
        P("groups", "dev", "side", None, None),
        P("groups", "dev", "side", None, None, None),
        P("groups", "dev", "side", None, None, None),
        P("groups", "dev", "side", None, None),
        P("groups", "dev", "side", None, None),
        P("groups", "dev", "side"),
        P(None, "dev"),
        P("groups", None, "side", "dev"),
        P(),
        P("groups", None, None, None),
        P("groups", None, "side", None),
        P("side", "dev", None),
        P("side", "dev", None),
        P("side", "dev", None),
    )
    return jax.shard_map(
        body,
        mesh=mesh,
        in_specs=placed,
        out_specs=P("groups", None, "side", "dev"),
        check_vma=False,
    )
```

time: 115 us -> 68.6 us (0.60)
  matrix products: 34.2 us -> 0 us
  Pallas kernels: 0 us -> 34.1 us
  waiting for transfers between devices: 30.8 us -> 4 us
  blocking collectives: 11.7 us -> 27 us
  between operations: 14.2 us -> 0.04 us
  starting transfers between devices: 13 us -> 0.67 us
  local copies, waits for them, and re-layouts: 6.55 us -> 1.39 us
  other arithmetic: 3.81 us -> 0.98 us
    dot_general x10 -> x0, matrix products: 34.2 us -> none  [the longest x1 14.7 us: layer(): jnp.einsum('nbf,fd->nbd', hidden, w_down[0], preferred_element_type=jnp.f...]
    pallas_call x0 -> x4, Pallas kernels: none -> 34.1 us  [the longest x1 22.5 us: experts(): pl.pallas_call(functools.partial(expert_kernel, dev_count, len(parts)), g...]
    all_to_all x2, blocking collectives: 7.78 us -> 27 us  [the longest x1 15.4 us: body(): lax.all_to_all(copies, 'side', split_axis=0, concat_axis=0, tiled=True)]
    unnamed x2 -> x0, waiting for transfers between devices: 15.4 us -> none
    all_to_all x2 -> x0, waiting for transfers between devices: 15.4 us -> none  [the longest x1 8.09 us: layer(): lax.all_to_all(lax.all_to_all(unpacked, 'dev', split_axis=3, concat_axis=...]
    all_to_all x2 -> x0, starting transfers between devices: 12.9 us -> none  [the longest x1 7.14 us: layer(): lax.all_to_all(lax.all_to_all(outgoing, 'dev', split_axis=0, concat_axis=...]
    ppermute x0 -> x3, waiting for transfers between devices: none -> 4 us  [the longest x1 1.51 us: body(): lax.ppermute(given, 'dev', swap).astype(jnp.float32)]
    all_gather x2 -> x0, blocking collectives: 3.91 us -> none  [the longest x1 1.96 us: layer(): rows_piece = lax.all_gather(normed, 'dev', axis=0, tiled=True)]
  transfers between devices with their start and end apart: 3 -> 3, of which waited for: 3 -> 3; matrix products, arithmetic and copies ran while one was open for 2% -> 0% of each run, Pallas kernels for 0% -> 0%
where the time goes in v1:
time: 68.6 us; the launch traced here: 68.2 us
  Pallas kernels  34.1 us (50%)
  blocking collectives  27 us (39%)
  waiting for transfers between devices  4 us (6%)
  local copies, waits for them, and re-layouts  1.39 us (2%)
  other arithmetic  0.98 us (1%)
    pallas_call x1, Pallas kernels, experts(): pl.pallas_call(functools.partial(expert_kernel, dev_count, len(parts)), g...  22.5 us
    all_to_all x1, blocking collectives, body(): lax.all_to_all(copies, 'side', split_axis=0, concat_axis=0, tiled=True)  15.4 us
    all_to_all x1, blocking collectives, body(): lax.all_to_all(total, 'side', split_axis=0, concat_axis=0, tiled=True)  11.6 us
    pallas_call x1, Pallas kernels, project(): pl.pallas_call(functools.partial(project_kernel, dev_count), grid=(inner...  6.65 us
    pallas_call x1, Pallas kernels, attend(): pl.pallas_call(attend_kernel, out_shape=jax.ShapeDtypeStruct((rows, head_...  3.09 us
    pallas_call x1, Pallas kernels, combine(): pl.pallas_call(combine_kernel, out_shape=jax.ShapeDtypeStruct(updated.sha...  1.87 us
    ppermute x1, waiting for transfers between devices, body(): lax.ppermute(given, 'dev', swap).astype(jnp.float32)  1.51 us
    ppermute x1, waiting for transfers between devices, body(): parts = (arrived, lax.ppermute(arrived, 'dev', swap))  1.43 us
  transfers between devices with their start and end apart: 3, of which 3 were waited for; matrix products, arithmetic and copies ran while one was open for 0% of the time, Pallas kernels for 0%

profile of v1, /device:TPU:0, one launch (start us, length us, event | category | flops | bytes accessed | tf_op | source)
XLA Modules:
  0.0 68.2 jit_solution(5389814366774139103)
XLA Ops:
  0.0 3.1 %attend.1.refs_0_ = bf16[4,3072]{1,0:T(4,128)(2,1)} custom-call(s32[2,1,2]{2,1,0:T(1,128)} %bitcast.28, bf16[4,24,128]{2,1,0:T(8,128)(2,1)} %bitcast.22, bf16[4,512,128]{2,1,0:T(8,128)(2,1)} %bitcast.20, bf16[4,512,128]{2,1,0:T(8,128)(2,1)} %bitcast.21, bf16[4,4,128]{2,1,0:T(4,128)(2,1)} %bitcast.26, bf16[4,4,128]{2,1,0:T(4,128)(2,1)} %bitcast.27), custom_call_target="tpu_custom_call" | custom-call | tf_op jit(solution)/shard_map/attend/pallas_call | solution.py:70
  3.1 0.5 collective-permute-start
  3.5 1.1 %collective-permute-done.refs_1_ = bf16[4,3072]{1,0:T(4,128)(2,1)S(1)} collective-permute-done((bf16[4,3072]{1,0:T(4,128)(2,1)}, bf16[4,3072]{1,0:T(4,128)(2,1)S(1)}, u32[]{:S(2)}, u32[]{:S(2)}) %collective-permute-start) | collective-permute-done | bytes 24608 | tf_op jit(solution)/shard_map/ppermute | solution.py:286
  4.6 0.0 copy-start.2
  4.6 0.6 copy-done.2
  5.2 6.6 %project.1 = (bf16[2,4,1536]{2,1,0:T(4,128)(2,1)}, bf16[8,2,4,1536]{3,2,1,0:T(4,128)(2,1)}) custom-call(bf16[4,3072]{1,0:T(4,128)(2,1)} %attend.1.refs_0_, bf16[4,3072]{1,0:T(4,128)(2,1)} %copy-done.2, bf16[3072,1536]{1,0:T(8,128)(2,1)} %refs_2_.1, bf16[2,4,1536]{2,1,0:T(4,128)(2,1)} %bitcast.23), custom_call_target="tpu_custom_call" | custom-call | tf_op jit(solution)/shard_map/project/pallas_call | solution.py:137
  11.9 15.4 %all_to_all.10 = bf16[8,2,4,1536]{3,2,1,0:T(4,128)(2,1)S(1)} all-to-all(bf16[8,2,4,1536]{3,2,1,0:T(4,128)(2,1)} %get-tuple-element.10), channel_id=1, replica_groups=mesh['groups'=2,'dev'=2,'side'=8] {'side'}, dimensions={0} | all-to-all | bytes 393216 | tf_op jit(solution)/shard_map/all_to_all | solution.py:296
  27.3 0.1 reshape.36.refs_0_
  27.3 0.0 copy-start
  27.4 0.1 collective-permute-start.1
  27.4 1.4 %collective-permute-done.1.refs_1_ = bf16[64,1536]{1,0:T(8,128)(2,1)S(1)} collective-permute-done((bf16[64,1536]{1,0:T(8,128)(2,1)S(1)}, bf16[64,1536]{1,0:T(8,128)(2,1)S(1)}, u32[]{:S(2)}, u32[]{:S(2)}) %collective-permute-start.1) | collective-permute-done | bytes 196640 | tf_op jit(solution)/shard_map/ppermute | solution.py:299
  28.9 0.0 copy-start.1
  28.9 0.0 copy-done
  28.9 0.7 copy-done.1
  29.5 22.5 %experts.1 = (bf16[64,1536]{1,0:T(8,128)(2,1)}, bf16[64,1536]{1,0:T(8,128)(2,1)}) custom-call(bf16[64,1536]{1,0:T(8,128)(2,1)} %copy-done, bf16[64,1536]{1,0:T(8,128)(2,1)} %copy-done.1, f32[1,3072]{1,0:T(1,128)} %bitcast.25, bf16[2688,3072]{1,0:T(8,128)(2,1)} %bitcast.17, bf16[2688,3072]{1,0:T(8,128)(2,1)} %bitcast.18, bf16[2688,3072]{1,0:T(8,128)(2,1)} %bitcast.19), custom_call_target="tpu_custom_call" | custom-call | tf_op jit(solution)/shard_map/experts/pallas_call | solution.py:202
  52.0 0.1 collective-permute-start.2
  52.2 1.5 %collective-permute-done.2 = bf16[64,1536]{1,0:T(8,128)(2,1)S(1)} collective-permute-done((bf16[64,1536]{1,0:T(8,128)(2,1)}, bf16[64,1536]{1,0:T(8,128)(2,1)S(1)}, u32[]{:S(2)}, u32[]{:S(2)}) %collective-permute-start.2) | collective-permute-done | bytes 196640 | tf_op jit(solution)/shard_map/ppermute | solution.py:305
  53.7 1.0 %add_convert_fusion = bf16[64,1536]{1,0:T(8,128)(2,1)S(1)} fusion(bf16[64,1536]{1,0:T(8,128)(2,1)S(1)} %collective-permute-done.2, bf16[64,1536]{1,0:T(8,128)(2,1)} %get-tuple-element.11), kind=kLoop, calls=%fused_computation | loop fusion | flops 393216 | bytes 589824 | tf_op jit(solution)/shard_map/convert_element_type | solution.py:310
  54.7 0.1 reshape.38
  54.7 11.6 %all_to_all.11.returned = bf16[8,2,4,1536]{3,2,1,0:T(4,128)(2,1)} all-to-all(bf16[8,2,4,1536]{3,2,1,0:T(4,128)(2,1)S(1)} %reshape.38), channel_id=1, replica_groups=mesh['groups'=2,'dev'=2,'side'=8] {'side'}, dimensions={0} | all-to-all | bytes 393216 | tf_op jit(solution)/shard_map/all_to_all | solution.py:311
  66.3 1.9 %combine.1 = bf16[2,4,1536]{2,1,0:T(4,128)(2,1)} custom-call(s32[2,4,4,8]{3,2,1,0:T(4,128)} %bitcast.24, f32[2,4,1,4]{3,2,1,0:T(1,128)} %probs.1, bf16[2,4,1536]{2,1,0:T(4,128)(2,1)} %get-tuple-element.9.updated, bf16[8,2,4,1536]{3,2,1,0:T(4,128)(2,1)} %all_to_all.11.returned), custom_call_target="tpu_custom_call" | custom-call | tf_op jit(solution)/shard_map/combine/pallas_call | solution.py:252
Async XLA Ops:
  3.1 1.5 %collective-permute-start = (bf16[4,3072]{1,0:T(4,128)(2,1)}, bf16[4,3072]{1,0:T(4,128)(2,1)S(1)}, u32[]{:S(2)}, u32[]{:S(2)}) collective-permute-start(bf16[4,3072]{1,0:T(4,128)(2,1)} %attend.1.refs_0_), channel_id=1, source_target_pairs={{0,8},{8,0},{1,9},{9,1},{2,10},{10,2},{3,11},{11,3},{4,12},{12,4},... | collective-permute-start | bytes 73736 | tf_op jit(solution)/shard_map/ppermute | solution.py:286
  4.6 0.6 copy-start.2
  27.3 1.5 %copy-start = (bf16[64,1536]{1,0:T(8,128)(2,1)}, bf16[64,1536]{1,0:T(8,128)(2,1)S(1)}, u32[]{:S(2)}) copy-start(bf16[64,1536]{1,0:T(8,128)(2,1)S(1)} %reshape.36.refs_0_) | copy-start | bytes 589828
  27.4 1.5 %collective-permute-start.1 = (bf16[64,1536]{1,0:T(8,128)(2,1)S(1)}, bf16[64,1536]{1,0:T(8,128)(2,1)S(1)}, u32[]{:S(2)}, u32[]{:S(2)}) collective-permute-start(bf16[64,1536]{1,0:T(8,128)(2,1)S(1)} %reshape.36.refs_0_), channel_id=1, source_target_pairs={{0,8},{8,0},{1,9},{9,1},{2,10},{10,2},{3,11},{11,3},{4,12},{12,4},... | collective-permute-start | bytes 589832 | tf_op jit(solution)/shard_map/ppermute | solution.py:299
  28.9 0.7 copy-start.1
  52.0 1.7 %collective-permute-start.2 = (bf16[64,1536]{1,0:T(8,128)(2,1)}, bf16[64,1536]{1,0:T(8,128)(2,1)S(1)}, u32[]{:S(2)}, u32[]{:S(2)}) collective-permute-start(bf16[64,1536]{1,0:T(8,128)(2,1)} %get-tuple-element.12), channel_id=1, source_target_pairs={{0,8},{8,0},{1,9},{9,1},{2,10},{10,2},{3,11},{11,3},{4,12},{12,4},... | collective-permute-start | bytes 589832 | tf_op jit(solution)/shard_map/ppermute | solution.py:305

commit v2 on v1

--- a/solution.py
+++ b/solution.py
@@ -9,7 +9,9 @@
 from jax.sharding import PartitionSpec as P
 
 norm_epsilon = 1e-05
-vmem_bytes = 60 * 1024 * 1024
+mebibyte = 1024 * 1024
+hint_flops = 20_000_000_000
+down_piece = 896
 last_last = (((1,), (1,)), ((), ()))
 
 smem_spec = pl.BlockSpec(memory_space=pltpu.SMEM)
@@ -73,8 +75,11 @@
         in_specs=[smem_spec] + [vmem_spec] * 5,
         out_specs=vmem_spec,
         scratch_shapes=[pltpu.VMEM((rows * head_count, head_width), jnp.float32)],
-        compiler_params=pltpu.CompilerParams(vmem_limit_bytes=vmem_bytes),
+        compiler_params=pltpu.CompilerParams(vmem_limit_bytes=8 * mebibyte),
         name="attend",
+        cost_estimate=pl.CostEstimate(
+            flops=hint_flops, transcendentals=0, bytes_accessed=cache_keys.size * 4
+        ),
     )(
         jnp.swapaxes(lengths, 1, 2),
         queries.reshape(rows, head_count, head_width),
@@ -92,128 +97,135 @@
 
 
 def project_kernel(dev_count, *refs):
-    attended, (out_weight, residual, updated, copies, total) = refs[:-5], refs[-5:]
+    attended, (out_weight, residual, updated, copies) = refs[:-4], refs[-4:]
     batch_count, row_count, _ = residual.shape
     local_rows = row_count // dev_count
-    step = pl.program_id(0)
-    depth = out_weight.shape[0]
-    columns = pl.ds(pl.multiple_of(step * depth, depth), depth)
-    dev_index = lax.axis_index("dev")
-
-    @pl.when(step == 0)
-    def _():
-        total[...] = jnp.zeros_like(total)
-
-    parts = [ref[:, columns] for ref in attended]
+    parts = [ref[...] for ref in attended]
     if len(parts) == 2:
-        parts = [p.astype(jnp.float32) for p in parts]
-        rows = jnp.concatenate(halves(dev_index, *parts), axis=0).astype(jnp.bfloat16)
+        parts = [part.astype(jnp.float32) for part in parts]
+        rows = jnp.concatenate(halves(lax.axis_index("dev"), *parts), axis=0).astype(jnp.bfloat16)
     else:
         rows = parts[0]
-    total[...] += jnp.dot(rows, out_weight[...], preferred_element_type=jnp.float32)
-
-    @pl.when(step == pl.num_programs(0) - 1)
-    def _():
-        result = total[...]
-        for batch in range(batch_count):
-            pieces = []
-            for dev in range(dev_count):
-                start = (dev * batch_count + batch) * local_rows
-                pieces.append(result[start : start + local_rows, :])
-            projected = jnp.concatenate(pieces, axis=0).astype(jnp.bfloat16)
-            rows = (
-                residual[batch].astype(jnp.float32) + projected.astype(jnp.float32)
-            ).astype(jnp.bfloat16)
-            updated[batch] = rows
-            for side in range(copies.shape[0]):
-                copies[side, batch] = rows
+    result = jnp.dot(rows, out_weight[...], preferred_element_type=jnp.float32)
+    whole = []
+    for batch in range(batch_count):
+        pieces = []
+        for dev in range(dev_count):
+            start = (dev * batch_count + batch) * local_rows
+            pieces.append(result[start : start + local_rows, :])
+        projected = jnp.concatenate(pieces, axis=0).astype(jnp.bfloat16)
+        rows = (residual[batch].astype(jnp.float32) + projected.astype(jnp.float32)).astype(
+            jnp.bfloat16
+        )
+        updated[batch] = rows
+        whole.append(rows.astype(jnp.float32))
+    whole = jnp.concatenate(whole, axis=0).astype(jnp.bfloat16)
+    for side in range(copies.shape[0]):
+        copies[side] = whole
 
 
 def project(attended, out_weight, residual, dev_count, side_count):
     batch_count, row_count, width = residual.shape
-    inner = out_weight.shape[0]
-    depth = 512
     rows = batch_count * row_count
     return pl.pallas_call(
         functools.partial(project_kernel, dev_count),
-        grid=(inner // depth,),
         out_shape=(
             jax.ShapeDtypeStruct((batch_count, row_count, width), jnp.bfloat16),
-            jax.ShapeDtypeStruct((side_count, batch_count, row_count, width), jnp.bfloat16),
+            jax.ShapeDtypeStruct((side_count, rows, width), jnp.bfloat16),
         ),
-        in_specs=[pl.BlockSpec(part.shape, lambda k: (0, 0)) for part in attended]
-        + [
-            pl.BlockSpec((depth, width), lambda k: (k, 0)),
-            pl.BlockSpec((batch_count, row_count, width), lambda k: (0, 0, 0)),
-        ],
-        out_specs=(
-            pl.BlockSpec((batch_count, row_count, width), lambda k: (0, 0, 0)),
-            pl.BlockSpec((side_count, batch_count, row_count, width), lambda k: (0, 0, 0, 0)),
+        in_specs=[vmem_spec] * (len(attended) + 2),
+        out_specs=(vmem_spec, vmem_spec),
+        compiler_params=pltpu.CompilerParams(vmem_limit_bytes=4 * mebibyte),
+        cost_estimate=pl.CostEstimate(
+            flops=hint_flops, transcendentals=0, bytes_accessed=out_weight.size * 2
         ),
-        scratch_shapes=[pltpu.VMEM((rows, width), jnp.float32)],
-        compiler_params=pltpu.CompilerParams(vmem_limit_bytes=vmem_bytes),
         name="project",
-    )(*attended, out_weight, residual)
+    )(*attended, pltpu.with_memory_space_constraint(out_weight, pltpu.VMEM), residual)
+
+
+def pieces_of(length, piece):
+    return [(start, min(piece, length - start)) for start in range(0, length, piece)]
 
 
 def expert_kernel(dev_count, part_count, *refs):
     parts, refs = refs[:part_count], refs[part_count:]
     gain, w_gate, w_up, w_down = refs[:4]
-    outs, (normed, total) = refs[4:-2], refs[-2:]
-    step = pl.program_id(1)
+    outs, (hidden, down, arrived) = refs[4:-3], refs[-3:]
+    units, width = w_gate.shape
     dev_index = lax.axis_index("dev")
-
-    @pl.when(step == 0)
+    copies = [
+        pltpu.make_async_copy(
+            w_down.at[pl.ds(start, size), :], down.at[pl.ds(start, size), :], arrived.at[index]
+        )
+        for index, (start, size) in enumerate(pieces_of(units, down_piece))
+    ]
+
+    @pl.when(pl.program_id(0) == 0)
     def _():
-        wide = [part[...].astype(jnp.float32) for part in parts]
-        if part_count == 2:
-            wide = halves(dev_index, *wide)
-        values = jnp.concatenate(wide, axis=1) if part_count > 1 else wide[0]
-        center = jnp.mean(values, axis=-1, keepdims=True)
-        values = values - center
-        spread = jnp.mean(jnp.square(values), axis=-1, keepdims=True)
-        normed[...] = (values * lax.rsqrt(spread + norm_epsilon) * gain[...]).astype(jnp.bfloat16)
-        total[...] = jnp.zeros_like(total)
-
-    rows = normed[...]
-    gate = lax.dot_general(rows, w_gate[...], last_last, preferred_element_type=jnp.float32)
-    up = lax.dot_general(rows, w_up[...], last_last, preferred_element_type=jnp.float32)
-    hidden = (gate / (1.0 + jnp.exp(-gate)) * up).astype(jnp.bfloat16)
-    total[...] += jnp.dot(hidden, w_down[...], preferred_element_type=jnp.float32)
-
-    @pl.when(step == pl.num_programs(1) - 1)
+        for copy in copies:
+            copy.start()
+
+    wide = [part[...].astype(jnp.float32) for part in parts]
+    if part_count == 2:
+        wide = halves(dev_index, *wide)
+    values = jnp.concatenate(wide, axis=1) if part_count > 1 else wide[0]
+    center = jnp.mean(values, axis=-1, keepdims=True)
+    values = values - center
+    spread = jnp.mean(jnp.square(values), axis=-1, keepdims=True)
+    rows = (values * lax.rsqrt(spread + norm_epsilon) * gain[...]).astype(jnp.bfloat16)
+    for start, size in pieces_of(units, 512):
+        span = slice(start, start + size)
+        gate = lax.dot_general(rows, w_gate[span, :], last_last, preferred_element_type=jnp.float32)
+        up = lax.dot_general(rows, w_up[span, :], last_last, preferred_element_type=jnp.float32)
+        hidden[:, span] = (gate / (1.0 + jnp.exp(-gate)) * up).astype(jnp.bfloat16)
+
+    @pl.when(pl.program_id(0) == 0)
     def _():
+        for copy in copies:
+            copy.wait()
+
+    half = width // 2
+    for start, size in pieces_of(half, 512):
+        low = jnp.dot(
+            hidden[...], down[:, start : start + size], preferred_element_type=jnp.float32
+        )
+        high = jnp.dot(
+            hidden[...],
+            down[:, half + start : half + start + size],
+            preferred_element_type=jnp.float32,
+        )
         if len(outs) == 2:
-            half = total.shape[1] // 2
-            low, high = total[:, :half], total[:, half:]
-            outs[0][...] = jnp.where(dev_index == 0, low, high).astype(jnp.bfloat16)
-            outs[1][...] = jnp.where(dev_index == 0, high, low).astype(jnp.bfloat16)
+            span = slice(start, start + size)
+            outs[0][:, span] = jnp.where(dev_index == 0, low, high).astype(jnp.bfloat16)
+            outs[1][:, span] = jnp.where(dev_index == 0, high, low).astype(jnp.bfloat16)
         else:
-            outs[0][...] = total[...].astype(jnp.bfloat16)
+            outs[0][:, start : start + size] = low.astype(jnp.bfloat16)
+            outs[0][:, half + start : half + start + size] = high.astype(jnp.bfloat16)
 
 
 def experts(parts, gain, w_gate, w_up, w_down, dev_count):
     rows = parts[0].shape[0]
     units, width = w_gate.shape
     block = min(rows, 128)
-    chunk = 384 if units % 384 == 0 else units
     out_width = width // 2 if dev_count == 2 else width
     out_count = 2 if dev_count == 2 else 1
+    resident = functools.partial(pltpu.with_memory_space_constraint, memory_space=pltpu.VMEM)
     return pl.pallas_call(
         functools.partial(expert_kernel, dev_count, len(parts)),
-        grid=(rows // block, units // chunk),
+        grid=(rows // block,),
         out_shape=[jax.ShapeDtypeStruct((rows, out_width), jnp.bfloat16)] * out_count,
-        in_specs=[pl.BlockSpec((block, part.shape[1]), lambda r, f: (r, 0)) for part in parts]
-        + [pl.BlockSpec((1, width), lambda r, f: (0, 0))]
-        + [pl.BlockSpec((chunk, width), lambda r, f: (f, 0))] * 3,
-        out_specs=[pl.BlockSpec((block, out_width), lambda r, f: (r, 0))] * out_count,
+        in_specs=[pl.BlockSpec((block, part.shape[1]), lambda r: (r, 0)) for part in parts]
+        + [pl.BlockSpec((1, width), lambda r: (0, 0)), vmem_spec, vmem_spec]
+        + [pl.BlockSpec(memory_space=pl.ANY)],
+        out_specs=[pl.BlockSpec((block, out_width), lambda r: (r, 0))] * out_count,
         scratch_shapes=[
-            pltpu.VMEM((block, width), jnp.bfloat16),
-            pltpu.VMEM((block, width), jnp.float32),
+            pltpu.VMEM((block, units), jnp.bfloat16),
+            pltpu.VMEM((units, width), jnp.bfloat16),
+            pltpu.SemaphoreType.DMA((len(pieces_of(units, down_piece)),)),
         ],
-        compiler_params=pltpu.CompilerParams(vmem_limit_bytes=vmem_bytes),
+        compiler_params=pltpu.CompilerParams(vmem_limit_bytes=19 * mebibyte),
         name="experts",
-    )(*parts, gain.reshape(1, width), w_gate, w_up, w_down)
+    )(*parts, gain.reshape(1, width), resident(w_gate), resident(w_up), w_down)
 
 
 def combine_kernel(routes, probs, updated, returned, out):
@@ -254,7 +266,7 @@
         out_shape=jax.ShapeDtypeStruct(updated.shape, jnp.bfloat16),
         in_specs=[smem_spec, smem_spec, vmem_spec, vmem_spec],
         out_specs=vmem_spec,
-        compiler_params=pltpu.CompilerParams(vmem_limit_bytes=vmem_bytes),
+        compiler_params=pltpu.CompilerParams(vmem_limit_bytes=8 * mebibyte),
         name="combine",
     )(jnp.swapaxes(routes, 2, 3), probs, updated, returned)
 

time: 68.6 us -> 60.7 us (0.88)
  Pallas kernels: 34.1 us -> 23.7 us
  local copies, waits for them, and re-layouts: 1.39 us -> 5.57 us
  other arithmetic: 0.98 us -> 0.05 us
    pallas_call x1, Pallas kernels: 6.65 us -> 1.34 us  [project(): pl.pallas_call(functools.partial(project_kernel, dev_count), out_shape=(j...]
    unnamed x6 -> x38, local copies, waits for them, and re-layouts: 1.28 us -> 5.51 us
    pallas_call x1, Pallas kernels: 22.5 us -> 19 us  [experts(): pl.pallas_call(functools.partial(expert_kernel, dev_count, len(parts)), g...]
    pallas_call x1, Pallas kernels: 3.09 us -> 1.69 us  [attend(): pl.pallas_call(attend_kernel, out_shape=jax.ShapeDtypeStruct((rows, head_...]
    convert_element_type x1, other arithmetic: 0.98 us -> 0.05 us  [body(): total.astype(jnp.bfloat16)]
where the time goes in v2:
time: 60.7 us; the launch traced here: 60.3 us
  blocking collectives  26.5 us (44%)
  Pallas kernels  23.7 us (39%)
  local copies, waits for them, and re-layouts  5.57 us (9%)
  waiting for transfers between devices  3.6 us (6%)
  starting transfers between devices  0.72 us (1%)
    pallas_call x1, Pallas kernels, experts(): pl.pallas_call(functools.partial(expert_kernel, dev_count, len(parts)), g...  19 us
    all_to_all x1, blocking collectives, body(): lax.all_to_all(copies, 'side', split_axis=0, concat_axis=0, tiled=True)  15.3 us
    all_to_all x1, blocking collectives, body(): lax.all_to_all(total, 'side', split_axis=0, concat_axis=0, tiled=True)  11.2 us
    unnamed x38, local copies, waits for them, and re-layouts  5.51 us
    pallas_call x1, Pallas kernels, combine(): pl.pallas_call(combine_kernel, out_shape=jax.ShapeDtypeStruct(updated.sha...  1.74 us
    pallas_call x1, Pallas kernels, attend(): pl.pallas_call(attend_kernel, out_shape=jax.ShapeDtypeStruct((rows, head_...  1.69 us
    ppermute x1, waiting for transfers between devices, body(): parts = (arrived, lax.ppermute(arrived, 'dev', swap))  1.44 us
    pallas_call x1, Pallas kernels, project(): pl.pallas_call(functools.partial(project_kernel, dev_count), out_shape=(j...  1.34 us
  transfers between devices with their start and end apart: 3, of which 3 were waited for; matrix products, arithmetic and copies ran while one was open for 0% of the time, Pallas kernels for 0%

profile of v2, /device:TPU:0, one launch (start us, length us, event | category | flops | bytes accessed | tf_op | source)
XLA Modules:
  0.0 60.3 jit_solution(12375009590890097303)
XLA Ops:
  0.0 1.0 %copy-done.4 = bf16[2,2,1,128,4,128]{5,4,3,2,1,0:T(4,128)(2,1)S(1)} copy-done((bf16[2,2,1,128,4,128]{5,4,3,2,1,0:T(4,128)(2,1)S(1)}, bf16[2,2,1,128,4,128]{5,4,3,2,1,0:T(4,128)(2,1)}, u32[]{:S(2)}) %copy-start.4) | copy-done | bytes 524312
  1.0 1.0 %copy-done.5 = bf16[2,2,1,128,4,128]{5,4,3,2,1,0:T(4,128)(2,1)S(1)} copy-done((bf16[2,2,1,128,4,128]{5,4,3,2,1,0:T(4,128)(2,1)S(1)}, bf16[2,2,1,128,4,128]{5,4,3,2,1,0:T(4,128)(2,1)}, u32[]{:S(2)}) %copy-start.5) | copy-done | bytes 524312
  2.1 0.7 %copy-done.6 = bf16[2,2,1,24,128]{4,3,2,1,0:T(8,128)(2,1)S(1)} copy-done((bf16[2,2,1,24,128]{4,3,2,1,0:T(8,128)(2,1)S(1)}, bf16[2,2,1,24,128]{4,3,2,1,0:T(8,128)(2,1)}, u32[]{:S(2)}) %copy-start.6) | copy-done | bytes 24600
  2.8 0.7 %copy-done.8 = bf16[2,2,1,4,128]{4,3,2,1,0:T(4,128)(2,1)S(1)} copy-done((bf16[2,2,1,4,128]{4,3,2,1,0:T(4,128)(2,1)S(1)}, bf16[2,2,1,4,128]{4,3,2,1,0:T(4,128)(2,1)}, u32[]{:S(2)}) %copy-start.8) | copy-done | bytes 4120
  3.5 0.7 %copy-done.9 = bf16[2,2,1,4,128]{4,3,2,1,0:T(4,128)(2,1)S(1)} copy-done((bf16[2,2,1,4,128]{4,3,2,1,0:T(4,128)(2,1)S(1)}, bf16[2,2,1,4,128]{4,3,2,1,0:T(4,128)(2,1)}, u32[]{:S(2)}) %copy-start.9) | copy-done | bytes 4120
  4.2 0.7 %copy-done.10 = s32[2,2,1]{1,2,0:T(1,128)S(1)} copy-done((s32[2,2,1]{1,2,0:T(1,128)S(1)}, s32[2,2,1]{1,2,0:T(1,128)}, u32[]{:S(2)}) %copy-start.10) | copy-done | bytes 40
  4.9 0.0 slice-start.4
  4.9 1.7 %attend.1.refs_0_ = bf16[4,3072]{1,0:T(4,128)(2,1)S(1)} custom-call(s32[2,1,2]{2,1,0:T(1,128)S(1)} %bitcast.34, bf16[4,24,128]{2,1,0:T(8,128)(2,1)S(1)} %bitcast.30, bf16[4,512,128]{2,1,0:T(8,128)(2,1)S(1)} %bitcast.28, bf16[4,512,128]{2,1,0:T(8,128)(2,1)S(1)} %bitcast.29, bf16[4,4,128]{2,1,0:T(4,128)(2,1)S(1)} %bitcast.32, bf16[4,4,128]{2,1,0:T(4,128)(2,1)S(1)} %bitcast.33), custom_call_target="tpu_custom_call" | custom-call | flops 20000000000 | bytes 1048576 | tf_op jit(solution)/shard_map/attend/pallas_call | solution.py:72
  6.6 0.5 collective-permute-start
  7.1 0.8 %collective-permute-done.refs_1_ = bf16[4,3072]{1,0:T(4,128)(2,1)S(1)} collective-permute-done((bf16[4,3072]{1,0:T(4,128)(2,1)S(1)}, bf16[4,3072]{1,0:T(4,128)(2,1)S(1)}, u32[]{:S(2)}, u32[]{:S(2)}) %collective-permute-start) | collective-permute-done | bytes 24608 | tf_op jit(solution)/shard_map/ppermute | solution.py:298
  8.0 0.6 copy-done.3
  8.6 0.0 copy-start.1
  8.6 1.3 %project.1 = (bf16[2,4,1536]{2,1,0:T(4,128)(2,1)S(1)}, bf16[8,8,1536]{2,1,0:T(8,128)(2,1)S(1)}) custom-call(bf16[4,3072]{1,0:T(4,128)(2,1)S(1)} %attend.1.refs_0_, bf16[4,3072]{1,0:T(4,128)(2,1)S(1)} %collective-permute-done.refs_1_, bf16[3072,1536]{1,0:T(8,128)(2,1)S(1)} %copy-done.3, bf16[2,4,1536]{2,1,0:T(4,128)(2,1)S(1)} %bitcast.31), custom_call_target="tpu_custom_call" | custom-call | flops 20000000000 | bytes 9437184 | tf_op jit(solution)/shard_map/project/pallas_call | solution.py:130
  9.9 15.3 %all_to_all.10 = bf16[8,8,1536]{2,1,0:T(8,128)(2,1)S(1)} all-to-all(bf16[8,8,1536]{2,1,0:T(8,128)(2,1)S(1)} %get-tuple-element.10), channel_id=1, replica_groups=mesh['groups'=2,'dev'=2,'side'=8] {'side'}, dimensions={0} | all-to-all | bytes 393216 | tf_op jit(solution)/shard_map/all_to_all | solution.py:308
  25.2 1.4 %collective-permute-done.1.refs_1_ = bf16[64,1536]{1,0:T(8,128)(2,1)S(1)} collective-permute-done((bf16[64,1536]{1,0:T(8,128)(2,1)S(1)}, bf16[64,1536]{1,0:T(8,128)(2,1)S(1)}, u32[]{:S(2)}, u32[]{:S(2)}) %collective-permute-start.1) | collective-permute-done | bytes 196640 | tf_op jit(solution)/shard_map/ppermute | solution.py:311
  26.7 0.0 copy-start
  26.7 0.0 copy-start.2
  26.8 19.0 %experts.1 = (bf16[64,1536]{1,0:T(8,128)(2,1)S(1)}, bf16[64,1536]{1,0:T(8,128)(2,1)S(1)}) custom-call(bf16[64,1536]{1,0:T(8,128)(2,1)S(1)} %bitcast.25, bf16[64,1536]{1,0:T(8,128)(2,1)S(1)} %collective-permute-done.1.refs_1_, f32[1,3072]{1,0:T(1,128)S(1)} %bitcast.27, bf16[2688,3072]{1,0:T(8,128)(2,1)S(1)} %bitcast.20, bf16[2688,3072]{1,0:T(8,128)(2,1)S(1)} %bitcast.23, ...), custom_call_target="tpu_custom_call" | custom-call | tf_op jit(solution)/shard_map/experts/pallas_call | solution.py:213
  45.7 0.2 collective-permute-start.2
  45.9 1.3 %collective-permute-done.2 = bf16[64,1536]{1,0:T(8,128)(2,1)S(1)} collective-permute-done((bf16[64,1536]{1,0:T(8,128)(2,1)S(1)}, bf16[64,1536]{1,0:T(8,128)(2,1)S(1)}, u32[]{:S(2)}, u32[]{:S(2)}) %collective-permute-start.2) | collective-permute-done | bytes 196640 | tf_op jit(solution)/shard_map/ppermute | solution.py:317
  47.2 0.1 add_convert_fusion
  47.3 0.1 reshape.38
  47.3 11.2 %all_to_all.11.returned = bf16[8,2,4,1536]{3,2,1,0:T(4,128)(2,1)S(1)} all-to-all(bf16[8,2,4,1536]{3,2,1,0:T(4,128)(2,1)S(1)} %reshape.38), channel_id=1, replica_groups=mesh['groups'=2,'dev'=2,'side'=8] {'side'}, dimensions={0} | all-to-all | bytes 393216 | tf_op jit(solution)/shard_map/all_to_all | solution.py:323
  58.6 1.7 %combine.1 = bf16[2,4,1536]{2,1,0:T(4,128)(2,1)} custom-call(s32[2,4,4,8]{3,2,1,0:T(4,128)S(1)} %bitcast.26, f32[2,4,1,4]{3,2,1,0:T(1,128)S(1)} %copy-done.2, bf16[2,4,1536]{2,1,0:T(4,128)(2,1)S(1)} %get-tuple-element.9.updated, bf16[8,2,4,1536]{3,2,1,0:T(4,128)(2,1)S(1)} %all_to_all.11.returned), custom_call_target="tpu_custom_call" | custom-call | tf_op jit(solution)/shard_map/combine/pallas_call | solution.py:264
  (30 shorter events, 0.1 us)
Async XLA Ops:
  0.0 1.0 %copy-start.4 = (bf16[2,2,1,128,4,128]{5,4,3,2,1,0:T(4,128)(2,1)S(1)}, bf16[2,2,1,128,4,128]{5,4,3,2,1,0:T(4,128)(2,1)}, u32[]{:S(2)}) copy-start(bf16[2,2,1,128,4,128]{5,4,3,2,1,0:T(4,128)(2,1)} %param.15) | copy-start | bytes 1572868
  1.0 1.0 %copy-start.5 = (bf16[2,2,1,128,4,128]{5,4,3,2,1,0:T(4,128)(2,1)S(1)}, bf16[2,2,1,128,4,128]{5,4,3,2,1,0:T(4,128)(2,1)}, u32[]{:S(2)}) copy-start(bf16[2,2,1,128,4,128]{5,4,3,2,1,0:T(4,128)(2,1)} %param.16) | copy-start | bytes 1572868
  2.1 0.7 %copy-start.6 = (bf16[2,2,1,24,128]{4,3,2,1,0:T(8,128)(2,1)S(1)}, bf16[2,2,1,24,128]{4,3,2,1,0:T(8,128)(2,1)}, u32[]{:S(2)}) copy-start(bf16[2,2,1,24,128]{4,3,2,1,0:T(8,128)(2,1)} %param.14) | copy-start | bytes 73732
  2.8 0.7 %copy-start.8 = (bf16[2,2,1,4,128]{4,3,2,1,0:T(4,128)(2,1)S(1)}, bf16[2,2,1,4,128]{4,3,2,1,0:T(4,128)(2,1)}, u32[]{:S(2)}) copy-start(bf16[2,2,1,4,128]{4,3,2,1,0:T(4,128)(2,1)} %param.17) | copy-start | bytes 12292
  3.5 0.7 %copy-start.9 = (bf16[2,2,1,4,128]{4,3,2,1,0:T(4,128)(2,1)S(1)}, bf16[2,2,1,4,128]{4,3,2,1,0:T(4,128)(2,1)}, u32[]{:S(2)}) copy-start(bf16[2,2,1,4,128]{4,3,2,1,0:T(4,128)(2,1)} %param.18) | copy-start | bytes 12292
  4.2 0.7 %copy-start.10 = (s32[2,2,1]{1,2,0:T(1,128)S(1)}, s32[2,2,1]{1,2,0:T(1,128)}, u32[]{:S(2)}) copy-start(s32[2,2,1]{1,2,0:T(1,128)} %param.19) | copy-start | bytes 52
  4.9 3.7 %copy-start.3 = (bf16[3072,1536]{1,0:T(8,128)(2,1)S(1)}, bf16[3072,1536]{1,0:T(8,128)(2,1)}, u32[]{:S(2)}) copy-start(bf16[3072,1536]{1,0:T(8,128)(2,1)} %refs_2_.1) | copy-start | bytes 28311556
  4.9 3.7 %copy-start.7 = (bf16[2,4,1,1536]{3,1,2,0:T(4,128)(2,1)S(1)}, bf16[2,4,1,1536]{3,1,2,0:T(4,128)(2,1)}, u32[]{:S(2)}) copy-start(bf16[2,4,1,1536]{3,1,2,0:T(4,128)(2,1)} %param.21) | copy-start | bytes 73732
  4.9 21.8 %slice-start = ((s8[16515072]{0:T(1024)(128)(4,1)}), s8[4194304]{0:T(1024)(128)(4,1)S(1)}, s32[]{:S(2)}) async-start(s8[16515072]{0:T(1024)(128)(4,1)} %bitcast.18), calls=%async_computation.2 | async-start | bytes 8388608
  4.9 21.8 %slice-start.1 = ((s8[16515072]{0:T(1024)(128)(4,1)}), s8[4194304]{0:T(1024)(128)(4,1)S(1)}, s32[]{:S(2)}) async-start(s8[16515072]{0:T(1024)(128)(4,1)} %bitcast.18), calls=%async_computation.3 | async-start | bytes 8388608
  4.9 21.8 %slice-start.4 = ((s8[16515072]{0:T(1024)(128)(4,1)}), s8[4194304]{0:T(1024)(128)(4,1)S(1)}, s32[]{:S(2)}) async-start(s8[16515072]{0:T(1024)(128)(4,1)} %bitcast.21), calls=%async_computation.6 | async-start | bytes 8388608
  4.9 21.8 %slice-start.5 = ((s8[16515072]{0:T(1024)(128)(4,1)}), s8[4194304]{0:T(1024)(128)(4,1)S(1)}, s32[]{:S(2)}) async-start(s8[16515072]{0:T(1024)(128)(4,1)} %bitcast.21), calls=%async_computation.7 | async-start | bytes 8388608
  6.6 1.4 %collective-permute-start = (bf16[4,3072]{1,0:T(4,128)(2,1)S(1)}, bf16[4,3072]{1,0:T(4,128)(2,1)S(1)}, u32[]{:S(2)}, u32[]{:S(2)}) collective-permute-start(bf16[4,3072]{1,0:T(4,128)(2,1)S(1)} %attend.1.refs_0_), channel_id=1, source_target_pairs={{0,8},{8,0},{1,9},{9,1},{2,10},{10,2},{3,11},{11,3},{4,12},{12,4},... | collective-permute-start | bytes 73736 | tf_op jit(solution)/shard_map/ppermute | solution.py:298
  8.6 18.1 %slice-start.2 = ((s8[16515072]{0:T(1024)(128)(4,1)}), s8[4194304]{0:T(1024)(128)(4,1)S(1)}, s32[]{:S(2)}) async-start(s8[16515072]{0:T(1024)(128)(4,1)} %bitcast.18), calls=%async_computation.4 | async-start | bytes 8388608
  8.6 18.1 %slice-start.3 = ((s8[16515072]{0:T(1024)(128)(4,1)}), s8[3932160]{0:T(1024)(128)(4,1)S(1)}, s32[]{:S(2)}) async-start(s8[16515072]{0:T(1024)(128)(4,1)} %bitcast.18), calls=%async_computation.5 | async-start | bytes 7864320
  8.6 18.1 %slice-start.6 = ((s8[16515072]{0:T(1024)(128)(4,1)}), s8[4194304]{0:T(1024)(128)(4,1)S(1)}, s32[]{:S(2)}) async-start(s8[16515072]{0:T(1024)(128)(4,1)} %bitcast.21), calls=%async_computation.8 | async-start | bytes 8388608
  8.6 18.1 %slice-start.7 = ((s8[16515072]{0:T(1024)(128)(4,1)}), s8[3932160]{0:T(1024)(128)(4,1)S(1)}, s32[]{:S(2)}) async-start(s8[16515072]{0:T(1024)(128)(4,1)} %bitcast.21), calls=%async_computation.9 | async-start | bytes 7864320
  8.6 18.1 %copy-start.1 = (f32[3072]{0:T(1024)S(1)}, f32[3072]{0:T(1024)}, u32[]{:S(2)}) copy-start(f32[3072]{0:T(1024)} %param.22) | copy-start | bytes 36868
  25.2 1.4 %collective-permute-start.1 = (bf16[64,1536]{1,0:T(8,128)(2,1)S(1)}, bf16[64,1536]{1,0:T(8,128)(2,1)S(1)}, u32[]{:S(2)}, u32[]{:S(2)}) collective-permute-start(bf16[64,1536]{1,0:T(8,128)(2,1)S(1)} %bitcast.24), channel_id=1, source_target_pairs={{0,8},{8,0},{1,9},{9,1},{2,10},{10,2},{3,11},{11,3},{4,12},{12,4},... | collective-permute-start | bytes 589832 | tf_op jit(solution)/shard_map/ppermute | solution.py:311
  26.7 31.8 %copy-start = (s32[2,4,8,4]{2,3,1,0:T(4,128)S(1)}, s32[2,4,8,4]{2,3,1,0:T(4,128)}, u32[]{:S(2)}) copy-start(s32[2,4,8,4]{2,3,1,0:T(4,128)} %param.23) | copy-start | bytes 3076
  26.7 31.8 %copy-start.2 = (f32[2,4,1,4]{3,2,1,0:T(1,128)S(1)}, f32[2,4,1,4]{3,2,1,0:T(1,128)}, u32[]{:S(2)}) copy-start(f32[2,4,1,4]{3,2,1,0:T(1,128)} %probs.1) | copy-start | bytes 388
  45.7 1.5 %collective-permute-start.2 = (bf16[64,1536]{1,0:T(8,128)(2,1)S(1)}, bf16[64,1536]{1,0:T(8,128)(2,1)S(1)}, u32[]{:S(2)}, u32[]{:S(2)}) collective-permute-start(bf16[64,1536]{1,0:T(8,128)(2,1)S(1)} %get-tuple-element.12), channel_id=1, source_target_pairs={{0,8},{8,0},{1,9},{9,1},{2,10},{10,2},{3,11},{11,3},{4,12},{12,4},... | collective-permute-start | bytes 589832 | tf_op jit(solution)/shard_map/ppermute | solution.py:317

commit v3 on v2

--- a/solution.py
+++ b/solution.py
@@ -16,9 +16,38 @@
 
 smem_spec = pl.BlockSpec(memory_space=pltpu.SMEM)
 vmem_spec = pl.BlockSpec(memory_space=pltpu.VMEM)
-
-
-def attend_kernel(lengths, queries, keys, values, new_keys, new_values, out, scratch):
+in_hbm = functools.partial(pltpu.with_memory_space_constraint, memory_space=pltpu.HBM)
+in_vmem = functools.partial(pltpu.with_memory_space_constraint, memory_space=pltpu.VMEM)
+
+
+def share_rows(routes, probs, shares):
+    batch_count, row_count, _ = shares.shape
+    top_count = routes.shape[2]
+    side_index = lax.axis_index("side")
+    row_ids = lax.broadcasted_iota(jnp.int32, shares.shape[1:], 0)
+    lane_ids = lax.broadcasted_iota(jnp.int32, shares.shape[1:], 1)
+    for batch in range(batch_count):
+
+        def place(row, placed):
+            for top in range(top_count):
+                expert = routes[batch, row, top, side_index]
+                placed = jnp.where(
+                    (row_ids == row) & (lane_ids == expert), probs[batch, row, 0, top], placed
+                )
+            return placed
+
+        placed = jnp.zeros(shares.shape[1:], jnp.float32)
+        if row_count <= 8:
+            for row in range(row_count):
+                placed = place(row, placed)
+        else:
+            placed = lax.fori_loop(0, row_count, place, placed)
+        shares[batch] = placed / jnp.sum(placed, axis=-1, keepdims=True)
+
+
+def attend_kernel(
+    lengths, routes, probs, queries, keys, values, new_keys, new_values, out, shares, scratch
+):
     row_count, head_count, head_width = queries.shape
     pair_count = keys.shape[1]
     key_heads = new_keys.shape[1]
@@ -61,9 +90,10 @@
         scratch[pl.ds(index, row_count, stride=head_count), :] for index in range(head_count)
     ]
     out[...] = jnp.concatenate(pieces, axis=1).astype(jnp.bfloat16)
-
-
-def attend(queries, cache_keys, cache_values, new_keys, new_values, lengths):
+    share_rows(routes, probs, shares)
+
+
+def attend(queries, cache_keys, cache_values, new_keys, new_values, lengths, routes, probs):
     batch_count, local_rows = queries.shape[:2]
     rows = batch_count * local_rows
     head_count, head_width = queries.shape[-2:]
@@ -71,9 +101,12 @@
     pairs = cache_keys.shape[-3] * key_heads
     return pl.pallas_call(
         attend_kernel,
-        out_shape=jax.ShapeDtypeStruct((rows, head_count * head_width), jnp.bfloat16),
-        in_specs=[smem_spec] + [vmem_spec] * 5,
-        out_specs=vmem_spec,
+        out_shape=(
+            jax.ShapeDtypeStruct((rows, head_count * head_width), jnp.bfloat16),
+            jax.ShapeDtypeStruct((batch_count, routes.shape[1], 128), jnp.float32),
+        ),
+        in_specs=[smem_spec] * 3 + [vmem_spec] * 5,
+        out_specs=(vmem_spec, vmem_spec),
         scratch_shapes=[pltpu.VMEM((rows * head_count, head_width), jnp.float32)],
         compiler_params=pltpu.CompilerParams(vmem_limit_bytes=8 * mebibyte),
         name="attend",
@@ -81,12 +114,14 @@
             flops=hint_flops, transcendentals=0, bytes_accessed=cache_keys.size * 4
         ),
     )(
-        jnp.swapaxes(lengths, 1, 2),
-        queries.reshape(rows, head_count, head_width),
-        cache_keys.reshape(rows, pairs, head_width),
-        cache_values.reshape(rows, pairs, head_width),
-        new_keys.reshape(rows, key_heads, head_width),
-        new_values.reshape(rows, key_heads, head_width),
+        in_hbm(jnp.swapaxes(lengths, 1, 2)),
+        in_hbm(jnp.swapaxes(routes, 2, 3)),
+        in_hbm(probs),
+        in_hbm(queries.reshape(rows, head_count, head_width)),
+        in_hbm(cache_keys.reshape(rows, pairs, head_width)),
+        in_hbm(cache_values.reshape(rows, pairs, head_width)),
+        in_hbm(new_keys.reshape(rows, key_heads, head_width)),
+        in_hbm(new_values.reshape(rows, key_heads, head_width)),
     )
 
 
@@ -140,7 +175,7 @@
             flops=hint_flops, transcendentals=0, bytes_accessed=out_weight.size * 2
         ),
         name="project",
-    )(*attended, pltpu.with_memory_space_constraint(out_weight, pltpu.VMEM), residual)
+    )(*attended, in_vmem(out_weight), residual)
 
 
 def pieces_of(length, piece):
@@ -173,11 +208,15 @@
     values = values - center
     spread = jnp.mean(jnp.square(values), axis=-1, keepdims=True)
     rows = (values * lax.rsqrt(spread + norm_epsilon) * gain[...]).astype(jnp.bfloat16)
-    for start, size in pieces_of(units, 512):
-        span = slice(start, start + size)
-        gate = lax.dot_general(rows, w_gate[span, :], last_last, preferred_element_type=jnp.float32)
-        up = lax.dot_general(rows, w_up[span, :], last_last, preferred_element_type=jnp.float32)
-        hidden[:, span] = (gate / (1.0 + jnp.exp(-gate)) * up).astype(jnp.bfloat16)
+    @pl.when(dev_index < dev_count)
+    def _():
+        for start, size in pieces_of(units, 896):
+            span = slice(start, start + size)
+            gate = lax.dot_general(
+                w_gate[span, :], rows, last_last, preferred_element_type=jnp.float32
+            )
+            up = lax.dot_general(w_up[span, :], rows, last_last, preferred_element_type=jnp.float32)
+            hidden[:, span] = (gate / (1.0 + jnp.exp(-gate)) * up).T.astype(jnp.bfloat16)
 
     @pl.when(pl.program_id(0) == 0)
     def _():
@@ -209,7 +248,6 @@
     block = min(rows, 128)
     out_width = width // 2 if dev_count == 2 else width
     out_count = 2 if dev_count == 2 else 1
-    resident = functools.partial(pltpu.with_memory_space_constraint, memory_space=pltpu.VMEM)
     return pl.pallas_call(
         functools.partial(expert_kernel, dev_count, len(parts)),
         grid=(rows // block,),
@@ -225,50 +263,28 @@
         ],
         compiler_params=pltpu.CompilerParams(vmem_limit_bytes=19 * mebibyte),
         name="experts",
-    )(*parts, gain.reshape(1, width), resident(w_gate), resident(w_up), w_down)
-
-
-def combine_kernel(routes, probs, updated, returned, out):
-    side_count = returned.shape[0]
-    batch_count, row_count, width = updated.shape
-    top_count = routes.shape[2]
-    side_index = lax.axis_index("side")
-    row_ids = lax.broadcasted_iota(jnp.int32, (row_count, 128), 0)
-    lane_ids = lax.broadcasted_iota(jnp.int32, (row_count, 128), 1)
+    )(*parts, gain.reshape(1, width), in_vmem(w_gate), in_vmem(w_up), w_down)
+
+
+def combine_kernel(shares, updated, returned, out):
+    batch_count = updated.shape[0]
     for batch in range(batch_count):
-
-        def place(row, shares):
-            for top in range(top_count):
-                expert = routes[batch, row, top, side_index]
-                shares = jnp.where(
-                    (row_ids == row) & (lane_ids == expert), probs[batch, row, 0, top], shares
-                )
-            return shares
-
-        shares = jnp.zeros((row_count, 128), jnp.float32)
-        if row_count <= 8:
-            for row in range(row_count):
-                shares = place(row, shares)
-        else:
-            shares = lax.fori_loop(0, row_count, place, shares)
-        shares = shares / jnp.sum(shares, axis=-1, keepdims=True)
-        mixture = jnp.zeros((row_count, width), jnp.float32)
-        for expert in range(side_count):
-            mixture = mixture + shares[:, expert : expert + 1] * returned[
-                expert, batch
-            ].astype(jnp.float32)
-        out[batch] = (updated[batch].astype(jnp.float32) + mixture).astype(jnp.bfloat16)
-
-
-def combine(routes, probs, updated, returned):
+        total = updated[batch].astype(jnp.float32)
+        for expert in range(returned.shape[0]):
+            share = shares[batch, :, expert : expert + 1]
+            total = total + share * returned[expert, batch].astype(jnp.float32)
+        out[batch] = total.astype(jnp.bfloat16)
+
+
+def combine(shares, updated, returned):
     return pl.pallas_call(
         combine_kernel,
         out_shape=jax.ShapeDtypeStruct(updated.shape, jnp.bfloat16),
-        in_specs=[smem_spec, smem_spec, vmem_spec, vmem_spec],
+        in_specs=[vmem_spec] * 3,
         out_specs=vmem_spec,
         compiler_params=pltpu.CompilerParams(vmem_limit_bytes=8 * mebibyte),
         name="combine",
-    )(jnp.swapaxes(routes, 2, 3), probs, updated, returned)
+    )(shares, updated, returned)
 
 
 def body(
@@ -293,7 +309,9 @@
     rows = batch_count * row_count
     swap = [(0, 1), (1, 0)]
 
-    attended = attend(queries, cache_keys, cache_values, new_keys, new_values, lengths)
+    attended, shares = attend(
+        queries, cache_keys, cache_values, new_keys, new_values, lengths, routes, route_probs
+    )
     if dev_count == 2:
         attended = (attended, lax.ppermute(attended, "dev", swap))
     else:
@@ -321,7 +339,7 @@
         total = jnp.sum(pieces.astype(jnp.float32), axis=1)
     total = total.astype(jnp.bfloat16).reshape(side_count, batch_count, row_count, column_width)
     returned = lax.all_to_all(total, "side", split_axis=0, concat_axis=0, tiled=True)
-    result = combine(routes, route_probs, updated, returned)
+    result = combine(shares, updated, returned)
     return result.reshape(residual.shape)
 
 

time: 60.7 us -> 48.2 us (0.79)
  Pallas kernels: 23.7 us -> 16.7 us
  local copies, waits for them, and re-layouts: 5.57 us -> 0.18 us
    pallas_call x1, Pallas kernels: 19 us -> 12.1 us  [experts(): pl.pallas_call(functools.partial(expert_kernel, dev_count, len(parts)), g...]
    unnamed x38 -> x22, local copies, waits for them, and re-layouts: 5.51 us -> 0.12 us
    pallas_call x1, Pallas kernels: 1.74 us -> 0.75 us  [combine(): pl.pallas_call(combine_kernel, out_shape=jax.ShapeDtypeStruct(updated.sha...]
    pallas_call x1, Pallas kernels: 1.69 us -> 2.52 us  [attend(): pl.pallas_call(attend_kernel, out_shape=(jax.ShapeDtypeStruct((rows, head...]
where the time goes in v3:
time: 48.2 us; the launch traced here: 48 us
  blocking collectives  26.6 us (55%)
  Pallas kernels  16.7 us (35%)
  waiting for transfers between devices  3.59 us (7%)
  starting transfers between devices  0.74 us (2%)
    all_to_all x1, blocking collectives, body(): lax.all_to_all(copies, 'side', split_axis=0, concat_axis=0, tiled=True)  15.4 us
    pallas_call x1, Pallas kernels, experts(): pl.pallas_call(functools.partial(expert_kernel, dev_count, len(parts)), g...  12.1 us
    all_to_all x1, blocking collectives, body(): lax.all_to_all(total, 'side', split_axis=0, concat_axis=0, tiled=True)  11.2 us
    pallas_call x1, Pallas kernels, attend(): pl.pallas_call(attend_kernel, out_shape=(jax.ShapeDtypeStruct((rows, head...  2.52 us
    ppermute x1, waiting for transfers between devices, body(): parts = (arrived, lax.ppermute(arrived, 'dev', swap))  1.44 us
    pallas_call x1, Pallas kernels, project(): pl.pallas_call(functools.partial(project_kernel, dev_count), out_shape=(j...  1.34 us
    ppermute x1, waiting for transfers between devices, body(): lax.ppermute(given, 'dev', swap).astype(jnp.float32)  1.31 us
  transfers between devices with their start and end apart: 3, of which 3 were waited for; matrix products, arithmetic and copies ran while one was open for 0% of the time, Pallas kernels for 0%

profile of v3, /device:TPU:0, one launch (start us, length us, event | category | flops | bytes accessed | tf_op | source)
XLA Modules:
  0.0 48.0 jit_solution(17272788907709721910)
XLA Ops:
  0.0 0.0 slice-start.5
  0.0 2.5 %attend.1 = (bf16[4,3072]{1,0:T(4,128)(2,1)S(1)}, f32[2,4,128]{2,1,0:T(4,128)S(1)}) custom-call(s32[2,1,2]{2,1,0:T(1,128)} %bitcast.35, s32[2,4,4,8]{3,2,1,0:T(4,128)} %bitcast.32, f32[2,4,1,4]{3,2,1,0:T(1,128)} %probs.1, bf16[4,24,128]{2,1,0:T(8,128)(2,1)} %bitcast.31, bf16[4,512,128]{2,1,0:T(8,128)(2,1)} %bitcast.29, bf16[4,512,128]{2,1,0:T(8,128)(2,1)} %bitcast.30, ...), custom_call_target="tpu_custom_call" | custom-call | flops 20000000000 | bytes 1048576 | tf_op jit(solution)/shard_map/attend/pallas_call | solution.py:102
  2.6 0.5 %collective-permute-start = (bf16[4,3072]{1,0:T(4,128)(2,1)S(1)}, bf16[4,3072]{1,0:T(4,128)(2,1)S(1)}, u32[]{:S(2)}, u32[]{:S(2)}) collective-permute-start(bf16[4,3072]{1,0:T(4,128)(2,1)S(1)} %get-tuple-element.12.refs_0_), channel_id=1, source_target_pairs={{0,8},{8,0},{1,9},{9,1},{2,10},{10,2},{3,11},{11,3},{4,12},{12,4},... | collective-permute-start | bytes 73736 | tf_op jit(solution)/shard_map/ppermute | solution.py:316
  3.1 0.8 %collective-permute-done.refs_1_ = bf16[4,3072]{1,0:T(4,128)(2,1)S(1)} collective-permute-done((bf16[4,3072]{1,0:T(4,128)(2,1)S(1)}, bf16[4,3072]{1,0:T(4,128)(2,1)S(1)}, u32[]{:S(2)}, u32[]{:S(2)}) %collective-permute-start) | collective-permute-done | bytes 24608 | tf_op jit(solution)/shard_map/ppermute | solution.py:316
  3.9 0.1 copy-done.1
  4.0 0.0 copy-done.2
  4.0 0.0 slice-start.7
  4.0 0.0 copy-start
  4.1 1.3 %project.1 = (bf16[2,4,1536]{2,1,0:T(4,128)(2,1)S(1)}, bf16[8,8,1536]{2,1,0:T(8,128)(2,1)S(1)}) custom-call(bf16[4,3072]{1,0:T(4,128)(2,1)S(1)} %get-tuple-element.12.refs_0_, bf16[4,3072]{1,0:T(4,128)(2,1)S(1)} %collective-permute-done.refs_1_, bf16[3072,1536]{1,0:T(8,128)(2,1)S(1)} %copy-done.1, bf16[2,4,1536]{2,1,0:T(4,128)(2,1)S(1)} %bitcast.27), custom_call_target="tpu_custom_call" | custom-call | flops 20000000000 | bytes 9437184 | tf_op jit(solution)/shard_map/project/pallas_call | solution.py:165
  5.4 15.4 %all_to_all.10 = bf16[8,8,1536]{2,1,0:T(8,128)(2,1)S(1)} all-to-all(bf16[8,8,1536]{2,1,0:T(8,128)(2,1)S(1)} %get-tuple-element.14), channel_id=1, replica_groups=mesh['groups'=2,'dev'=2,'side'=8] {'side'}, dimensions={0} | all-to-all | bytes 393216 | tf_op jit(solution)/shard_map/all_to_all | solution.py:326
  20.8 0.0 collective-permute-start.1
  20.8 1.4 %collective-permute-done.1.refs_1_ = bf16[64,1536]{1,0:T(8,128)(2,1)S(1)} collective-permute-done((bf16[64,1536]{1,0:T(8,128)(2,1)S(1)}, bf16[64,1536]{1,0:T(8,128)(2,1)S(1)}, u32[]{:S(2)}, u32[]{:S(2)}) %collective-permute-start.1) | collective-permute-done | bytes 196640 | tf_op jit(solution)/shard_map/ppermute | solution.py:329
  22.3 0.0 slice-done
  22.3 0.0 slice-done.1
  22.3 0.0 slice-done.4
  22.3 0.0 slice-done.5
  22.3 0.0 slice-done.2
  22.4 12.1 %experts.1 = (bf16[64,1536]{1,0:T(8,128)(2,1)S(1)}, bf16[64,1536]{1,0:T(8,128)(2,1)S(1)}) custom-call(bf16[64,1536]{1,0:T(8,128)(2,1)S(1)} %bitcast.25, bf16[64,1536]{1,0:T(8,128)(2,1)S(1)} %collective-permute-done.1.refs_1_, f32[1,3072]{1,0:T(1,128)S(1)} %bitcast.26, bf16[2688,3072]{1,0:T(8,128)(2,1)S(1)} %bitcast.20, bf16[2688,3072]{1,0:T(8,128)(2,1)S(1)} %bitcast.23, ...), custom_call_target="tpu_custom_call" | custom-call | tf_op jit(solution)/shard_map/experts/pallas_call | solution.py:251
  34.5 0.2 collective-permute-start.2
  34.7 1.3 %collective-permute-done.2 = bf16[64,1536]{1,0:T(8,128)(2,1)S(1)} collective-permute-done((bf16[64,1536]{1,0:T(8,128)(2,1)S(1)}, bf16[64,1536]{1,0:T(8,128)(2,1)S(1)}, u32[]{:S(2)}, u32[]{:S(2)}) %collective-permute-start.2) | collective-permute-done | bytes 196640 | tf_op jit(solution)/shard_map/ppermute | solution.py:335
  36.0 0.1 add_convert_fusion
  36.0 0.1 reshape.38
  36.1 11.2 %all_to_all.11.returned = bf16[8,2,4,1536]{3,2,1,0:T(4,128)(2,1)S(1)} all-to-all(bf16[8,2,4,1536]{3,2,1,0:T(4,128)(2,1)S(1)} %reshape.38), channel_id=1, replica_groups=mesh['groups'=2,'dev'=2,'side'=8] {'side'}, dimensions={0} | all-to-all | bytes 393216 | tf_op jit(solution)/shard_map/all_to_all | solution.py:341
  47.3 0.8 %combine.1 = bf16[2,4,1536]{2,1,0:T(4,128)(2,1)} custom-call(f32[2,4,128]{2,1,0:T(4,128)S(1)} %get-tuple-element.11.shares, bf16[2,4,1536]{2,1,0:T(4,128)(2,1)S(1)} %get-tuple-element.13.updated, bf16[8,2,4,1536]{3,2,1,0:T(4,128)(2,1)S(1)} %all_to_all.11.returned), custom_call_target="tpu_custom_call" | custom-call | tf_op jit(solution)/shard_map/combine/pallas_call | solution.py:280
  (14 shorter events, 0.0 us)
Async XLA Ops:
  0.0 4.0 %copy-start.1 = (bf16[3072,1536]{1,0:T(8,128)(2,1)S(1)}, bf16[3072,1536]{1,0:T(8,128)(2,1)}, u32[]{:S(2)}) copy-start(bf16[3072,1536]{1,0:T(8,128)(2,1)} %refs_2_.1) | copy-start | bytes 28311556
  0.0 4.0 %copy-start.2 = (bf16[2,4,1,1536]{3,1,2,0:T(4,128)(2,1)S(1)}, bf16[2,4,1,1536]{3,1,2,0:T(4,128)(2,1)}, u32[]{:S(2)}) copy-start(bf16[2,4,1,1536]{3,1,2,0:T(4,128)(2,1)} %param.21) | copy-start | bytes 73732
  0.0 22.3 %slice-start = ((s8[16515072]{0:T(1024)(128)(4,1)}), s8[4194304]{0:T(1024)(128)(4,1)S(1)}, s32[]{:S(2)}) async-start(s8[16515072]{0:T(1024)(128)(4,1)} %bitcast.18), calls=%async_computation.2 | async-start | bytes 8388608
  0.0 22.3 %slice-start.1 = ((s8[16515072]{0:T(1024)(128)(4,1)}), s8[4194304]{0:T(1024)(128)(4,1)S(1)}, s32[]{:S(2)}) async-start(s8[16515072]{0:T(1024)(128)(4,1)} %bitcast.18), calls=%async_computation.3 | async-start | bytes 8388608
  0.0 22.3 %slice-start.4 = ((s8[16515072]{0:T(1024)(128)(4,1)}), s8[4194304]{0:T(1024)(128)(4,1)S(1)}, s32[]{:S(2)}) async-start(s8[16515072]{0:T(1024)(128)(4,1)} %bitcast.21), calls=%async_computation.6 | async-start | bytes 8388608
  0.0 22.3 %slice-start.5 = ((s8[16515072]{0:T(1024)(128)(4,1)}), s8[4194304]{0:T(1024)(128)(4,1)S(1)}, s32[]{:S(2)}) async-start(s8[16515072]{0:T(1024)(128)(4,1)} %bitcast.21), calls=%async_computation.7 | async-start | bytes 8388608
  2.6 1.4 %collective-permute-start = (bf16[4,3072]{1,0:T(4,128)(2,1)S(1)}, bf16[4,3072]{1,0:T(4,128)(2,1)S(1)}, u32[]{:S(2)}, u32[]{:S(2)}) collective-permute-start(bf16[4,3072]{1,0:T(4,128)(2,1)S(1)} %get-tuple-element.12.refs_0_), channel_id=1, source_target_pairs={{0,8},{8,0},{1,9},{9,1},{2,10},{10,2},{3,11},{11,3},{4,12},{12,4},... | collective-permute-start | bytes 73736 | tf_op jit(solution)/shard_map/ppermute | solution.py:316
  4.0 18.3 %slice-start.2 = ((s8[16515072]{0:T(1024)(128)(4,1)}), s8[4194304]{0:T(1024)(128)(4,1)S(1)}, s32[]{:S(2)}) async-start(s8[16515072]{0:T(1024)(128)(4,1)} %bitcast.18), calls=%async_computation.4 | async-start | bytes 8388608
  4.0 18.3 %slice-start.3 = ((s8[16515072]{0:T(1024)(128)(4,1)}), s8[3932160]{0:T(1024)(128)(4,1)S(1)}, s32[]{:S(2)}) async-start(s8[16515072]{0:T(1024)(128)(4,1)} %bitcast.18), calls=%async_computation.5 | async-start | bytes 7864320
  4.0 18.3 %slice-start.6 = ((s8[16515072]{0:T(1024)(128)(4,1)}), s8[4194304]{0:T(1024)(128)(4,1)S(1)}, s32[]{:S(2)}) async-start(s8[16515072]{0:T(1024)(128)(4,1)} %bitcast.21), calls=%async_computation.8 | async-start | bytes 8388608
  4.0 18.3 %slice-start.7 = ((s8[16515072]{0:T(1024)(128)(4,1)}), s8[3932160]{0:T(1024)(128)(4,1)S(1)}, s32[]{:S(2)}) async-start(s8[16515072]{0:T(1024)(128)(4,1)} %bitcast.21), calls=%async_computation.9 | async-start | bytes 7864320
  4.0 18.3 %copy-start = (f32[3072]{0:T(1024)S(1)}, f32[3072]{0:T(1024)}, u32[]{:S(2)}) copy-start(f32[3072]{0:T(1024)} %param.22) | copy-start | bytes 36868
  20.8 1.4 %collective-permute-start.1 = (bf16[64,1536]{1,0:T(8,128)(2,1)S(1)}, bf16[64,1536]{1,0:T(8,128)(2,1)S(1)}, u32[]{:S(2)}, u32[]{:S(2)}) collective-permute-start(bf16[64,1536]{1,0:T(8,128)(2,1)S(1)} %bitcast.24), channel_id=1, source_target_pairs={{0,8},{8,0},{1,9},{9,1},{2,10},{10,2},{3,11},{11,3},{4,12},{12,4},... | collective-permute-start | bytes 589832 | tf_op jit(solution)/shard_map/ppermute | solution.py:329
  34.5 1.5 %collective-permute-start.2 = (bf16[64,1536]{1,0:T(8,128)(2,1)S(1)}, bf16[64,1536]{1,0:T(8,128)(2,1)S(1)}, u32[]{:S(2)}, u32[]{:S(2)}) collective-permute-start(bf16[64,1536]{1,0:T(8,128)(2,1)S(1)} %get-tuple-element.16), channel_id=1, source_target_pairs={{0,8},{8,0},{1,9},{9,1},{2,10},{10,2},{3,11},{11,3},{4,12},{12,4},... | collective-permute-start | bytes 589832 | tf_op jit(solution)/shard_map/ppermute | solution.py:335

commit v4 on v3

--- a/solution.py
+++ b/solution.py
@@ -11,7 +11,6 @@
 norm_epsilon = 1e-05
 mebibyte = 1024 * 1024
 hint_flops = 20_000_000_000
-down_piece = 896
 last_last = (((1,), (1,)), ((), ()))
 
 smem_spec = pl.BlockSpec(memory_space=pltpu.SMEM)
@@ -108,7 +107,7 @@
         in_specs=[smem_spec] * 3 + [vmem_spec] * 5,
         out_specs=(vmem_spec, vmem_spec),
         scratch_shapes=[pltpu.VMEM((rows * head_count, head_width), jnp.float32)],
-        compiler_params=pltpu.CompilerParams(vmem_limit_bytes=8 * mebibyte),
+        compiler_params=pltpu.CompilerParams(vmem_limit_bytes=3 * mebibyte),
         name="attend",
         cost_estimate=pl.CostEstimate(
             flops=hint_flops, transcendentals=0, bytes_accessed=cache_keys.size * 4
@@ -170,7 +169,7 @@
         ),
         in_specs=[vmem_spec] * (len(attended) + 2),
         out_specs=(vmem_spec, vmem_spec),
-        compiler_params=pltpu.CompilerParams(vmem_limit_bytes=4 * mebibyte),
+        compiler_params=pltpu.CompilerParams(vmem_limit_bytes=2 * mebibyte),
         cost_estimate=pl.CostEstimate(
             flops=hint_flops, transcendentals=0, bytes_accessed=out_weight.size * 2
         ),
@@ -182,88 +181,121 @@
     return [(start, min(piece, length - start)) for start in range(0, length, piece)]
 
 
-def expert_kernel(dev_count, part_count, *refs):
-    parts, refs = refs[:part_count], refs[part_count:]
-    gain, w_gate, w_up, w_down = refs[:4]
-    outs, (hidden, down, arrived) = refs[4:-3], refs[-3:]
-    units, width = w_gate.shape
+def normalize(parts, gain):
+    width = sum(part.shape[1] for part in parts)
+    center = sum(jnp.sum(part, axis=-1, keepdims=True) for part in parts) / width
+    parts = [part - center for part in parts]
+    spread = sum(jnp.sum(jnp.square(part), axis=-1, keepdims=True) for part in parts) / width
+    values = jnp.concatenate(parts, axis=1) if len(parts) > 1 else parts[0]
+    return (values * lax.rsqrt(spread + norm_epsilon) * gain).astype(jnp.bfloat16)
+
+
+def hidden_rows(parts, gain, w_gate, w_up, hidden):
+    rows = normalize(parts, gain[...])
+    for start, size in pieces_of(w_gate.shape[0], 896):
+        span = slice(start, start + size)
+        gate = lax.dot_general(w_gate[span, :], rows, last_last, preferred_element_type=jnp.float32)
+        up = lax.dot_general(w_up[span, :], rows, last_last, preferred_element_type=jnp.float32)
+        hidden[:, span] = (gate / (1.0 + jnp.exp(-gate)) * up).T.astype(jnp.bfloat16)
+
+
+def pair_kernel(own, other, gain, w_gate, w_up, w_down, hidden, given, kept, lent, arrived):
     dev_index = lax.axis_index("dev")
+    width = own.shape[1]
     copies = [
         pltpu.make_async_copy(
-            w_down.at[pl.ds(start, size), :], down.at[pl.ds(start, size), :], arrived.at[index]
+            w_down.at[:, pl.ds(pl.multiple_of(dev * width, width), width)],
+            target,
+            arrived.at[index],
         )
-        for index, (start, size) in enumerate(pieces_of(units, down_piece))
+        for index, (dev, target) in enumerate(((1 - dev_index, lent), (dev_index, kept)))
     ]
-
-    @pl.when(pl.program_id(0) == 0)
+    for copy in copies:
+        copy.start()
+
+    @pl.when(dev_index < 2)
     def _():
-        for copy in copies:
-            copy.start()
-
-    wide = [part[...].astype(jnp.float32) for part in parts]
-    if part_count == 2:
-        wide = halves(dev_index, *wide)
-    values = jnp.concatenate(wide, axis=1) if part_count > 1 else wide[0]
-    center = jnp.mean(values, axis=-1, keepdims=True)
-    values = values - center
-    spread = jnp.mean(jnp.square(values), axis=-1, keepdims=True)
-    rows = (values * lax.rsqrt(spread + norm_epsilon) * gain[...]).astype(jnp.bfloat16)
-    @pl.when(dev_index < dev_count)
-    def _():
-        for start, size in pieces_of(units, 896):
-            span = slice(start, start + size)
-            gate = lax.dot_general(
-                w_gate[span, :], rows, last_last, preferred_element_type=jnp.float32
-            )
-            up = lax.dot_general(w_up[span, :], rows, last_last, preferred_element_type=jnp.float32)
-            hidden[:, span] = (gate / (1.0 + jnp.exp(-gate)) * up).T.astype(jnp.bfloat16)
-
-    @pl.when(pl.program_id(0) == 0)
-    def _():
-        for copy in copies:
-            copy.wait()
-
-    half = width // 2
-    for start, size in pieces_of(half, 512):
-        low = jnp.dot(
-            hidden[...], down[:, start : start + size], preferred_element_type=jnp.float32
-        )
-        high = jnp.dot(
-            hidden[...],
-            down[:, half + start : half + start + size],
-            preferred_element_type=jnp.float32,
-        )
-        if len(outs) == 2:
-            span = slice(start, start + size)
-            outs[0][:, span] = jnp.where(dev_index == 0, low, high).astype(jnp.bfloat16)
-            outs[1][:, span] = jnp.where(dev_index == 0, high, low).astype(jnp.bfloat16)
-        else:
-            outs[0][:, start : start + size] = low.astype(jnp.bfloat16)
-            outs[0][:, half + start : half + start + size] = high.astype(jnp.bfloat16)
-
-
-def experts(parts, gain, w_gate, w_up, w_down, dev_count):
-    rows = parts[0].shape[0]
+        parts = halves(dev_index, own[...].astype(jnp.float32), other[...].astype(jnp.float32))
+        hidden_rows(parts, gain, w_gate, w_up, hidden)
+
+    for copy in copies:
+        copy.wait()
+    given[...] = jnp.dot(hidden[...], lent[...], preferred_element_type=jnp.float32).astype(
+        jnp.bfloat16
+    )
+
+
+def down_kernel(hidden, kept, out):
+    out[...] = jnp.dot(hidden[...], kept[...], preferred_element_type=jnp.float32).astype(
+        jnp.bfloat16
+    )
+
+
+def pair_experts(arrived, gain, w_gate, w_up, w_down):
+    swap = [(0, 1), (1, 0)]
+    rows, half = arrived.shape
+    units, width = w_gate.shape
+    hidden, given, kept = pl.pallas_call(
+        pair_kernel,
+        out_shape=(
+            jax.ShapeDtypeStruct((rows, units), jnp.bfloat16),
+            jax.ShapeDtypeStruct((rows, half), jnp.bfloat16),
+            pltpu.VMEM((units, half), jnp.bfloat16),
+        ),
+        in_specs=[vmem_spec] * 5 + [pl.BlockSpec(memory_space=pl.ANY)],
+        out_specs=(vmem_spec,) * 3,
+        scratch_shapes=[
+            pltpu.VMEM((units, half), jnp.bfloat16),
+            pltpu.SemaphoreType.DMA((2,)),
+        ],
+        compiler_params=pltpu.CompilerParams(vmem_limit_bytes=12 * mebibyte),
+        name="experts",
+    )(
+        arrived,
+        lax.ppermute(arrived, "dev", swap),
+        gain.reshape(1, width),
+        in_vmem(w_gate),
+        in_vmem(w_up),
+        in_hbm(w_down),
+    )
+    taken = lax.ppermute(given, "dev", swap)
+    own = pl.pallas_call(
+        down_kernel,
+        out_shape=jax.ShapeDtypeStruct((rows, half), jnp.bfloat16),
+        in_specs=[vmem_spec, vmem_spec],
+        out_specs=vmem_spec,
+        compiler_params=pltpu.CompilerParams(vmem_limit_bytes=2 * mebibyte),
+        name="down_own",
+    )(hidden, in_vmem(kept))
+    return own.astype(jnp.float32) + taken.astype(jnp.float32)
+
+
+def whole_kernel(rows, gain, w_gate, w_up, w_down, out, hidden):
+    hidden_rows([rows[...].astype(jnp.float32)], gain, w_gate, w_up, hidden)
+    out[...] = jnp.dot(hidden[...], w_down[...], preferred_element_type=jnp.float32).astype(
+        jnp.bfloat16
+    )
+
+
+def whole_experts(arrived, gain, w_gate, w_up, w_down):
+    rows, part_width = arrived.shape
     units, width = w_gate.shape
     block = min(rows, 128)
-    out_width = width // 2 if dev_count == 2 else width
-    out_count = 2 if dev_count == 2 else 1
-    return pl.pallas_call(
-        functools.partial(expert_kernel, dev_count, len(parts)),
+    gathered = lax.all_gather(arrived, "dev", axis=1, tiled=True)
+    given = pl.pallas_call(
+        whole_kernel,
         grid=(rows // block,),
-        out_shape=[jax.ShapeDtypeStruct((rows, out_width), jnp.bfloat16)] * out_count,
-        in_specs=[pl.BlockSpec((block, part.shape[1]), lambda r: (r, 0)) for part in parts]
-        + [pl.BlockSpec((1, width), lambda r: (0, 0)), vmem_spec, vmem_spec]
-        + [pl.BlockSpec(memory_space=pl.ANY)],
-        out_specs=[pl.BlockSpec((block, out_width), lambda r: (r, 0))] * out_count,
-        scratch_shapes=[
-            pltpu.VMEM((block, units), jnp.bfloat16),
-            pltpu.VMEM((units, width), jnp.bfloat16),
-            pltpu.SemaphoreType.DMA((len(pieces_of(units, down_piece)),)),
-        ],
-        compiler_params=pltpu.CompilerParams(vmem_limit_bytes=19 * mebibyte),
+        out_shape=jax.ShapeDtypeStruct((rows, width), jnp.bfloat16),
+        in_specs=[pl.BlockSpec((block, width), lambda r: (r, 0))]
+        + [pl.BlockSpec((1, width), lambda r: (0, 0)), vmem_spec, vmem_spec, vmem_spec],
+        out_specs=pl.BlockSpec((block, width), lambda r: (r, 0)),
+        scratch_shapes=[pltpu.VMEM((block, units), jnp.bfloat16)],
+        compiler_params=pltpu.CompilerParams(vmem_limit_bytes=24 * mebibyte),
         name="experts",
-    )(*parts, gain.reshape(1, width), in_vmem(w_gate), in_vmem(w_up), w_down)
+    )(gathered, gain.reshape(1, width), w_gate, w_up, w_down)
+    pieces = given.reshape(rows, width // part_width, part_width)
+    pieces = lax.all_to_all(pieces, "dev", split_axis=1, concat_axis=1, tiled=True)
+    return jnp.sum(pieces.astype(jnp.float32), axis=1)
 
 
 def combine_kernel(shares, updated, returned, out):
@@ -325,18 +357,8 @@
     )
     arrived = lax.all_to_all(copies, "side", split_axis=0, concat_axis=0, tiled=True)
     arrived = arrived.reshape(side_count * rows, column_width)
-    if dev_count == 2:
-        parts = (arrived, lax.ppermute(arrived, "dev", swap))
-    else:
-        parts = (lax.all_gather(arrived, "dev", axis=1, tiled=True),)
-    sums = experts(parts, norm_gain, w_gate[0], w_up[0], w_down[0], dev_count)
-    if dev_count == 2:
-        own, given = sums
-        total = own.astype(jnp.float32) + lax.ppermute(given, "dev", swap).astype(jnp.float32)
-    else:
-        pieces = sums[0].reshape(side_count * rows, dev_count, column_width)
-        pieces = lax.all_to_all(pieces, "dev", split_axis=1, concat_axis=1, tiled=True)
-        total = jnp.sum(pieces.astype(jnp.float32), axis=1)
+    gather_and_run = pair_experts if dev_count == 2 else whole_experts
+    total = gather_and_run(arrived, norm_gain, w_gate[0], w_up[0], w_down[0])
     total = total.astype(jnp.bfloat16).reshape(side_count, batch_count, row_count, column_width)
     returned = lax.all_to_all(total, "side", split_axis=0, concat_axis=0, tiled=True)
     result = combine(shares, updated, returned)

time: 48.2 us -> 47.2 us (0.979)
  waiting for transfers between devices: 3.59 us -> 2.29 us
    ppermute x2, waiting for transfers between devices: 2.74 us -> 1.44 us  [the longest x1 1.44 us: pair_experts(): lax.ppermute(arrived, 'dev', swap)]
    pallas_call x1 -> x2, Pallas kernels: 12.1 us -> 12.1 us  [the longest x1 10.6 us: pair_experts(): pl.pallas_call(pair_kernel, out_shape=(jax.ShapeDtypeStruct((rows, units)...]
  transfers between devices with their start and end apart: 3 -> 3, of which waited for: 3 -> 2; matrix products, arithmetic and copies ran while one was open for 0% -> 0% of each run, Pallas kernels for 0% -> 3%
where the time goes in v4:
time: 47.2 us; the launch traced here: 47 us
  blocking collectives  26.9 us (57%)
  Pallas kernels  16.8 us (36%)
  waiting for transfers between devices  2.29 us (5%)
  starting transfers between devices  0.73 us (2%)
    all_to_all x1, blocking collectives, body(): lax.all_to_all(copies, 'side', split_axis=0, concat_axis=0, tiled=True)  15.4 us
    all_to_all x1, blocking collectives, body(): lax.all_to_all(total, 'side', split_axis=0, concat_axis=0, tiled=True)  11.4 us
    pallas_call x1, Pallas kernels, pair_experts(): pl.pallas_call(pair_kernel, out_shape=(jax.ShapeDtypeStruct((rows, units)...  10.6 us
    pallas_call x1, Pallas kernels, attend(): pl.pallas_call(attend_kernel, out_shape=(jax.ShapeDtypeStruct((rows, head...  2.52 us
    pallas_call x1, Pallas kernels, pair_experts(): pl.pallas_call(down_kernel, out_shape=jax.ShapeDtypeStruct((rows, half),...  1.54 us
    ppermute x1, waiting for transfers between devices, pair_experts(): lax.ppermute(arrived, 'dev', swap)  1.44 us
    pallas_call x1, Pallas kernels, project(): pl.pallas_call(functools.partial(project_kernel, dev_count), out_shape=(j...  1.34 us
  transfers between devices with their start and end apart: 3, of which 2 were waited for; matrix products, arithmetic and copies ran while one was open for 0% of the time, Pallas kernels for 3%

profile of v4, /device:TPU:0, one launch (start us, length us, event | category | flops | bytes accessed | tf_op | source)
XLA Modules:
  0.0 47.0 jit_solution(8007693545417929855)
XLA Ops:
  0.0 0.0 slice-start.5
  0.0 2.5 %attend.1 = (bf16[4,3072]{1,0:T(4,128)(2,1)S(1)}, f32[2,4,128]{2,1,0:T(4,128)S(1)}) custom-call(s32[2,1,2]{2,1,0:T(1,128)} %bitcast.35, s32[2,4,4,8]{3,2,1,0:T(4,128)} %bitcast.32, f32[2,4,1,4]{3,2,1,0:T(1,128)} %probs.1, bf16[4,24,128]{2,1,0:T(8,128)(2,1)} %bitcast.31, bf16[4,512,128]{2,1,0:T(8,128)(2,1)} %bitcast.29, bf16[4,512,128]{2,1,0:T(8,128)(2,1)} %bitcast.30, ...), custom_call_target="tpu_custom_call" | custom-call | flops 20000000000 | bytes 1048576 | tf_op jit(solution)/shard_map/attend/pallas_call | solution.py:101
  2.6 0.5 %collective-permute-start = (bf16[4,3072]{1,0:T(4,128)(2,1)S(1)}, bf16[4,3072]{1,0:T(4,128)(2,1)S(1)}, u32[]{:S(2)}, u32[]{:S(2)}) collective-permute-start(bf16[4,3072]{1,0:T(4,128)(2,1)S(1)} %get-tuple-element.13.refs_0_), channel_id=1, source_target_pairs={{0,8},{8,0},{1,9},{9,1},{2,10},{10,2},{3,11},{11,3},{4,12},{12,4},... | collective-permute-start | bytes 73736 | tf_op jit(solution)/shard_map/ppermute | solution.py:348
  3.1 0.8 %collective-permute-done.refs_1_ = bf16[4,3072]{1,0:T(4,128)(2,1)S(1)} collective-permute-done((bf16[4,3072]{1,0:T(4,128)(2,1)S(1)}, bf16[4,3072]{1,0:T(4,128)(2,1)S(1)}, u32[]{:S(2)}, u32[]{:S(2)}) %collective-permute-start) | collective-permute-done | bytes 24608 | tf_op jit(solution)/shard_map/ppermute | solution.py:348
  3.9 0.1 copy-done.1
  4.0 0.0 copy-done.2
  4.0 0.0 slice-start.7
  4.0 0.0 copy-start
  4.1 1.3 %project.1 = (bf16[2,4,1536]{2,1,0:T(4,128)(2,1)S(1)}, bf16[8,8,1536]{2,1,0:T(8,128)(2,1)S(1)}) custom-call(bf16[4,3072]{1,0:T(4,128)(2,1)S(1)} %get-tuple-element.13.refs_0_, bf16[4,3072]{1,0:T(4,128)(2,1)S(1)} %collective-permute-done.refs_1_, bf16[3072,1536]{1,0:T(8,128)(2,1)S(1)} %copy-done.1, bf16[2,4,1536]{2,1,0:T(4,128)(2,1)S(1)} %bitcast.27), custom_call_target="tpu_custom_call" | custom-call | flops 20000000000 | bytes 9437184 | tf_op jit(solution)/shard_map/project/pallas_call | solution.py:164
  5.4 15.4 %all_to_all.10 = bf16[8,8,1536]{2,1,0:T(8,128)(2,1)S(1)} all-to-all(bf16[8,8,1536]{2,1,0:T(8,128)(2,1)S(1)} %get-tuple-element.15), channel_id=1, replica_groups=mesh['groups'=2,'dev'=2,'side'=8] {'side'}, dimensions={0} | all-to-all | bytes 393216 | tf_op jit(solution)/shard_map/all_to_all | solution.py:358
  20.8 0.0 collective-permute-start.1
  20.8 1.4 %collective-permute-done.1.other = bf16[64,1536]{1,0:T(8,128)(2,1)S(1)} collective-permute-done((bf16[64,1536]{1,0:T(8,128)(2,1)S(1)}, bf16[64,1536]{1,0:T(8,128)(2,1)S(1)}, u32[]{:S(2)}, u32[]{:S(2)}) %collective-permute-start.1) | collective-permute-done | bytes 196640 | tf_op jit(solution)/shard_map/ppermute | solution.py:255
  22.3 0.0 slice-done
  22.3 0.0 slice-done.1
  22.3 0.0 slice-done.4
  22.3 0.0 slice-done.5
  22.4 10.6 %experts.1 = (bf16[64,2688]{1,0:T(8,128)(2,1)S(1)}, bf16[64,1536]{1,0:T(8,128)(2,1)S(1)}, bf16[2688,1536]{1,0:T(8,128)(2,1)S(1)}) custom-call(bf16[64,1536]{1,0:T(8,128)(2,1)S(1)} %bitcast.25, bf16[64,1536]{1,0:T(8,128)(2,1)S(1)} %collective-permute-done.1.other, f32[1,3072]{1,0:T(1,128)S(1)} %bitcast.26, bf16[2688,3072]{1,0:T(8,128)(2,1)S(1)} %bitcast.20, ...), custom_call_target="tpu_custom_call" | custom-call | tf_op jit(solution)/shard_map/experts/pallas_call | solution.py:238
  33.0 0.2 collective-permute-start.2
  33.2 1.5 %down_own.1 = bf16[64,1536]{1,0:T(8,128)(2,1)S(1)} custom-call(bf16[64,2688]{1,0:T(8,128)(2,1)S(1)} %get-tuple-element.16.hidden, bf16[2688,1536]{1,0:T(8,128)(2,1)S(1)} %get-tuple-element.17.kept), custom_call_target="tpu_custom_call" | custom-call | tf_op jit(solution)/shard_map/down_own/pallas_call | solution.py:262
  34.7 0.0 collective-permute-done.2
  34.7 0.1 add_convert_fusion
  34.8 0.1 reshape.38
  34.8 11.4 %all_to_all.11.returned = bf16[8,2,4,1536]{3,2,1,0:T(4,128)(2,1)S(1)} all-to-all(bf16[8,2,4,1536]{3,2,1,0:T(4,128)(2,1)S(1)} %reshape.38), channel_id=1, replica_groups=mesh['groups'=2,'dev'=2,'side'=8] {'side'}, dimensions={0} | all-to-all | bytes 393216 | tf_op jit(solution)/shard_map/all_to_all | solution.py:363
  46.3 0.8 %combine.1 = bf16[2,4,1536]{2,1,0:T(4,128)(2,1)} custom-call(f32[2,4,128]{2,1,0:T(4,128)S(1)} %get-tuple-element.12.shares, bf16[2,4,1536]{2,1,0:T(4,128)(2,1)S(1)} %get-tuple-element.14.updated, bf16[8,2,4,1536]{3,2,1,0:T(4,128)(2,1)S(1)} %all_to_all.11.returned), custom_call_target="tpu_custom_call" | custom-call | tf_op jit(solution)/shard_map/combine/pallas_call | solution.py:312
  (15 shorter events, 0.0 us)
Async XLA Ops:
  0.0 4.0 %copy-start.1 = (bf16[3072,1536]{1,0:T(8,128)(2,1)S(1)}, bf16[3072,1536]{1,0:T(8,128)(2,1)}, u32[]{:S(2)}) copy-start(bf16[3072,1536]{1,0:T(8,128)(2,1)} %refs_2_.1) | copy-start | bytes 28311556
  0.0 4.0 %copy-start.2 = (bf16[2,4,1,1536]{3,1,2,0:T(4,128)(2,1)S(1)}, bf16[2,4,1,1536]{3,1,2,0:T(4,128)(2,1)}, u32[]{:S(2)}) copy-start(bf16[2,4,1,1536]{3,1,2,0:T(4,128)(2,1)} %param.21) | copy-start | bytes 73732
  0.0 22.3 %slice-start = ((s8[16515072]{0:T(1024)(128)(4,1)}), s8[4194304]{0:T(1024)(128)(4,1)S(1)}, s32[]{:S(2)}) async-start(s8[16515072]{0:T(1024)(128)(4,1)} %bitcast.18), calls=%async_computation.2 | async-start | bytes 8388608
  0.0 22.3 %slice-start.1 = ((s8[16515072]{0:T(1024)(128)(4,1)}), s8[4194304]{0:T(1024)(128)(4,1)S(1)}, s32[]{:S(2)}) async-start(s8[16515072]{0:T(1024)(128)(4,1)} %bitcast.18), calls=%async_computation.3 | async-start | bytes 8388608
  0.0 22.3 %slice-start.4 = ((s8[16515072]{0:T(1024)(128)(4,1)}), s8[4194304]{0:T(1024)(128)(4,1)S(1)}, s32[]{:S(2)}) async-start(s8[16515072]{0:T(1024)(128)(4,1)} %bitcast.21), calls=%async_computation.6 | async-start | bytes 8388608
  0.0 22.3 %slice-start.5 = ((s8[16515072]{0:T(1024)(128)(4,1)}), s8[4194304]{0:T(1024)(128)(4,1)S(1)}, s32[]{:S(2)}) async-start(s8[16515072]{0:T(1024)(128)(4,1)} %bitcast.21), calls=%async_computation.7 | async-start | bytes 8388608
  2.6 1.4 %collective-permute-start = (bf16[4,3072]{1,0:T(4,128)(2,1)S(1)}, bf16[4,3072]{1,0:T(4,128)(2,1)S(1)}, u32[]{:S(2)}, u32[]{:S(2)}) collective-permute-start(bf16[4,3072]{1,0:T(4,128)(2,1)S(1)} %get-tuple-element.13.refs_0_), channel_id=1, source_target_pairs={{0,8},{8,0},{1,9},{9,1},{2,10},{10,2},{3,11},{11,3},{4,12},{12,4},... | collective-permute-start | bytes 73736 | tf_op jit(solution)/shard_map/ppermute | solution.py:348
  4.0 18.3 %slice-start.2 = ((s8[16515072]{0:T(1024)(128)(4,1)}), s8[4194304]{0:T(1024)(128)(4,1)S(1)}, s32[]{:S(2)}) async-start(s8[16515072]{0:T(1024)(128)(4,1)} %bitcast.18), calls=%async_computation.4 | async-start | bytes 8388608
  4.0 18.3 %slice-start.3 = ((s8[16515072]{0:T(1024)(128)(4,1)}), s8[3932160]{0:T(1024)(128)(4,1)S(1)}, s32[]{:S(2)}) async-start(s8[16515072]{0:T(1024)(128)(4,1)} %bitcast.18), calls=%async_computation.5 | async-start | bytes 7864320
  4.0 18.3 %slice-start.6 = ((s8[16515072]{0:T(1024)(128)(4,1)}), s8[4194304]{0:T(1024)(128)(4,1)S(1)}, s32[]{:S(2)}) async-start(s8[16515072]{0:T(1024)(128)(4,1)} %bitcast.21), calls=%async_computation.8 | async-start | bytes 8388608
  4.0 18.3 %slice-start.7 = ((s8[16515072]{0:T(1024)(128)(4,1)}), s8[3932160]{0:T(1024)(128)(4,1)S(1)}, s32[]{:S(2)}) async-start(s8[16515072]{0:T(1024)(128)(4,1)} %bitcast.21), calls=%async_computation.9 | async-start | bytes 7864320
  4.0 18.3 %copy-start = (f32[3072]{0:T(1024)S(1)}, f32[3072]{0:T(1024)}, u32[]{:S(2)}) copy-start(f32[3072]{0:T(1024)} %param.22) | copy-start | bytes 36868
  20.8 1.4 %collective-permute-start.1 = (bf16[64,1536]{1,0:T(8,128)(2,1)S(1)}, bf16[64,1536]{1,0:T(8,128)(2,1)S(1)}, u32[]{:S(2)}, u32[]{:S(2)}) collective-permute-start(bf16[64,1536]{1,0:T(8,128)(2,1)S(1)} %bitcast.24), channel_id=1, source_target_pairs={{0,8},{8,0},{1,9},{9,1},{2,10},{10,2},{3,11},{11,3},{4,12},{12,4},... | collective-permute-start | bytes 589832 | tf_op jit(solution)/shard_map/ppermute | solution.py:255
  33.0 1.7 %collective-permute-start.2 = (bf16[64,1536]{1,0:T(8,128)(2,1)S(1)}, bf16[64,1536]{1,0:T(8,128)(2,1)S(1)}, u32[]{:S(2)}, u32[]{:S(2)}) collective-permute-start(bf16[64,1536]{1,0:T(8,128)(2,1)S(1)} %get-tuple-element.18), channel_id=1, source_target_pairs={{0,8},{8,0},{1,9},{9,1},{2,10},{10,2},{3,11},{11,3},{4,12},{12,4},... | collective-permute-start | bytes 589832 | tf_op jit(solution)/shard_map/ppermute | solution.py:261

commit v5 on v4

--- a/solution.py
+++ b/solution.py
@@ -10,6 +10,7 @@
 
 norm_epsilon = 1e-05
 mebibyte = 1024 * 1024
+mxu_count, mxu_size = 2, 256
 hint_flops = 20_000_000_000
 last_last = (((1,), (1,)), ((), ()))
 
@@ -187,11 +188,11 @@
     parts = [part - center for part in parts]
     spread = sum(jnp.sum(jnp.square(part), axis=-1, keepdims=True) for part in parts) / width
     values = jnp.concatenate(parts, axis=1) if len(parts) > 1 else parts[0]
-    return (values * lax.rsqrt(spread + norm_epsilon) * gain).astype(jnp.bfloat16)
+    return values * lax.rsqrt(spread + norm_epsilon) * gain
 
 
 def hidden_rows(parts, gain, w_gate, w_up, hidden):
-    rows = normalize(parts, gain[...])
+    rows = normalize(parts, gain[...]).astype(jnp.bfloat16)
     for start, size in pieces_of(w_gate.shape[0], 896):
         span = slice(start, start + size)
         gate = lax.dot_general(w_gate[span, :], rows, last_last, preferred_element_type=jnp.float32)
@@ -199,9 +200,130 @@
         hidden[:, span] = (gate / (1.0 + jnp.exp(-gate)) * up).T.astype(jnp.bfloat16)
 
 
-def pair_kernel(own, other, gain, w_gate, w_up, w_down, hidden, given, kept, lent, arrived):
+def mixed_plan(units, inner):
+    own = units // mxu_count
+    blocks = own // mxu_size
+    rest = own - blocks * mxu_size
+    return own, blocks, rest, (own + rest) // 2, inner // mxu_size
+
+
+def mixed_products(normed, turned, w_gate, w_up, hidden, held, *sums):
+    units, inner = w_gate.shape
+    row_count = normed.shape[0]
+    own, blocks, rest, streamed, depth = mixed_plan(units, inner)
+    wide, narrow = sums[:mxu_count], sums[mxu_count:]
+
+    def piece(index):
+        return slice(index * mxu_size, (index + 1) * mxu_size)
+
+    for turn in range(2):
+        loaded = [(block, k) for block in range(blocks) for k in range(depth)]
+        middle = (len(loaded) + 1) // 2
+        loaded = loaded[:middle] if turn == 0 else loaded[middle:]
+        steps, done = [], 0
+        for k in range(depth):
+            upto = (k + 1) * len(loaded) // depth
+            steps += loaded[done : done + 1] + [(None, k)] + loaded[done + 1 : upto]
+            done = upto
+
+        def load(index, unit):
+            block, k = steps[index]
+            if block is None:
+                pltpu.matmul_push_rhs(turned[piece(k), :], index % 2, unit)
+            else:
+                start = unit * own + block * mxu_size
+                tile = w_up[start : start + mxu_size, piece(k)]
+                pltpu.matmul_push_rhs(tile, index % 2, unit, transpose=True)
+
+        def multiply(index, unit):
+            block, k = steps[index]
+            start, stop = unit * own, (unit + 1) * own
+            if block is not None:
+                target, left = narrow[unit * blocks + block], normed[:, piece(k)]
+            elif turn == 0:
+                target, left = wide[unit], w_gate[start : start + streamed, piece(k)]
+            else:
+                target, left = wide[unit], w_gate[start + streamed : stop, piece(k)]
+                if rest:
+                    left = jnp.concatenate([left, w_up[stop - rest : stop, piece(k)]], axis=0)
+            pltpu.matmul_acc_lhs(target, left, load_staged_rhs=index % 2)
+
+        for unit in range(mxu_count):
+            load(0, unit)
+            load(1, unit)
+        for index in range(len(steps)):
+            for unit in range(mxu_count):
+                multiply(index, unit)
+                if index + 2 < len(steps):
+                    load(index + 2, unit)
+        for unit in range(mxu_count):
+            result = pltpu.matmul_pop(wide[unit])[:, :128]
+            start = unit * own
+            if turn == 0:
+                held[start : start + streamed, :] = result
+            else:
+                held[start + streamed : start + own, :] = result[: own - streamed]
+                if rest:
+                    held[units + unit * rest : units + (unit + 1) * rest, :] = result[
+                        own - streamed :
+                    ]
+
+    for unit in range(mxu_count):
+        for block in range(blocks):
+            start = unit * own + block * mxu_size
+            up = pltpu.matmul_pop(narrow[unit * blocks + block])
+            gate = held[start : start + mxu_size, :].T[:row_count]
+            hidden[:, start : start + mxu_size] = (gate / (1.0 + jnp.exp(-gate)) * up).astype(
+                jnp.bfloat16
+            )
+        if rest:
+            start = unit * own + blocks * mxu_size
+            gate = held[start : start + rest, :]
+            up = held[units + unit * rest : units + (unit + 1) * rest, :]
+            value = (gate / (1.0 + jnp.exp(-gate)) * up).T[:row_count]
+            hidden[:, start : start + rest] = value.astype(jnp.bfloat16)
+
+
+def loaded_products(hidden, weight, out, *sums):
+    row_count, inner = hidden.shape
+    blocks = out.shape[1] // mxu_size // mxu_count
+    starts = list(range(0, inner - mxu_size + 1, mxu_size))
+    left = inner - starts[-1] - mxu_size
+    lefts = [hidden[:, start : start + mxu_size] for start in starts]
+    if left:
+        starts.append(inner - mxu_size)
+        zeros = jnp.zeros((row_count, mxu_size - left), jnp.bfloat16)
+        lefts.append(jnp.concatenate([zeros, hidden[:, inner - left :]], axis=1))
+    steps = [(block, k) for block in range(blocks) for k in range(len(starts))]
+
+    def load(index, unit):
+        block, k = steps[index]
+        column = (unit * blocks + block) * mxu_size
+        tile = weight[starts[k] : starts[k] + mxu_size, column : column + mxu_size]
+        pltpu.matmul_push_rhs(tile, index % 2, unit)
+
+    for unit in range(mxu_count):
+        load(0, unit)
+        load(1, unit)
+    for index, (block, k) in enumerate(steps):
+        for unit in range(mxu_count):
+            pltpu.matmul_acc_lhs(
+                sums[unit * blocks + block], lefts[k], load_staged_rhs=index % 2
+            )
+            if index + 2 < len(steps):
+                load(index + 2, unit)
+        if k == len(starts) - 1:
+            for unit in range(mxu_count):
+                column = (unit * blocks + block) * mxu_size
+                result = pltpu.matmul_pop(sums[unit * blocks + block])
+                out[:, column : column + mxu_size] = result.astype(jnp.bfloat16)
+
+
+def pair_kernel(own, other, gain, w_gate, w_up, w_down, hidden, given, kept, *scratch):
+    lent, normed, turned, held, arrived = scratch
     dev_index = lax.axis_index("dev")
-    width = own.shape[1]
+    row_count, width = own.shape
+    units, inner = w_gate.shape
     copies = [
         pltpu.make_async_copy(
             w_down.at[:, pl.ds(pl.multiple_of(dev * width, width), width)],
@@ -216,13 +338,30 @@
     @pl.when(dev_index < 2)
     def _():
         parts = halves(dev_index, own[...].astype(jnp.float32), other[...].astype(jnp.float32))
-        hidden_rows(parts, gain, w_gate, w_up, hidden)
+        rows = normalize(parts, gain[...])
+        normed[...] = rows.astype(jnp.bfloat16)
+        columns = rows.T.astype(jnp.bfloat16)
+        turned[:, :128] = jnp.concatenate(
+            [columns, jnp.zeros((inner, 128 - row_count), jnp.bfloat16)], axis=1
+        )
+        turned[:, 128:] = jnp.zeros((inner, mxu_size - 128), jnp.bfloat16)
+        _, blocks, _, streamed, _ = mixed_plan(units, inner)
+        sums = [pltpu.ACC(unit)((streamed, mxu_size), jnp.float32) for unit in range(mxu_count)]
+        for unit in range(mxu_count):
+            sums += [pltpu.ACC(unit)((row_count, mxu_size), jnp.float32)] * blocks
+        pl.run_scoped(
+            functools.partial(mixed_products, normed, turned, w_gate, w_up, hidden, held), *sums
+        )
 
     for copy in copies:
         copy.wait()
-    given[...] = jnp.dot(hidden[...], lent[...], preferred_element_type=jnp.float32).astype(
-        jnp.bfloat16
-    )
+    blocks = width // mxu_size // mxu_count
+    sums = [
+        pltpu.ACC(unit)((row_count, mxu_size), jnp.float32)
+        for unit in range(mxu_count)
+        for _ in range(blocks)
+    ]
+    pl.run_scoped(functools.partial(loaded_products, hidden, lent, given), *sums)
 
 
 def down_kernel(hidden, kept, out):
@@ -246,6 +385,9 @@
         out_specs=(vmem_spec,) * 3,
         scratch_shapes=[
             pltpu.VMEM((units, half), jnp.bfloat16),
+            pltpu.VMEM((rows, width), jnp.bfloat16),
+            pltpu.VMEM((width, mxu_size), jnp.bfloat16),
+            pltpu.VMEM((units + mxu_count * mxu_size, 128), jnp.float32),
             pltpu.SemaphoreType.DMA((2,)),
         ],
         compiler_params=pltpu.CompilerParams(vmem_limit_bytes=12 * mebibyte),

time: 47.2 us -> 45.6 us (0.966)
  Pallas kernels: 16.8 us -> 15.1 us
    pallas_call x1, Pallas kernels: 10.6 us -> 8.97 us  [pair_experts(): pl.pallas_call(pair_kernel, out_shape=(jax.ShapeDtypeStruct((rows, units)...]
where the time goes in v5:
time: 45.6 us; the launch traced here: 45.4 us
  blocking collectives  26.9 us (59%)
  Pallas kernels  15.1 us (33%)
  waiting for transfers between devices  2.29 us (5%)
  starting transfers between devices  0.72 us (2%)
    all_to_all x1, blocking collectives, body(): lax.all_to_all(copies, 'side', split_axis=0, concat_axis=0, tiled=True)  15.4 us
    all_to_all x1, blocking collectives, body(): lax.all_to_all(total, 'side', split_axis=0, concat_axis=0, tiled=True)  11.4 us
    pallas_call x1, Pallas kernels, pair_experts(): pl.pallas_call(pair_kernel, out_shape=(jax.ShapeDtypeStruct((rows, units)...  8.97 us
    pallas_call x1, Pallas kernels, attend(): pl.pallas_call(attend_kernel, out_shape=(jax.ShapeDtypeStruct((rows, head...  2.52 us
    pallas_call x1, Pallas kernels, pair_experts(): pl.pallas_call(down_kernel, out_shape=jax.ShapeDtypeStruct((rows, half),...  1.54 us
    ppermute x1, waiting for transfers between devices, pair_experts(): lax.ppermute(arrived, 'dev', swap)  1.44 us
    pallas_call x1, Pallas kernels, project(): pl.pallas_call(functools.partial(project_kernel, dev_count), out_shape=(j...  1.34 us
  transfers between devices with their start and end apart: 3, of which 2 were waited for; matrix products, arithmetic and copies ran while one was open for 0% of the time, Pallas kernels for 3%

profile of v5, /device:TPU:0, one launch (start us, length us, event | category | flops | bytes accessed | tf_op | source)
XLA Modules:
  0.0 45.4 jit_solution(16080917035350210607)
XLA Ops:
  0.0 0.0 slice-start.5
  0.0 2.5 %attend.1 = (bf16[4,3072]{1,0:T(4,128)(2,1)S(1)}, f32[2,4,128]{2,1,0:T(4,128)S(1)}) custom-call(s32[2,1,2]{2,1,0:T(1,128)} %bitcast.35, s32[2,4,4,8]{3,2,1,0:T(4,128)} %bitcast.32, f32[2,4,1,4]{3,2,1,0:T(1,128)} %probs.1, bf16[4,24,128]{2,1,0:T(8,128)(2,1)} %bitcast.31, bf16[4,512,128]{2,1,0:T(8,128)(2,1)} %bitcast.29, bf16[4,512,128]{2,1,0:T(8,128)(2,1)} %bitcast.30, ...), custom_call_target="tpu_custom_call" | custom-call | flops 20000000000 | bytes 1048576 | tf_op jit(solution)/shard_map/attend/pallas_call | solution.py:102
  2.6 0.5 %collective-permute-start = (bf16[4,3072]{1,0:T(4,128)(2,1)S(1)}, bf16[4,3072]{1,0:T(4,128)(2,1)S(1)}, u32[]{:S(2)}, u32[]{:S(2)}) collective-permute-start(bf16[4,3072]{1,0:T(4,128)(2,1)S(1)} %get-tuple-element.13.refs_0_), channel_id=1, source_target_pairs={{0,8},{8,0},{1,9},{9,1},{2,10},{10,2},{3,11},{11,3},{4,12},{12,4},... | collective-permute-start | bytes 73736 | tf_op jit(solution)/shard_map/ppermute | solution.py:490
  3.1 0.8 %collective-permute-done.refs_1_ = bf16[4,3072]{1,0:T(4,128)(2,1)S(1)} collective-permute-done((bf16[4,3072]{1,0:T(4,128)(2,1)S(1)}, bf16[4,3072]{1,0:T(4,128)(2,1)S(1)}, u32[]{:S(2)}, u32[]{:S(2)}) %collective-permute-start) | collective-permute-done | bytes 24608 | tf_op jit(solution)/shard_map/ppermute | solution.py:490
  3.9 0.1 copy-done.1
  4.0 0.0 copy-done.2
  4.0 0.0 slice-start.7
  4.0 0.0 copy-start
  4.1 1.3 %project.1 = (bf16[2,4,1536]{2,1,0:T(4,128)(2,1)S(1)}, bf16[8,8,1536]{2,1,0:T(8,128)(2,1)S(1)}) custom-call(bf16[4,3072]{1,0:T(4,128)(2,1)S(1)} %get-tuple-element.13.refs_0_, bf16[4,3072]{1,0:T(4,128)(2,1)S(1)} %collective-permute-done.refs_1_, bf16[3072,1536]{1,0:T(8,128)(2,1)S(1)} %copy-done.1, bf16[2,4,1536]{2,1,0:T(4,128)(2,1)S(1)} %bitcast.27), custom_call_target="tpu_custom_call" | custom-call | flops 20000000000 | bytes 9437184 | tf_op jit(solution)/shard_map/project/pallas_call | solution.py:165
  5.4 15.4 %all_to_all.10 = bf16[8,8,1536]{2,1,0:T(8,128)(2,1)S(1)} all-to-all(bf16[8,8,1536]{2,1,0:T(8,128)(2,1)S(1)} %get-tuple-element.15), channel_id=1, replica_groups=mesh['groups'=2,'dev'=2,'side'=8] {'side'}, dimensions={0} | all-to-all | bytes 393216 | tf_op jit(solution)/shard_map/all_to_all | solution.py:500
  20.8 0.0 collective-permute-start.1
  20.8 1.4 %collective-permute-done.1.other = bf16[64,1536]{1,0:T(8,128)(2,1)S(1)} collective-permute-done((bf16[64,1536]{1,0:T(8,128)(2,1)S(1)}, bf16[64,1536]{1,0:T(8,128)(2,1)S(1)}, u32[]{:S(2)}, u32[]{:S(2)}) %collective-permute-start.1) | collective-permute-done | bytes 196640 | tf_op jit(solution)/shard_map/ppermute | solution.py:397
  22.3 0.0 slice-done
  22.3 0.0 slice-done.1
  22.3 0.0 slice-done.4
  22.3 0.0 slice-done.5
  22.4 9.0 %experts.1 = (bf16[64,2688]{1,0:T(8,128)(2,1)S(1)}, bf16[64,1536]{1,0:T(8,128)(2,1)S(1)}, bf16[2688,1536]{1,0:T(8,128)(2,1)S(1)}) custom-call(bf16[64,1536]{1,0:T(8,128)(2,1)S(1)} %bitcast.25, bf16[64,1536]{1,0:T(8,128)(2,1)S(1)} %collective-permute-done.1.other, f32[1,3072]{1,0:T(1,128)S(1)} %bitcast.26, bf16[2688,3072]{1,0:T(8,128)(2,1)S(1)} %bitcast.20, ...), custom_call_target="tpu_custom_call" | custom-call | tf_op jit(solution)/shard_map/experts/pallas_call | solution.py:377
  31.3 0.2 collective-permute-start.2
  31.5 1.5 %down_own.1 = bf16[64,1536]{1,0:T(8,128)(2,1)S(1)} custom-call(bf16[64,2688]{1,0:T(8,128)(2,1)S(1)} %get-tuple-element.16.hidden, bf16[2688,1536]{1,0:T(8,128)(2,1)S(1)} %get-tuple-element.17.kept), custom_call_target="tpu_custom_call" | custom-call | tf_op jit(solution)/shard_map/down_own/pallas_call | solution.py:404
  33.1 0.0 collective-permute-done.2
  33.1 0.1 add_convert_fusion
  33.1 0.1 reshape.38
  33.2 11.4 %all_to_all.11.returned = bf16[8,2,4,1536]{3,2,1,0:T(4,128)(2,1)S(1)} all-to-all(bf16[8,2,4,1536]{3,2,1,0:T(4,128)(2,1)S(1)} %reshape.38), channel_id=1, replica_groups=mesh['groups'=2,'dev'=2,'side'=8] {'side'}, dimensions={0} | all-to-all | bytes 393216 | tf_op jit(solution)/shard_map/all_to_all | solution.py:505
  44.6 0.8 %combine.1 = bf16[2,4,1536]{2,1,0:T(4,128)(2,1)} custom-call(f32[2,4,128]{2,1,0:T(4,128)S(1)} %get-tuple-element.12.shares, bf16[2,4,1536]{2,1,0:T(4,128)(2,1)S(1)} %get-tuple-element.14.updated, bf16[8,2,4,1536]{3,2,1,0:T(4,128)(2,1)S(1)} %all_to_all.11.returned), custom_call_target="tpu_custom_call" | custom-call | tf_op jit(solution)/shard_map/combine/pallas_call | solution.py:454
  (15 shorter events, 0.0 us)
Async XLA Ops:
  0.0 4.0 %copy-start.1 = (bf16[3072,1536]{1,0:T(8,128)(2,1)S(1)}, bf16[3072,1536]{1,0:T(8,128)(2,1)}, u32[]{:S(2)}) copy-start(bf16[3072,1536]{1,0:T(8,128)(2,1)} %refs_2_.1) | copy-start | bytes 28311556
  0.0 4.0 %copy-start.2 = (bf16[2,4,1,1536]{3,1,2,0:T(4,128)(2,1)S(1)}, bf16[2,4,1,1536]{3,1,2,0:T(4,128)(2,1)}, u32[]{:S(2)}) copy-start(bf16[2,4,1,1536]{3,1,2,0:T(4,128)(2,1)} %param.21) | copy-start | bytes 73732
  0.0 22.3 %slice-start = ((s8[16515072]{0:T(1024)(128)(4,1)}), s8[4194304]{0:T(1024)(128)(4,1)S(1)}, s32[]{:S(2)}) async-start(s8[16515072]{0:T(1024)(128)(4,1)} %bitcast.18), calls=%async_computation.2 | async-start | bytes 8388608
  0.0 22.3 %slice-start.1 = ((s8[16515072]{0:T(1024)(128)(4,1)}), s8[4194304]{0:T(1024)(128)(4,1)S(1)}, s32[]{:S(2)}) async-start(s8[16515072]{0:T(1024)(128)(4,1)} %bitcast.18), calls=%async_computation.3 | async-start | bytes 8388608
  0.0 22.3 %slice-start.4 = ((s8[16515072]{0:T(1024)(128)(4,1)}), s8[4194304]{0:T(1024)(128)(4,1)S(1)}, s32[]{:S(2)}) async-start(s8[16515072]{0:T(1024)(128)(4,1)} %bitcast.21), calls=%async_computation.6 | async-start | bytes 8388608
  0.0 22.3 %slice-start.5 = ((s8[16515072]{0:T(1024)(128)(4,1)}), s8[4194304]{0:T(1024)(128)(4,1)S(1)}, s32[]{:S(2)}) async-start(s8[16515072]{0:T(1024)(128)(4,1)} %bitcast.21), calls=%async_computation.7 | async-start | bytes 8388608
  2.6 1.4 %collective-permute-start = (bf16[4,3072]{1,0:T(4,128)(2,1)S(1)}, bf16[4,3072]{1,0:T(4,128)(2,1)S(1)}, u32[]{:S(2)}, u32[]{:S(2)}) collective-permute-start(bf16[4,3072]{1,0:T(4,128)(2,1)S(1)} %get-tuple-element.13.refs_0_), channel_id=1, source_target_pairs={{0,8},{8,0},{1,9},{9,1},{2,10},{10,2},{3,11},{11,3},{4,12},{12,4},... | collective-permute-start | bytes 73736 | tf_op jit(solution)/shard_map/ppermute | solution.py:490
  4.0 18.3 %slice-start.2 = ((s8[16515072]{0:T(1024)(128)(4,1)}), s8[4194304]{0:T(1024)(128)(4,1)S(1)}, s32[]{:S(2)}) async-start(s8[16515072]{0:T(1024)(128)(4,1)} %bitcast.18), calls=%async_computation.4 | async-start | bytes 8388608
  4.0 18.3 %slice-start.3 = ((s8[16515072]{0:T(1024)(128)(4,1)}), s8[3932160]{0:T(1024)(128)(4,1)S(1)}, s32[]{:S(2)}) async-start(s8[16515072]{0:T(1024)(128)(4,1)} %bitcast.18), calls=%async_computation.5 | async-start | bytes 7864320
  4.0 18.3 %slice-start.6 = ((s8[16515072]{0:T(1024)(128)(4,1)}), s8[4194304]{0:T(1024)(128)(4,1)S(1)}, s32[]{:S(2)}) async-start(s8[16515072]{0:T(1024)(128)(4,1)} %bitcast.21), calls=%async_computation.8 | async-start | bytes 8388608
  4.0 18.3 %slice-start.7 = ((s8[16515072]{0:T(1024)(128)(4,1)}), s8[3932160]{0:T(1024)(128)(4,1)S(1)}, s32[]{:S(2)}) async-start(s8[16515072]{0:T(1024)(128)(4,1)} %bitcast.21), calls=%async_computation.9 | async-start | bytes 7864320
  4.0 18.3 %copy-start = (f32[3072]{0:T(1024)S(1)}, f32[3072]{0:T(1024)}, u32[]{:S(2)}) copy-start(f32[3072]{0:T(1024)} %param.22) | copy-start | bytes 36868
  20.8 1.4 %collective-permute-start.1 = (bf16[64,1536]{1,0:T(8,128)(2,1)S(1)}, bf16[64,1536]{1,0:T(8,128)(2,1)S(1)}, u32[]{:S(2)}, u32[]{:S(2)}) collective-permute-start(bf16[64,1536]{1,0:T(8,128)(2,1)S(1)} %bitcast.24), channel_id=1, source_target_pairs={{0,8},{8,0},{1,9},{9,1},{2,10},{10,2},{3,11},{11,3},{4,12},{12,4},... | collective-permute-start | bytes 589832 | tf_op jit(solution)/shard_map/ppermute | solution.py:397
  31.3 1.7 %collective-permute-start.2 = (bf16[64,1536]{1,0:T(8,128)(2,1)S(1)}, bf16[64,1536]{1,0:T(8,128)(2,1)S(1)}, u32[]{:S(2)}, u32[]{:S(2)}) collective-permute-start(bf16[64,1536]{1,0:T(8,128)(2,1)S(1)} %get-tuple-element.18), channel_id=1, source_target_pairs={{0,8},{8,0},{1,9},{9,1},{2,10},{10,2},{3,11},{11,3},{4,12},{12,4},... | collective-permute-start | bytes 589832 | tf_op jit(solution)/shard_map/ppermute | solution.py:403

commit v6 on v5

--- a/solution.py
+++ b/solution.py
@@ -67,25 +67,37 @@
             result = jnp.where(key_head == index, wide[index : index + 1, :], result)
         return result
 
-    for row in range(row_count):
-        query = queries[row]
-        scores = (
-            lax.dot_general(query, keys[row], last_last, preferred_element_type=jnp.float32)
-            * factor
+    all_rows = range(row_count)
+    scores = [
+        lax.dot_general(queries[row], keys[row], last_last, preferred_element_type=jnp.float32)
+        for row in all_rows
+    ]
+    fresh = [
+        jnp.sum(queries[row].astype(jnp.float32) * spread(new_keys[row]), axis=-1, keepdims=True)
+        for row in all_rows
+    ]
+    lengths_of = [lengths[row // local_rows, 0, row % local_rows] for row in all_rows]
+    raised = [
+        jnp.where(position < lengths_of[row], jnp.exp(scores[row] * factor), 0.0)
+        for row in all_rows
+    ]
+    raised_new = [jnp.exp(fresh[row] * factor) for row in all_rows]
+    inverse = [
+        1.0 / (jnp.sum(raised[row], axis=-1, keepdims=True) + raised_new[row]) for row in all_rows
+    ]
+    mixed = [
+        jnp.dot(
+            (raised[row] * inverse[row]).astype(jnp.bfloat16),
+            values[row],
+            preferred_element_type=jnp.float32,
         )
-        length = lengths[row // local_rows, 0, row % local_rows]
-        raised = jnp.where(position < length, jnp.exp(scores), 0.0)
-        fresh = (
-            jnp.sum(query.astype(jnp.float32) * spread(new_keys[row]), axis=-1, keepdims=True)
-            * factor
+        for row in all_rows
+    ]
+    for row in all_rows:
+        weight_new = (raised_new[row] * inverse[row]).astype(jnp.bfloat16).astype(jnp.float32)
+        scratch[pl.ds(row * head_count, head_count), :] = mixed[row] + weight_new * spread(
+            new_values[row]
         )
-        raised_new = jnp.exp(fresh)
-        denominator = jnp.sum(raised, axis=-1, keepdims=True) + raised_new
-        weights = (raised / denominator).astype(jnp.bfloat16)
-        weight_new = (raised_new / denominator).astype(jnp.bfloat16).astype(jnp.float32)
-        mixed = jnp.dot(weights, values[row], preferred_element_type=jnp.float32)
-        mixed = mixed + weight_new * spread(new_values[row])
-        scratch[pl.ds(row * head_count, head_count), :] = mixed
     pieces = [
         scratch[pl.ds(index, row_count, stride=head_count), :] for index in range(head_count)
     ]
@@ -108,7 +120,7 @@
         in_specs=[smem_spec] * 3 + [vmem_spec] * 5,
         out_specs=(vmem_spec, vmem_spec),
         scratch_shapes=[pltpu.VMEM((rows * head_count, head_width), jnp.float32)],
-        compiler_params=pltpu.CompilerParams(vmem_limit_bytes=3 * mebibyte),
+        compiler_params=pltpu.CompilerParams(vmem_limit_bytes=50 * mebibyte),
         name="attend",
         cost_estimate=pl.CostEstimate(
             flops=hint_flops, transcendentals=0, bytes_accessed=cache_keys.size * 4
@@ -441,13 +453,15 @@
 
 
 def combine_kernel(shares, updated, returned, out):
-    batch_count = updated.shape[0]
+    batch_count, row_count, _ = updated.shape
+    weights = jnp.concatenate([shares[batch] for batch in range(batch_count)], axis=0)
+    total = jnp.concatenate(
+        [updated[batch].astype(jnp.float32) for batch in range(batch_count)], axis=0
+    )
+    for expert in range(returned.shape[0]):
+        total = total + weights[:, expert : expert + 1] * returned[expert].astype(jnp.float32)
     for batch in range(batch_count):
-        total = updated[batch].astype(jnp.float32)
-        for expert in range(returned.shape[0]):
-            share = shares[batch, :, expert : expert + 1]
-            total = total + share * returned[expert, batch].astype(jnp.float32)
-        out[batch] = total.astype(jnp.bfloat16)
+        out[batch] = total[batch * row_count : (batch + 1) * row_count].astype(jnp.bfloat16)
 
 
 def combine(shares, updated, returned):
@@ -501,7 +515,7 @@
     arrived = arrived.reshape(side_count * rows, column_width)
     gather_and_run = pair_experts if dev_count == 2 else whole_experts
     total = gather_and_run(arrived, norm_gain, w_gate[0], w_up[0], w_down[0])
-    total = total.astype(jnp.bfloat16).reshape(side_count, batch_count, row_count, column_width)
+    total = total.astype(jnp.bfloat16).reshape(side_count, rows, column_width)
     returned = lax.all_to_all(total, "side", split_axis=0, concat_axis=0, tiled=True)
     result = combine(shares, updated, returned)
     return result.reshape(residual.shape)

time: 45.6 us -> 45.3 us (level)
  Pallas kernels: 15.1 us -> 14.5 us
  local copies, waits for them, and re-layouts: 0.18 us -> 0.75 us
    unnamed x22 -> x10, local copies, waits for them, and re-layouts: 0.12 us -> 0.75 us
    pallas_call x1, Pallas kernels: 2.52 us -> 1.92 us  [attend(): pl.pallas_call(attend_kernel, out_shape=(jax.ShapeDtypeStruct((rows, head...]
where the time goes in v6:
time: 45.3 us; the launch traced here: 45.1 us
  blocking collectives  26.7 us (59%)
  Pallas kernels  14.5 us (32%)
  waiting for transfers between devices  2.29 us (5%)
  local copies, waits for them, and re-layouts  0.75 us (2%)
  starting transfers between devices  0.71 us (2%)
    all_to_all x1, blocking collectives, body(): lax.all_to_all(copies, 'side', split_axis=0, concat_axis=0, tiled=True)  15.3 us
    all_to_all x1, blocking collectives, body(): lax.all_to_all(total, 'side', split_axis=0, concat_axis=0, tiled=True)  11.4 us
    pallas_call x1, Pallas kernels, pair_experts(): pl.pallas_call(pair_kernel, out_shape=(jax.ShapeDtypeStruct((rows, units)...  8.96 us
    pallas_call x1, Pallas kernels, attend(): pl.pallas_call(attend_kernel, out_shape=(jax.ShapeDtypeStruct((rows, head...  1.92 us
    pallas_call x1, Pallas kernels, pair_experts(): pl.pallas_call(down_kernel, out_shape=jax.ShapeDtypeStruct((rows, half),...  1.54 us
    ppermute x1, waiting for transfers between devices, pair_experts(): lax.ppermute(arrived, 'dev', swap)  1.44 us
    pallas_call x1, Pallas kernels, project(): pl.pallas_call(functools.partial(project_kernel, dev_count), out_shape=(j...  1.34 us
  transfers between devices with their start and end apart: 3, of which 2 were waited for; matrix products, arithmetic and copies ran while one was open for 0% of the time, Pallas kernels for 3%

profile of v6, /device:TPU:0, one launch (start us, length us, event | category | flops | bytes accessed | tf_op | source)
XLA Modules:
  0.0 45.1 jit_solution(15845282764138482951)
XLA Ops:
  0.0 0.0 copy-start.3
  0.0 0.0 copy-start.4
  0.0 1.9 %attend.1 = (bf16[4,3072]{1,0:T(4,128)(2,1)S(1)}, f32[2,4,128]{2,1,0:T(4,128)S(1)}) custom-call(s32[2,1,2]{2,1,0:T(1,128)} %bitcast.33, s32[2,4,4,8]{3,2,1,0:T(4,128)} %bitcast.30, f32[2,4,1,4]{3,2,1,0:T(1,128)} %probs.1, bf16[4,24,128]{2,1,0:T(8,128)(2,1)} %bitcast.29, bf16[4,512,128]{2,1,0:T(8,128)(2,1)} %bitcast.27, bf16[4,512,128]{2,1,0:T(8,128)(2,1)} %bitcast.28, ...), custom_call_target="tpu_custom_call" | custom-call | flops 20000000000 | bytes 1048576 | tf_op jit(solution)/shard_map/attend/pallas_call | solution.py:114
  1.9 0.5 %collective-permute-start = (bf16[4,3072]{1,0:T(4,128)(2,1)S(1)}, bf16[4,3072]{1,0:T(4,128)(2,1)S(1)}, u32[]{:S(2)}, u32[]{:S(2)}) collective-permute-start(bf16[4,3072]{1,0:T(4,128)(2,1)S(1)} %get-tuple-element.13.refs_0_), channel_id=1, source_target_pairs={{0,8},{8,0},{1,9},{9,1},{2,10},{10,2},{3,11},{11,3},{4,12},{12,4},... | collective-permute-start | bytes 73736 | tf_op jit(solution)/shard_map/ppermute | solution.py:504
  2.5 0.8 %collective-permute-done.refs_1_ = bf16[4,3072]{1,0:T(4,128)(2,1)S(1)} collective-permute-done((bf16[4,3072]{1,0:T(4,128)(2,1)S(1)}, bf16[4,3072]{1,0:T(4,128)(2,1)S(1)}, u32[]{:S(2)}, u32[]{:S(2)}) %collective-permute-start) | collective-permute-done | bytes 24608 | tf_op jit(solution)/shard_map/ppermute | solution.py:504
  3.3 0.7 %copy-done.3 = bf16[3072,1536]{1,0:T(8,128)(2,1)S(1)} copy-done((bf16[3072,1536]{1,0:T(8,128)(2,1)S(1)}, bf16[3072,1536]{1,0:T(8,128)(2,1)}, u32[]{:S(2)}) %copy-start.3) | copy-done | bytes 9437208
  4.0 0.0 copy-done.4
  4.0 0.0 copy-start
  4.0 0.0 copy-start.1
  4.0 0.0 copy-start.2
  4.1 1.3 %project.1 = (bf16[2,4,1536]{2,1,0:T(4,128)(2,1)S(1)}, bf16[8,8,1536]{2,1,0:T(8,128)(2,1)S(1)}) custom-call(bf16[4,3072]{1,0:T(4,128)(2,1)S(1)} %get-tuple-element.13.refs_0_, bf16[4,3072]{1,0:T(4,128)(2,1)S(1)} %collective-permute-done.refs_1_, bf16[3072,1536]{1,0:T(8,128)(2,1)S(1)} %copy-done.3, bf16[2,4,1536]{2,1,0:T(4,128)(2,1)S(1)} %bitcast.25), custom_call_target="tpu_custom_call" | custom-call | flops 20000000000 | bytes 9437184 | tf_op jit(solution)/shard_map/project/pallas_call | solution.py:177
  5.4 15.3 %all_to_all.10 = bf16[8,8,1536]{2,1,0:T(8,128)(2,1)S(1)} all-to-all(bf16[8,8,1536]{2,1,0:T(8,128)(2,1)S(1)} %get-tuple-element.15), channel_id=1, replica_groups=mesh['groups'=2,'dev'=2,'side'=8] {'side'}, dimensions={0} | all-to-all | bytes 393216 | tf_op jit(solution)/shard_map/all_to_all | solution.py:514
  20.7 0.0 collective-permute-start.1
  20.7 1.4 %collective-permute-done.1.other = bf16[64,1536]{1,0:T(8,128)(2,1)S(1)} collective-permute-done((bf16[64,1536]{1,0:T(8,128)(2,1)S(1)}, bf16[64,1536]{1,0:T(8,128)(2,1)S(1)}, u32[]{:S(2)}, u32[]{:S(2)}) %collective-permute-start.1) | collective-permute-done | bytes 196640 | tf_op jit(solution)/shard_map/ppermute | solution.py:409
  22.1 0.0 copy-done
  22.1 0.0 copy-done.1
  22.1 0.0 copy-done.2
  22.1 9.0 %experts.1 = (bf16[64,2688]{1,0:T(8,128)(2,1)S(1)}, bf16[64,1536]{1,0:T(8,128)(2,1)S(1)}, bf16[2688,1536]{1,0:T(8,128)(2,1)S(1)}) custom-call(bf16[64,1536]{1,0:T(8,128)(2,1)S(1)} %bitcast.23, bf16[64,1536]{1,0:T(8,128)(2,1)S(1)} %collective-permute-done.1.other, f32[1,3072]{1,0:T(1,128)S(1)} %bitcast.24, bf16[2688,3072]{1,0:T(8,128)(2,1)S(1)} %bitcast.20, ...), custom_call_target="tpu_custom_call" | custom-call | tf_op jit(solution)/shard_map/experts/pallas_call | solution.py:389
  31.1 0.2 collective-permute-start.2
  31.3 1.5 %down_own.1 = bf16[64,1536]{1,0:T(8,128)(2,1)S(1)} custom-call(bf16[64,2688]{1,0:T(8,128)(2,1)S(1)} %get-tuple-element.16.hidden, bf16[2688,1536]{1,0:T(8,128)(2,1)S(1)} %get-tuple-element.17.kept), custom_call_target="tpu_custom_call" | custom-call | tf_op jit(solution)/shard_map/down_own/pallas_call | solution.py:416
  32.8 0.0 collective-permute-done.2
  32.8 0.1 fusion
  32.9 11.4 %all_to_all.11.returned = bf16[8,8,1536]{2,1,0:T(8,128)(2,1)S(1)} all-to-all(bf16[8,8,1536]{2,1,0:T(8,128)(2,1)S(1)} %fusion), channel_id=1, replica_groups=mesh['groups'=2,'dev'=2,'side'=8] {'side'}, dimensions={0} | all-to-all | bytes 393216 | tf_op jit(solution)/shard_map/all_to_all | solution.py:519
  44.3 0.7 %combine.1 = bf16[2,4,1536]{2,1,0:T(4,128)(2,1)} custom-call(f32[2,4,128]{2,1,0:T(4,128)S(1)} %get-tuple-element.12.shares, bf16[2,4,1536]{2,1,0:T(4,128)(2,1)S(1)} %get-tuple-element.14.updated, bf16[8,8,1536]{2,1,0:T(8,128)(2,1)S(1)} %all_to_all.11.returned), custom_call_target="tpu_custom_call" | custom-call | tf_op jit(solution)/shard_map/combine/pallas_call | solution.py:468
Async XLA Ops:
  0.0 4.0 %copy-start.3 = (bf16[3072,1536]{1,0:T(8,128)(2,1)S(1)}, bf16[3072,1536]{1,0:T(8,128)(2,1)}, u32[]{:S(2)}) copy-start(bf16[3072,1536]{1,0:T(8,128)(2,1)} %refs_2_.1) | copy-start | bytes 28311556
  0.0 4.0 %copy-start.4 = (bf16[2,4,1,1536]{3,1,2,0:T(4,128)(2,1)S(1)}, bf16[2,4,1,1536]{3,1,2,0:T(4,128)(2,1)}, u32[]{:S(2)}) copy-start(bf16[2,4,1,1536]{3,1,2,0:T(4,128)(2,1)} %param.21) | copy-start | bytes 73732
  1.9 1.4 %collective-permute-start = (bf16[4,3072]{1,0:T(4,128)(2,1)S(1)}, bf16[4,3072]{1,0:T(4,128)(2,1)S(1)}, u32[]{:S(2)}, u32[]{:S(2)}) collective-permute-start(bf16[4,3072]{1,0:T(4,128)(2,1)S(1)} %get-tuple-element.13.refs_0_), channel_id=1, source_target_pairs={{0,8},{8,0},{1,9},{9,1},{2,10},{10,2},{3,11},{11,3},{4,12},{12,4},... | collective-permute-start | bytes 73736 | tf_op jit(solution)/shard_map/ppermute | solution.py:504
  4.0 18.1 %copy-start = (bf16[1,2688,3072]{2,1,0:T(8,128)(2,1)S(1)}, bf16[1,2688,3072]{2,1,0:T(8,128)(2,1)}, u32[]{:S(2)}) copy-start(bf16[1,2688,3072]{2,1,0:T(8,128)(2,1)} %param.25) | copy-start | bytes 49545220
  4.0 18.1 %copy-start.1 = (bf16[1,2688,3072]{2,1,0:T(8,128)(2,1)S(1)}, bf16[1,2688,3072]{2,1,0:T(8,128)(2,1)}, u32[]{:S(2)}) copy-start(bf16[1,2688,3072]{2,1,0:T(8,128)(2,1)} %param.26) | copy-start | bytes 49545220
  4.0 18.1 %copy-start.2 = (f32[3072]{0:T(1024)S(1)}, f32[3072]{0:T(1024)}, u32[]{:S(2)}) copy-start(f32[3072]{0:T(1024)} %param.22) | copy-start | bytes 36868
  20.7 1.4 %collective-permute-start.1 = (bf16[64,1536]{1,0:T(8,128)(2,1)S(1)}, bf16[64,1536]{1,0:T(8,128)(2,1)S(1)}, u32[]{:S(2)}, u32[]{:S(2)}) collective-permute-start(bf16[64,1536]{1,0:T(8,128)(2,1)S(1)} %bitcast.22), channel_id=1, source_target_pairs={{0,8},{8,0},{1,9},{9,1},{2,10},{10,2},{3,11},{11,3},{4,12},{12,4},... | collective-permute-start | bytes 589832 | tf_op jit(solution)/shard_map/ppermute | solution.py:409
  31.1 1.7 %collective-permute-start.2 = (bf16[64,1536]{1,0:T(8,128)(2,1)S(1)}, bf16[64,1536]{1,0:T(8,128)(2,1)S(1)}, u32[]{:S(2)}, u32[]{:S(2)}) collective-permute-start(bf16[64,1536]{1,0:T(8,128)(2,1)S(1)} %get-tuple-element.18), channel_id=1, source_target_pairs={{0,8},{8,0},{1,9},{9,1},{2,10},{10,2},{3,11},{11,3},{4,12},{12,4},... | collective-permute-start | bytes 589832 | tf_op jit(solution)/shard_map/ppermute | solution.py:415

commit v7 on v6

--- a/solution.py
+++ b/solution.py
@@ -228,6 +228,16 @@
     def piece(index):
         return slice(index * mxu_size, (index + 1) * mxu_size)
 
+    def finish(block):
+        for unit in range(mxu_count):
+            start = unit * own + block * mxu_size
+            up = pltpu.matmul_pop(narrow[unit * blocks + block])
+            gate = held[start : start + mxu_size, :].T[:row_count]
+            hidden[:, start : start + mxu_size] = (gate / (1.0 + jnp.exp(-gate)) * up).astype(
+                jnp.bfloat16
+            )
+
+    finished = 0
     for turn in range(2):
         loaded = [(block, k) for block in range(blocks) for k in range(depth)]
         middle = (len(loaded) + 1) // 2
@@ -280,14 +290,12 @@
                         own - streamed :
                     ]
 
+        ready = blocks if turn else min(middle // depth, streamed // mxu_size)
+        for block in range(finished, ready):
+            finish(block)
+        finished = ready
+
     for unit in range(mxu_count):
-        for block in range(blocks):
-            start = unit * own + block * mxu_size
-            up = pltpu.matmul_pop(narrow[unit * blocks + block])
-            gate = held[start : start + mxu_size, :].T[:row_count]
-            hidden[:, start : start + mxu_size] = (gate / (1.0 + jnp.exp(-gate)) * up).astype(
-                jnp.bfloat16
-            )
         if rest:
             start = unit * own + blocks * mxu_size
             gate = held[start : start + rest, :]

time: 45.3 us -> 45.2 us (level)
  no operation moved by 1% of the time
where the time goes in v7:
time: 45.2 us; the launch traced here: 45 us
  blocking collectives  26.7 us (59%)
  Pallas kernels  14.5 us (32%)
  waiting for transfers between devices  2.29 us (5%)
  local copies, waits for them, and re-layouts  0.75 us (2%)
  starting transfers between devices  0.71 us (2%)
    all_to_all x1, blocking collectives, body(): lax.all_to_all(copies, 'side', split_axis=0, concat_axis=0, tiled=True)  15.3 us
    all_to_all x1, blocking collectives, body(): lax.all_to_all(total, 'side', split_axis=0, concat_axis=0, tiled=True)  11.4 us
    pallas_call x1, Pallas kernels, pair_experts(): pl.pallas_call(pair_kernel, out_shape=(jax.ShapeDtypeStruct((rows, units)...  8.93 us
    pallas_call x1, Pallas kernels, attend(): pl.pallas_call(attend_kernel, out_shape=(jax.ShapeDtypeStruct((rows, head...  1.92 us
    pallas_call x1, Pallas kernels, pair_experts(): pl.pallas_call(down_kernel, out_shape=jax.ShapeDtypeStruct((rows, half),...  1.54 us
    ppermute x1, waiting for transfers between devices, pair_experts(): lax.ppermute(arrived, 'dev', swap)  1.44 us
    pallas_call x1, Pallas kernels, project(): pl.pallas_call(functools.partial(project_kernel, dev_count), out_shape=(j...  1.34 us
  transfers between devices with their start and end apart: 3, of which 2 were waited for; matrix products, arithmetic and copies ran while one was open for 0% of the time, Pallas kernels for 3%

profile of v7, /device:TPU:0, one launch (start us, length us, event | category | flops | bytes accessed | tf_op | source)
XLA Modules:
  0.0 45.0 jit_solution(650635529671235412)
XLA Ops:
  0.0 0.0 copy-start.3
  0.0 0.0 copy-start.4
  0.0 1.9 %attend.1 = (bf16[4,3072]{1,0:T(4,128)(2,1)S(1)}, f32[2,4,128]{2,1,0:T(4,128)S(1)}) custom-call(s32[2,1,2]{2,1,0:T(1,128)} %bitcast.33, s32[2,4,4,8]{3,2,1,0:T(4,128)} %bitcast.30, f32[2,4,1,4]{3,2,1,0:T(1,128)} %probs.1, bf16[4,24,128]{2,1,0:T(8,128)(2,1)} %bitcast.29, bf16[4,512,128]{2,1,0:T(8,128)(2,1)} %bitcast.27, bf16[4,512,128]{2,1,0:T(8,128)(2,1)} %bitcast.28, ...), custom_call_target="tpu_custom_call" | custom-call | flops 20000000000 | bytes 1048576 | tf_op jit(solution)/shard_map/attend/pallas_call | solution.py:114
  1.9 0.5 %collective-permute-start = (bf16[4,3072]{1,0:T(4,128)(2,1)S(1)}, bf16[4,3072]{1,0:T(4,128)(2,1)S(1)}, u32[]{:S(2)}, u32[]{:S(2)}) collective-permute-start(bf16[4,3072]{1,0:T(4,128)(2,1)S(1)} %get-tuple-element.13.refs_0_), channel_id=1, source_target_pairs={{0,8},{8,0},{1,9},{9,1},{2,10},{10,2},{3,11},{11,3},{4,12},{12,4},... | collective-permute-start | bytes 73736 | tf_op jit(solution)/shard_map/ppermute | solution.py:512
  2.5 0.8 %collective-permute-done.refs_1_ = bf16[4,3072]{1,0:T(4,128)(2,1)S(1)} collective-permute-done((bf16[4,3072]{1,0:T(4,128)(2,1)S(1)}, bf16[4,3072]{1,0:T(4,128)(2,1)S(1)}, u32[]{:S(2)}, u32[]{:S(2)}) %collective-permute-start) | collective-permute-done | bytes 24608 | tf_op jit(solution)/shard_map/ppermute | solution.py:512
  3.3 0.7 %copy-done.3 = bf16[3072,1536]{1,0:T(8,128)(2,1)S(1)} copy-done((bf16[3072,1536]{1,0:T(8,128)(2,1)S(1)}, bf16[3072,1536]{1,0:T(8,128)(2,1)}, u32[]{:S(2)}) %copy-start.3) | copy-done | bytes 9437208
  4.0 0.0 copy-done.4
  4.0 0.0 copy-start
  4.0 0.0 copy-start.1
  4.0 0.0 copy-start.2
  4.1 1.3 %project.1 = (bf16[2,4,1536]{2,1,0:T(4,128)(2,1)S(1)}, bf16[8,8,1536]{2,1,0:T(8,128)(2,1)S(1)}) custom-call(bf16[4,3072]{1,0:T(4,128)(2,1)S(1)} %get-tuple-element.13.refs_0_, bf16[4,3072]{1,0:T(4,128)(2,1)S(1)} %collective-permute-done.refs_1_, bf16[3072,1536]{1,0:T(8,128)(2,1)S(1)} %copy-done.3, bf16[2,4,1536]{2,1,0:T(4,128)(2,1)S(1)} %bitcast.25), custom_call_target="tpu_custom_call" | custom-call | flops 20000000000 | bytes 9437184 | tf_op jit(solution)/shard_map/project/pallas_call | solution.py:177
  5.4 15.3 %all_to_all.10 = bf16[8,8,1536]{2,1,0:T(8,128)(2,1)S(1)} all-to-all(bf16[8,8,1536]{2,1,0:T(8,128)(2,1)S(1)} %get-tuple-element.15), channel_id=1, replica_groups=mesh['groups'=2,'dev'=2,'side'=8] {'side'}, dimensions={0} | all-to-all | bytes 393216 | tf_op jit(solution)/shard_map/all_to_all | solution.py:522
  20.7 0.0 collective-permute-start.1
  20.7 1.4 %collective-permute-done.1.other = bf16[64,1536]{1,0:T(8,128)(2,1)S(1)} collective-permute-done((bf16[64,1536]{1,0:T(8,128)(2,1)S(1)}, bf16[64,1536]{1,0:T(8,128)(2,1)S(1)}, u32[]{:S(2)}, u32[]{:S(2)}) %collective-permute-start.1) | collective-permute-done | bytes 196640 | tf_op jit(solution)/shard_map/ppermute | solution.py:417
  22.1 0.0 copy-done
  22.1 0.0 copy-done.1
  22.1 0.0 copy-done.2
  22.1 8.9 %experts.1 = (bf16[64,2688]{1,0:T(8,128)(2,1)S(1)}, bf16[64,1536]{1,0:T(8,128)(2,1)S(1)}, bf16[2688,1536]{1,0:T(8,128)(2,1)S(1)}) custom-call(bf16[64,1536]{1,0:T(8,128)(2,1)S(1)} %bitcast.23, bf16[64,1536]{1,0:T(8,128)(2,1)S(1)} %collective-permute-done.1.other, f32[1,3072]{1,0:T(1,128)S(1)} %bitcast.24, bf16[2688,3072]{1,0:T(8,128)(2,1)S(1)} %bitcast.20, ...), custom_call_target="tpu_custom_call" | custom-call | tf_op jit(solution)/shard_map/experts/pallas_call | solution.py:397
  31.1 0.2 collective-permute-start.2
  31.2 1.5 %down_own.1 = bf16[64,1536]{1,0:T(8,128)(2,1)S(1)} custom-call(bf16[64,2688]{1,0:T(8,128)(2,1)S(1)} %get-tuple-element.16.hidden, bf16[2688,1536]{1,0:T(8,128)(2,1)S(1)} %get-tuple-element.17.kept), custom_call_target="tpu_custom_call" | custom-call | tf_op jit(solution)/shard_map/down_own/pallas_call | solution.py:424
  32.8 0.0 collective-permute-done.2
  32.8 0.1 fusion
  32.9 11.4 %all_to_all.11.returned = bf16[8,8,1536]{2,1,0:T(8,128)(2,1)S(1)} all-to-all(bf16[8,8,1536]{2,1,0:T(8,128)(2,1)S(1)} %fusion), channel_id=1, replica_groups=mesh['groups'=2,'dev'=2,'side'=8] {'side'}, dimensions={0} | all-to-all | bytes 393216 | tf_op jit(solution)/shard_map/all_to_all | solution.py:527
  44.3 0.7 %combine.1 = bf16[2,4,1536]{2,1,0:T(4,128)(2,1)} custom-call(f32[2,4,128]{2,1,0:T(4,128)S(1)} %get-tuple-element.12.shares, bf16[2,4,1536]{2,1,0:T(4,128)(2,1)S(1)} %get-tuple-element.14.updated, bf16[8,8,1536]{2,1,0:T(8,128)(2,1)S(1)} %all_to_all.11.returned), custom_call_target="tpu_custom_call" | custom-call | tf_op jit(solution)/shard_map/combine/pallas_call | solution.py:476
Async XLA Ops:
  0.0 4.0 %copy-start.3 = (bf16[3072,1536]{1,0:T(8,128)(2,1)S(1)}, bf16[3072,1536]{1,0:T(8,128)(2,1)}, u32[]{:S(2)}) copy-start(bf16[3072,1536]{1,0:T(8,128)(2,1)} %refs_2_.1) | copy-start | bytes 28311556
  0.0 4.0 %copy-start.4 = (bf16[2,4,1,1536]{3,1,2,0:T(4,128)(2,1)S(1)}, bf16[2,4,1,1536]{3,1,2,0:T(4,128)(2,1)}, u32[]{:S(2)}) copy-start(bf16[2,4,1,1536]{3,1,2,0:T(4,128)(2,1)} %param.21) | copy-start | bytes 73732
  1.9 1.4 %collective-permute-start = (bf16[4,3072]{1,0:T(4,128)(2,1)S(1)}, bf16[4,3072]{1,0:T(4,128)(2,1)S(1)}, u32[]{:S(2)}, u32[]{:S(2)}) collective-permute-start(bf16[4,3072]{1,0:T(4,128)(2,1)S(1)} %get-tuple-element.13.refs_0_), channel_id=1, source_target_pairs={{0,8},{8,0},{1,9},{9,1},{2,10},{10,2},{3,11},{11,3},{4,12},{12,4},... | collective-permute-start | bytes 73736 | tf_op jit(solution)/shard_map/ppermute | solution.py:512
  4.0 18.1 %copy-start = (bf16[1,2688,3072]{2,1,0:T(8,128)(2,1)S(1)}, bf16[1,2688,3072]{2,1,0:T(8,128)(2,1)}, u32[]{:S(2)}) copy-start(bf16[1,2688,3072]{2,1,0:T(8,128)(2,1)} %param.25) | copy-start | bytes 49545220
  4.0 18.1 %copy-start.1 = (bf16[1,2688,3072]{2,1,0:T(8,128)(2,1)S(1)}, bf16[1,2688,3072]{2,1,0:T(8,128)(2,1)}, u32[]{:S(2)}) copy-start(bf16[1,2688,3072]{2,1,0:T(8,128)(2,1)} %param.26) | copy-start | bytes 49545220
  4.0 18.1 %copy-start.2 = (f32[3072]{0:T(1024)S(1)}, f32[3072]{0:T(1024)}, u32[]{:S(2)}) copy-start(f32[3072]{0:T(1024)} %param.22) | copy-start | bytes 36868
  20.7 1.4 %collective-permute-start.1 = (bf16[64,1536]{1,0:T(8,128)(2,1)S(1)}, bf16[64,1536]{1,0:T(8,128)(2,1)S(1)}, u32[]{:S(2)}, u32[]{:S(2)}) collective-permute-start(bf16[64,1536]{1,0:T(8,128)(2,1)S(1)} %bitcast.22), channel_id=1, source_target_pairs={{0,8},{8,0},{1,9},{9,1},{2,10},{10,2},{3,11},{11,3},{4,12},{12,4},... | collective-permute-start | bytes 589832 | tf_op jit(solution)/shard_map/ppermute | solution.py:417
  31.1 1.7 %collective-permute-start.2 = (bf16[64,1536]{1,0:T(8,128)(2,1)S(1)}, bf16[64,1536]{1,0:T(8,128)(2,1)S(1)}, u32[]{:S(2)}, u32[]{:S(2)}) collective-permute-start(bf16[64,1536]{1,0:T(8,128)(2,1)S(1)} %get-tuple-element.18), channel_id=1, source_target_pairs={{0,8},{8,0},{1,9},{9,1},{2,10},{10,2},{3,11},{11,3},{4,12},{12,4},... | collective-permute-start | bytes 589832 | tf_op jit(solution)/shard_map/ppermute | solution.py:423

commit v8 on v7

--- a/solution.py
+++ b/solution.py
@@ -11,7 +11,7 @@
 norm_epsilon = 1e-05
 mebibyte = 1024 * 1024
 mxu_count, mxu_size = 2, 256
-hint_flops = 20_000_000_000
+hint_flops = 40_000_000_000
 last_last = (((1,), (1,)), ((), ()))
 
 smem_spec = pl.BlockSpec(memory_space=pltpu.SMEM)
@@ -123,7 +123,7 @@
         compiler_params=pltpu.CompilerParams(vmem_limit_bytes=50 * mebibyte),
         name="attend",
         cost_estimate=pl.CostEstimate(
-            flops=hint_flops, transcendentals=0, bytes_accessed=cache_keys.size * 4
+            flops=8_000_000_000, transcendentals=0, bytes_accessed=cache_keys.size * 4
         ),
     )(
         in_hbm(jnp.swapaxes(lengths, 1, 2)),

time: 45.2 us -> 45.2 us (level)
  no operation moved by 1% of the time
where the time goes in v8:
time: 45.2 us; the launch traced here: 45 us
  blocking collectives  26.7 us (59%)
  Pallas kernels  14.4 us (32%)
  waiting for transfers between devices  2.29 us (5%)
  local copies, waits for them, and re-layouts  0.74 us (2%)
  starting transfers between devices  0.73 us (2%)
    all_to_all x1, blocking collectives, body(): lax.all_to_all(copies, 'side', split_axis=0, concat_axis=0, tiled=True)  15.3 us
    all_to_all x1, blocking collectives, body(): lax.all_to_all(total, 'side', split_axis=0, concat_axis=0, tiled=True)  11.4 us
    pallas_call x1, Pallas kernels, pair_experts(): pl.pallas_call(pair_kernel, out_shape=(jax.ShapeDtypeStruct((rows, units)...  8.93 us
    pallas_call x1, Pallas kernels, attend(): pl.pallas_call(attend_kernel, out_shape=(jax.ShapeDtypeStruct((rows, head...  1.92 us
    pallas_call x1, Pallas kernels, pair_experts(): pl.pallas_call(down_kernel, out_shape=jax.ShapeDtypeStruct((rows, half),...  1.54 us
    ppermute x1, waiting for transfers between devices, pair_experts(): lax.ppermute(arrived, 'dev', swap)  1.44 us
    pallas_call x1, Pallas kernels, project(): pl.pallas_call(functools.partial(project_kernel, dev_count), out_shape=(j...  1.34 us
  transfers between devices with their start and end apart: 3, of which 2 were waited for; matrix products, arithmetic and copies ran while one was open for 0% of the time, Pallas kernels for 3%

profile of v8, /device:TPU:0, one launch (start us, length us, event | category | flops | bytes accessed | tf_op | source)
XLA Modules:
  0.0 45.0 jit_solution(7432130908213357522)
XLA Ops:
  0.0 0.0 copy-start.3
  0.0 0.0 slice-start
  0.0 0.0 slice-start.1
  0.0 1.9 %attend.1 = (bf16[4,3072]{1,0:T(4,128)(2,1)S(1)}, f32[2,4,128]{2,1,0:T(4,128)S(1)}) custom-call(s32[2,1,2]{2,1,0:T(1,128)} %bitcast.35, s32[2,4,4,8]{3,2,1,0:T(4,128)} %bitcast.32, f32[2,4,1,4]{3,2,1,0:T(1,128)} %probs.1, bf16[4,24,128]{2,1,0:T(8,128)(2,1)} %bitcast.31, bf16[4,512,128]{2,1,0:T(8,128)(2,1)} %bitcast.29, bf16[4,512,128]{2,1,0:T(8,128)(2,1)} %bitcast.30, ...), custom_call_target="tpu_custom_call" | custom-call | flops 8000000000 | bytes 1048576 | tf_op jit(solution)/shard_map/attend/pallas_call | solution.py:114
  1.9 0.5 %collective-permute-start = (bf16[4,3072]{1,0:T(4,128)(2,1)S(1)}, bf16[4,3072]{1,0:T(4,128)(2,1)S(1)}, u32[]{:S(2)}, u32[]{:S(2)}) collective-permute-start(bf16[4,3072]{1,0:T(4,128)(2,1)S(1)} %get-tuple-element.13.refs_0_), channel_id=1, source_target_pairs={{0,8},{8,0},{1,9},{9,1},{2,10},{10,2},{3,11},{11,3},{4,12},{12,4},... | collective-permute-start | bytes 73736 | tf_op jit(solution)/shard_map/ppermute | solution.py:512
  2.5 0.8 %collective-permute-done.refs_1_ = bf16[4,3072]{1,0:T(4,128)(2,1)S(1)} collective-permute-done((bf16[4,3072]{1,0:T(4,128)(2,1)S(1)}, bf16[4,3072]{1,0:T(4,128)(2,1)S(1)}, u32[]{:S(2)}, u32[]{:S(2)}) %collective-permute-start) | collective-permute-done | bytes 24608 | tf_op jit(solution)/shard_map/ppermute | solution.py:512
  3.3 0.0 copy-done.3
  3.3 0.0 slice-done
  3.3 0.5 %slice-done.1 = s8[4194304]{0:T(1024)(128)(4,1)S(1)} async-done(((s8[9437184]{0:T(1024)(128)(4,1)}), s8[4194304]{0:T(1024)(128)(4,1)S(1)}, s32[]{:S(2)}) %slice-start.1) | async-done | bytes 4194328
  3.8 0.2 slice-done.2
  4.1 1.3 %project.1 = (bf16[2,4,1536]{2,1,0:T(4,128)(2,1)S(1)}, bf16[8,8,1536]{2,1,0:T(8,128)(2,1)S(1)}) custom-call(bf16[4,3072]{1,0:T(4,128)(2,1)S(1)} %get-tuple-element.13.refs_0_, bf16[4,3072]{1,0:T(4,128)(2,1)S(1)} %collective-permute-done.refs_1_, bf16[3072,1536]{1,0:T(8,128)(2,1)S(1)} %bitcast.26, bf16[2,4,1536]{2,1,0:T(4,128)(2,1)S(1)} %bitcast.27), custom_call_target="tpu_custom_call" | custom-call | flops 40000000000 | bytes 9437184 | tf_op jit(solution)/shard_map/project/pallas_call | solution.py:177
  5.4 15.3 %all_to_all.10 = bf16[8,8,1536]{2,1,0:T(8,128)(2,1)S(1)} all-to-all(bf16[8,8,1536]{2,1,0:T(8,128)(2,1)S(1)} %get-tuple-element.15), channel_id=1, replica_groups=mesh['groups'=2,'dev'=2,'side'=8] {'side'}, dimensions={0} | all-to-all | bytes 393216 | tf_op jit(solution)/shard_map/all_to_all | solution.py:522
  20.7 0.0 collective-permute-start.1
  20.7 1.4 %collective-permute-done.1.other = bf16[64,1536]{1,0:T(8,128)(2,1)S(1)} collective-permute-done((bf16[64,1536]{1,0:T(8,128)(2,1)S(1)}, bf16[64,1536]{1,0:T(8,128)(2,1)S(1)}, u32[]{:S(2)}, u32[]{:S(2)}) %collective-permute-start.1) | collective-permute-done | bytes 196640 | tf_op jit(solution)/shard_map/ppermute | solution.py:417
  22.1 0.0 copy-done
  22.1 0.0 copy-done.1
  22.1 0.0 copy-done.2
  22.1 8.9 %experts.1 = (bf16[64,2688]{1,0:T(8,128)(2,1)S(1)}, bf16[64,1536]{1,0:T(8,128)(2,1)S(1)}, bf16[2688,1536]{1,0:T(8,128)(2,1)S(1)}) custom-call(bf16[64,1536]{1,0:T(8,128)(2,1)S(1)} %bitcast.23, bf16[64,1536]{1,0:T(8,128)(2,1)S(1)} %collective-permute-done.1.other, f32[1,3072]{1,0:T(1,128)S(1)} %bitcast.24, bf16[2688,3072]{1,0:T(8,128)(2,1)S(1)} %bitcast.20, ...), custom_call_target="tpu_custom_call" | custom-call | tf_op jit(solution)/shard_map/experts/pallas_call | solution.py:397
  31.1 0.2 collective-permute-start.2
  31.3 1.5 %down_own.1 = bf16[64,1536]{1,0:T(8,128)(2,1)S(1)} custom-call(bf16[64,2688]{1,0:T(8,128)(2,1)S(1)} %get-tuple-element.16.hidden, bf16[2688,1536]{1,0:T(8,128)(2,1)S(1)} %get-tuple-element.17.kept), custom_call_target="tpu_custom_call" | custom-call | tf_op jit(solution)/shard_map/down_own/pallas_call | solution.py:424
  32.8 0.0 collective-permute-done.2
  32.8 0.1 fusion
  32.9 11.4 %all_to_all.11.returned = bf16[8,8,1536]{2,1,0:T(8,128)(2,1)S(1)} all-to-all(bf16[8,8,1536]{2,1,0:T(8,128)(2,1)S(1)} %fusion), channel_id=1, replica_groups=mesh['groups'=2,'dev'=2,'side'=8] {'side'}, dimensions={0} | all-to-all | bytes 393216 | tf_op jit(solution)/shard_map/all_to_all | solution.py:527
  44.3 0.7 %combine.1 = bf16[2,4,1536]{2,1,0:T(4,128)(2,1)} custom-call(f32[2,4,128]{2,1,0:T(4,128)S(1)} %get-tuple-element.12.shares, bf16[2,4,1536]{2,1,0:T(4,128)(2,1)S(1)} %get-tuple-element.14.updated, bf16[8,8,1536]{2,1,0:T(8,128)(2,1)S(1)} %all_to_all.11.returned), custom_call_target="tpu_custom_call" | custom-call | tf_op jit(solution)/shard_map/combine/pallas_call | solution.py:476
  (5 shorter events, 0.0 us)
Async XLA Ops:
  0.0 3.3 %copy-start.3 = (bf16[2,4,1,1536]{3,1,2,0:T(4,128)(2,1)S(1)}, bf16[2,4,1,1536]{3,1,2,0:T(4,128)(2,1)}, u32[]{:S(2)}) copy-start(bf16[2,4,1,1536]{3,1,2,0:T(4,128)(2,1)} %param.21) | copy-start | bytes 73732
  0.0 3.3 %slice-start = ((s8[9437184]{0:T(1024)(128)(4,1)}), s8[4194304]{0:T(1024)(128)(4,1)S(1)}, s32[]{:S(2)}) async-start(s8[9437184]{0:T(1024)(128)(4,1)} %bitcast.25), calls=%async_computation.2 | async-start | bytes 8388608
  0.0 3.8 %slice-start.1 = ((s8[9437184]{0:T(1024)(128)(4,1)}), s8[4194304]{0:T(1024)(128)(4,1)S(1)}, s32[]{:S(2)}) async-start(s8[9437184]{0:T(1024)(128)(4,1)} %bitcast.25), calls=%async_computation.3 | async-start | bytes 8388608
  0.0 4.0 %slice-start.2 = ((s8[9437184]{0:T(1024)(128)(4,1)}), s8[1048576]{0:T(1024)(128)(4,1)S(1)}, s32[]{:S(2)}) async-start(s8[9437184]{0:T(1024)(128)(4,1)} %bitcast.25), calls=%async_computation.4 | async-start | bytes 2097152
  1.9 1.4 %collective-permute-start = (bf16[4,3072]{1,0:T(4,128)(2,1)S(1)}, bf16[4,3072]{1,0:T(4,128)(2,1)S(1)}, u32[]{:S(2)}, u32[]{:S(2)}) collective-permute-start(bf16[4,3072]{1,0:T(4,128)(2,1)S(1)} %get-tuple-element.13.refs_0_), channel_id=1, source_target_pairs={{0,8},{8,0},{1,9},{9,1},{2,10},{10,2},{3,11},{11,3},{4,12},{12,4},... | collective-permute-start | bytes 73736 | tf_op jit(solution)/shard_map/ppermute | solution.py:512
  4.0 18.1 %copy-start = (bf16[1,2688,3072]{2,1,0:T(8,128)(2,1)S(1)}, bf16[1,2688,3072]{2,1,0:T(8,128)(2,1)}, u32[]{:S(2)}) copy-start(bf16[1,2688,3072]{2,1,0:T(8,128)(2,1)} %param.25) | copy-start | bytes 49545220
  4.1 18.1 %copy-start.1 = (bf16[1,2688,3072]{2,1,0:T(8,128)(2,1)S(1)}, bf16[1,2688,3072]{2,1,0:T(8,128)(2,1)}, u32[]{:S(2)}) copy-start(bf16[1,2688,3072]{2,1,0:T(8,128)(2,1)} %param.26) | copy-start | bytes 49545220
  4.1 18.1 %copy-start.2 = (f32[3072]{0:T(1024)S(1)}, f32[3072]{0:T(1024)}, u32[]{:S(2)}) copy-start(f32[3072]{0:T(1024)} %param.22) | copy-start | bytes 36868
  20.7 1.4 %collective-permute-start.1 = (bf16[64,1536]{1,0:T(8,128)(2,1)S(1)}, bf16[64,1536]{1,0:T(8,128)(2,1)S(1)}, u32[]{:S(2)}, u32[]{:S(2)}) collective-permute-start(bf16[64,1536]{1,0:T(8,128)(2,1)S(1)} %bitcast.22), channel_id=1, source_target_pairs={{0,8},{8,0},{1,9},{9,1},{2,10},{10,2},{3,11},{11,3},{4,12},{12,4},... | collective-permute-start | bytes 589832 | tf_op jit(solution)/shard_map/ppermute | solution.py:417
  31.1 1.7 %collective-permute-start.2 = (bf16[64,1536]{1,0:T(8,128)(2,1)S(1)}, bf16[64,1536]{1,0:T(8,128)(2,1)S(1)}, u32[]{:S(2)}, u32[]{:S(2)}) collective-permute-start(bf16[64,1536]{1,0:T(8,128)(2,1)S(1)} %get-tuple-element.18), channel_id=1, source_target_pairs={{0,8},{8,0},{1,9},{9,1},{2,10},{10,2},{3,11},{11,3},{4,12},{12,4},... | collective-permute-start | bytes 589832 | tf_op jit(solution)/shard_map/ppermute | solution.py:423
